TPU v7x, 32 devices: a whole 2x2x4 slice. The times are simulated.
32 devices in a mesh: row: 16 (over z, y, core), off: 2 (over x).
Axes of the slice: x: 2, y: 2, z: 4, core: 2. Of those that a mesh axis runs over, the one named last changes fastest.
Arguments:
- vectors: float32 [16384, 128], P(('row', 'off')), may hold values from -6 to 6
- blocks: float32 [16, 2, 48, 128, 128], P('row', 'off'), may hold values from -0.125 to 0.125
- lists: int32 [16, 2, 2, 48], P('row', 'off'), may hold values from 0 to 7, as said below
Outputs:
- filtered: float32 [16384, 128], P(('row', 'off'))
Inputs may be any that keep to these rules, and one draw needn't show every extreme that they name: `lists`: within each tile the 48 listed blocks are distinct positions of its 8 x 8 grid of blocks.
All inputs are finite; a program needn't handle non-finite values.
Results may differ from a plain program's by a relative error of at most 0.00011.
Values sent between devices are 32-bit elements; how exact they have to be, the bound alone decides.
No kernel may reach another device: no remote copies, remote signals or barrier semaphores. Data moves between devices by JAX's collectives and lax.ppermute only.
A program may use at most 64 MiB of HBM per device.

v0:
```python
import functools

import jax
import jax.numpy as jnp
from jax import lax
from jax.experimental import pallas as pl
from jax.experimental.pallas import tpu as pltpu
from jax.sharding import PartitionSpec as P

DEGREE = 4
GROUPS = 2

first_scale = 0.4
later_scale = 0.8

VMEM = pl.BlockSpec(memory_space=pltpu.VMEM)
SMEM = pl.BlockSpec(memory_space=pltpu.SMEM)


def halves(values):
    high = values.astype(jnp.bfloat16)
    low = (values - high.astype(jnp.float32)).astype(jnp.bfloat16)
    return high, low


def product(left, high_ref, low_ref, strip):
    rows, depth = left.shape
    high, low = halves(left)
    both = jnp.concatenate([high, low], axis=0)
    for start in range(0, high_ref.shape[1], strip):
        at = slice(start, start + strip)
        main = jnp.dot(both, high_ref[:, at], preferred_element_type=jnp.float32)
        rest = jnp.dot(high, low_ref[:, at], preferred_element_type=jnp.float32)
        yield at, main[:rows] + main[rows:] + rest


def dense_kernel(lists_ref, blocks_ref, high_ref, low_ref, high_t_ref, low_t_ref):
    size = blocks_ref.shape[-1]
    for ref in (high_ref, low_ref, high_t_ref, low_t_ref):
        ref[...] = jnp.zeros_like(ref)

    @pl.loop(0, blocks_ref.shape[0])
    def _(k):
        row = pl.ds(pl.multiple_of(lists_ref[0, k] * size, size), size)
        col = pl.ds(pl.multiple_of(lists_ref[1, k] * size, size), size)
        block = blocks_ref[k]
        high, low = halves(block)
        high_ref[row, col] = high
        low_ref[row, col] = low
        high, low = halves(block.T)
        high_t_ref[col, row] = high
        low_t_ref[col, row] = low


def first_kernel(n_off, groups, offset_ref, *refs):
    pieces, (high_ref, low_ref), outs = refs[:n_off], refs[n_off : n_off + 2], refs[n_off + 2 :]
    rows = pieces[0].shape[0]
    width = pieces[0].shape[1] // groups
    for step, piece in enumerate(pieces):
        owner = lax.rem(offset_ref[0] - step + n_off, n_off)
        at = pl.ds(pl.multiple_of(owner * rows, rows), rows)
        turned = piece[...].T
        for group in range(groups):
            outs[group][:, at] = turned[group * width : (group + 1) * width]
    for group in range(groups):
        for at, value in product(outs[group][...], high_ref, low_ref, 256):
            outs[groups + group][:, at] = value


def step_kernel(n_off, scale, *refs):
    terms = refs[:n_off]
    has_previous = len(refs) == n_off + 5
    high_ref, low_ref, vectors_ref, out_ref = refs[-4:]
    total = terms[0][...]
    for term in terms[1:]:
        total = total + term[...]
    total = scale * total
    if has_previous:
        total = total - refs[n_off][...]
    vectors_ref[...] = total
    for at, value in product(total, high_ref, low_ref, 256):
        out_ref[:, at] = value


def far_kernel(far_ref, back_ref, high_ref, low_ref, out_ref):
    for at, value in product(far_ref[...], high_ref, low_ref, 256):
        out_ref[:, at] = value + back_ref[:, at]


def last_far_kernel(n_off, offset_ref, far_ref, back_ref, high_ref, low_ref, total_ref, *outs):
    for at, value in product(far_ref[...], high_ref, low_ref, 256):
        total_ref[:, at] = value + back_ref[:, at]
    rows = outs[0].shape[1]
    for step, out in enumerate(outs):
        owner = lax.rem(offset_ref[0] + step, n_off)
        out[...] = total_ref[:, pl.ds(pl.multiple_of(owner * rows, rows), rows)]


def last_kernel(n_off, groups, offset_ref, *refs):
    out_ref = refs[-1]
    rows = out_ref.shape[0]
    at = pl.ds(pl.multiple_of(offset_ref[0] * rows, rows), rows)
    result = []
    for group in range(groups):
        terms = refs[group * n_off : (group + 1) * n_off]
        total = terms[0][...]
        for term in terms[1:]:
            total = total + term[...]
        result.append(later_scale * total - refs[groups * n_off + group][:, at])
    out_ref[...] = jnp.concatenate(result, axis=0).T


def kernel_call(body, in_specs, shapes, scratch=(), flops=0, limit=24):
    return pl.pallas_call(
        body,
        out_shape=shapes,
        in_specs=in_specs,
        out_specs=[VMEM] * len(shapes),
        scratch_shapes=list(scratch),
        compiler_params=pltpu.CompilerParams(vmem_limit_bytes=limit * 2**20),
        cost_estimate=pl.CostEstimate(flops=flops, bytes_accessed=0, transcendentals=0),
    )


def per_device(vectors, blocks, lists):
    n_off = lax.axis_size("off")
    n_row = lax.axis_size("row")
    offset = lax.axis_index("off")[None].astype(jnp.int32)
    piece_rows, width = vectors.shape
    tile_rows = piece_rows * n_off
    group_width = width // GROUPS
    both = ("row", "off")

    def shifted(value, distance):
        return lax.ppermute(value, "off", [(d, (d + distance) % n_off) for d in range(n_off)])

    def route(sign):
        return [
            (i * n_off + d, (i + sign * d) % n_row * n_off + d)
            for i in range(n_row)
            for d in range(n_off)
        ]

    def pull(value):
        return lax.ppermute(value, both, route(-1))

    def push(value):
        return lax.ppermute(value, both, route(1))

    f32 = lambda *shape: jax.ShapeDtypeStruct(shape, jnp.float32)
    bf16 = jax.ShapeDtypeStruct((tile_rows, tile_rows), jnp.bfloat16)
    group_shape = f32(group_width, tile_rows)
    flops = 6 * group_width * tile_rows * tile_rows

    pieces = [vectors] + [shifted(vectors, s) for s in range(1, n_off)]
    high, low, high_t, low_t = kernel_call(
        dense_kernel, [SMEM, VMEM], [bf16] * 4
    )(lists[0, 0], blocks[0, 0])

    outs = kernel_call(
        functools.partial(first_kernel, n_off, GROUPS),
        [SMEM] + [VMEM] * (n_off + 2),
        [group_shape] * (2 * GROUPS),
        flops=flops * GROUPS,
    )(offset, *pieces, high, low)
    current, products = list(outs[:GROUPS]), list(outs[GROUPS:])
    previous = [None] * GROUPS
    totals = [None] * GROUPS
    for degree in range(DEGREE):
        scale = first_scale if degree == 1 else later_scale
        fars, backs = [None] * GROUPS, [None] * GROUPS
        for g in range(GROUPS):
            if degree > 0:
                terms = [totals[g]] + [shifted(totals[g], s) for s in range(1, n_off)]
                older = [] if previous[g] is None else [previous[g]]
                following, products[g] = kernel_call(
                    functools.partial(step_kernel, n_off, scale),
                    [VMEM] * (n_off + len(older) + 2),
                    [group_shape] * 2,
                    flops=flops,
                )(*terms, *older, high, low)
                previous[g], current[g] = current[g], following
            backs[g] = push(products[g])
            fars[g] = pull(current[g])
        for g in range(GROUPS):
            if degree < DEGREE - 1:
                [totals[g]] = kernel_call(
                    far_kernel, [VMEM] * 4, [group_shape], flops=flops
                )(fars[g], backs[g], high_t, low_t)
            else:
                totals[g] = kernel_call(
                    functools.partial(last_far_kernel, n_off),
                    [SMEM] + [VMEM] * 4,
                    [f32(group_width, tile_rows)] + [f32(group_width, piece_rows)] * n_off,
                    flops=flops,
                )(offset, fars[g], backs[g], high_t, low_t)[1:]
    terms = []
    for g in range(GROUPS):
        terms.append(totals[g][0])
        terms.extend(shifted(totals[g][s], s) for s in range(1, n_off))
    [result] = kernel_call(
        functools.partial(last_kernel, n_off, GROUPS),
        [SMEM] + [VMEM] * (GROUPS * (n_off + 1)),
        [f32(piece_rows, width)],
    )(offset, *terms, *previous)
    return result


def solution(mesh):
    in_specs = (
        P(("row", "off"), None),
        P("row", "off", None, None, None),
        P("row", "off", None, None),
    )
    out_specs = P(("row", "off"), None)
    return jax.shard_map(
        per_device, mesh=mesh, in_specs=in_specs, out_specs=out_specs, check_vma=False
    )
```

profile of v0, /device:TPU:0, one launch (start us, length us, event | category | flops | bytes accessed | tf_op | source)
XLA Modules:
  0.0 118.8 jit_solution(11306007770183102047)
XLA Ops:
  0.0 2.9 %collective-permute-start = (f32[512,128]{1,0:T(8,128)}, f32[512,128]{1,0:T(8,128)S(1)}, u32[]{:S(2)}, u32[]{:S(2)}) collective-permute-start(f32[512,128]{1,0:T(8,128)} %refs_0_.1), channel_id=1, source_target_pairs={{0,1},{1,0},{2,3},{3,2},{4,5},{5,4},{6,7},{7,6},{8,9},{9,8},{10,11... | collective-permute-start | bytes 786440 | tf_op jit(solution)/shard_map/ppermute | solution.py:135
  2.9 1.9 %copy-done = f32[1,1,48,128,128]{4,3,2,1,0:T(8,128)S(1)} copy-done((f32[1,1,48,128,128]{4,3,2,1,0:T(8,128)S(1)}, f32[1,1,48,128,128]{4,3,2,1,0:T(8,128)}, u32[]{:S(2)}) %copy-start) | copy-done | bytes 3145752
  4.8 0.7 copy-done.2
  5.5 6.4 %shard_map.37 = (bf16[1024,1024]{1,0:T(8,128)(2,1)S(1)}, bf16[1024,1024]{1,0:T(8,128)(2,1)S(1)}, bf16[1024,1024]{1,0:T(8,128)(2,1)S(1)}, bf16[1024,1024]{1,0:T(8,128)(2,1)S(1)}) custom-call(s32[2,48]{1,0:T(2,128)S(1)} %bitcast.4, f32[48,128,128]{2,1,0:T(8,128)S(1)} %bitcast.3), custom_call_target="tpu_custom_call" | custom-call | tf_op jit(solution)/shard_map/pallas_call | solution.py:156
  11.9 1.6 %shard_map.38 = (f32[64,1024]{1,0:T(8,128)S(1)}, f32[64,1024]{1,0:T(8,128)S(1)}, f32[64,1024]{1,0:T(8,128)S(1)}, f32[64,1024]{1,0:T(8,128)S(1)}) custom-call(s32[1]{0:T(128)} %bitcast.offset_ref, f32[512,128]{1,0:T(8,128)S(1)} %copy-done.1, f32[512,128]{1,0:T(8,128)S(1)} %collective-permute-done.refs_1_, ...), custom_call_target="tpu_custom_call" | custom-call | flops 805306368 | tf_op jit(solution)/shard_map/pallas_call | solution.py:160
  13.5 0.7 collective-permute-start.2
  14.2 0.7 collective-permute-start.1
  14.9 0.7 collective-permute-start.14
  15.6 0.7 collective-permute-start.13
  16.3 0.8 shard_map.39.refs_0_
  17.1 13.9 %collective-permute-start.3 = (f32[64,1024]{1,0:T(8,128)S(1)}, f32[64,1024]{1,0:T(8,128)S(1)}, u32[]{:S(2)}, u32[]{:S(2)}) collective-permute-start(f32[64,1024]{1,0:T(8,128)S(1)} %shard_map.39.refs_0_), channel_id=1, source_target_pairs={{0,1},{1,0},{2,3},{3,2},{4,5},{5,4},{6,7},{7,6},{8,9},{9,8},{10,11... | collective-permute-start | bytes 786440 | tf_op jit(solution)/shard_map/ppermute | solution.py:135
  31.0 0.8 shard_map.46.refs_0_
  31.8 3.0 %collective-permute-start.15 = (f32[64,1024]{1,0:T(8,128)S(1)}, f32[64,1024]{1,0:T(8,128)S(1)}, u32[]{:S(2)}, u32[]{:S(2)}) collective-permute-start(f32[64,1024]{1,0:T(8,128)S(1)} %shard_map.46.refs_0_), channel_id=1, source_target_pairs={{0,1},{1,0},{2,3},{3,2},{4,5},{5,4},{6,7},{7,6},{8,9},{9,8},{10,11... | collective-permute-start | bytes 786440 | tf_op jit(solution)/shard_map/ppermute | solution.py:135
  35.4 0.8 shard_map.40
  36.2 0.7 collective-permute-start.5
  36.8 0.7 collective-permute-start.4
  37.5 3.5 %collective-permute-done.15.refs_1_ = f32[64,1024]{1,0:T(8,128)S(1)} collective-permute-done((f32[64,1024]{1,0:T(8,128)S(1)}, f32[64,1024]{1,0:T(8,128)S(1)}, u32[]{:S(2)}, u32[]{:S(2)}) %collective-permute-start.15) | collective-permute-done | bytes 262176 | tf_op jit(solution)/shard_map/ppermute | solution.py:135
  41.1 0.8 shard_map.47
  41.9 0.7 collective-permute-start.17
  42.6 0.7 collective-permute-start.16
  43.3 0.8 shard_map.41.refs_0_
  44.1 12.5 %collective-permute-start.6 = (f32[64,1024]{1,0:T(8,128)S(1)}, f32[64,1024]{1,0:T(8,128)S(1)}, u32[]{:S(2)}, u32[]{:S(2)}) collective-permute-start(f32[64,1024]{1,0:T(8,128)S(1)} %shard_map.41.refs_0_), channel_id=1, source_target_pairs={{0,1},{1,0},{2,3},{3,2},{4,5},{5,4},{6,7},{7,6},{8,9},{9,8},{10,11... | collective-permute-start | bytes 786440 | tf_op jit(solution)/shard_map/ppermute | solution.py:135
  56.6 0.8 shard_map.48.refs_0_
  57.4 3.0 %collective-permute-start.18 = (f32[64,1024]{1,0:T(8,128)S(1)}, f32[64,1024]{1,0:T(8,128)S(1)}, u32[]{:S(2)}, u32[]{:S(2)}) collective-permute-start(f32[64,1024]{1,0:T(8,128)S(1)} %shard_map.48.refs_0_), channel_id=1, source_target_pairs={{0,1},{1,0},{2,3},{3,2},{4,5},{5,4},{6,7},{7,6},{8,9},{9,8},{10,11... | collective-permute-start | bytes 786440 | tf_op jit(solution)/shard_map/ppermute | solution.py:135
  60.4 1.5 %collective-permute-done.6.refs_1_ = f32[64,1024]{1,0:T(8,128)S(1)} collective-permute-done((f32[64,1024]{1,0:T(8,128)S(1)}, f32[64,1024]{1,0:T(8,128)S(1)}, u32[]{:S(2)}, u32[]{:S(2)}) %collective-permute-start.6) | collective-permute-done | bytes 262176 | tf_op jit(solution)/shard_map/ppermute | solution.py:135
  61.9 0.8 shard_map.42
  62.7 0.7 collective-permute-start.8
  63.4 0.7 collective-permute-start.7
  64.8 0.8 shard_map.49
  65.6 0.7 collective-permute-start.20
  66.3 0.7 collective-permute-start.19
  67.0 0.8 shard_map.43.refs_0_
  67.8 15.0 %collective-permute-start.9 = (f32[64,1024]{1,0:T(8,128)S(1)}, f32[64,1024]{1,0:T(8,128)S(1)}, u32[]{:S(2)}, u32[]{:S(2)}) collective-permute-start(f32[64,1024]{1,0:T(8,128)S(1)} %shard_map.43.refs_0_), channel_id=1, source_target_pairs={{0,1},{1,0},{2,3},{3,2},{4,5},{5,4},{6,7},{7,6},{8,9},{9,8},{10,11... | collective-permute-start | bytes 786440 | tf_op jit(solution)/shard_map/ppermute | solution.py:135
  82.8 0.8 shard_map.50.refs_0_
  83.6 3.0 %collective-permute-start.21 = (f32[64,1024]{1,0:T(8,128)S(1)}, f32[64,1024]{1,0:T(8,128)S(1)}, u32[]{:S(2)}, u32[]{:S(2)}) collective-permute-start(f32[64,1024]{1,0:T(8,128)S(1)} %shard_map.50.refs_0_), channel_id=1, source_target_pairs={{0,1},{1,0},{2,3},{3,2},{4,5},{5,4},{6,7},{7,6},{8,9},{9,8},{10,11... | collective-permute-start | bytes 786440 | tf_op jit(solution)/shard_map/ppermute | solution.py:135
  86.6 1.5 %collective-permute-done.9.refs_1_ = f32[64,1024]{1,0:T(8,128)S(1)} collective-permute-done((f32[64,1024]{1,0:T(8,128)S(1)}, f32[64,1024]{1,0:T(8,128)S(1)}, u32[]{:S(2)}, u32[]{:S(2)}) %collective-permute-start.9) | collective-permute-done | bytes 262176 | tf_op jit(solution)/shard_map/ppermute | solution.py:135
  88.1 0.8 shard_map.44
  88.9 0.7 collective-permute-start.10
  89.6 0.7 collective-permute-start.11
  91.0 0.8 shard_map.51
  91.8 0.7 collective-permute-start.22
  92.5 0.7 collective-permute-start.23
  93.2 1.5 %shard_map.45 = (f32[64,1024]{1,0:T(8,128)}, f32[64,512]{1,0:T(8,128)S(1)}, f32[64,512]{1,0:T(8,128)S(1)}) custom-call(s32[1]{0:T(128)} %bitcast.offset_ref, f32[64,1024]{1,0:T(8,128)S(1)} %collective-permute-done.10.far_ref, f32[64,1024]{1,0:T(8,128)S(1)} %collective-permute-done.11.back_ref, bf16[1024,1024]{1,0:T(8,128)(2,1)S(1)} %get-tuple-element.33.high_ref, ...), custom_call_target="tpu_custom_call" | custom-call | flops 402653184 | tf_op jit(solution)/shard_map/pallas_call | solution.py:191
  94.7 11.9 %collective-permute-start.12 = (f32[64,512]{1,0:T(8,128)S(1)}, f32[64,512]{1,0:T(8,128)S(1)}, u32[]{:S(2)}, u32[]{:S(2)}) collective-permute-start(f32[64,512]{1,0:T(8,128)S(1)} %get-tuple-element.42), channel_id=1, source_target_pairs={{0,1},{1,0},{2,3},{3,2},{4,5},{5,4},{6,7},{7,6},{8,9},{9,8},{10,11... | collective-permute-start | bytes 393224 | tf_op jit(solution)/shard_map/ppermute | solution.py:135
  106.6 1.5 %shard_map.52 = (f32[64,1024]{1,0:T(8,128)}, f32[64,512]{1,0:T(8,128)S(1)}, f32[64,512]{1,0:T(8,128)S(1)}) custom-call(s32[1]{0:T(128)} %bitcast.offset_ref, f32[64,1024]{1,0:T(8,128)S(1)} %collective-permute-done.22.far_ref, f32[64,1024]{1,0:T(8,128)S(1)} %collective-permute-done.23.back_ref, bf16[1024,1024]{1,0:T(8,128)(2,1)S(1)} %get-tuple-element.33.high_ref, ...), custom_call_target="tpu_custom_call" | custom-call | flops 402653184 | tf_op jit(solution)/shard_map/pallas_call | solution.py:191
  108.1 6.9 %collective-permute-start.24 = (f32[64,512]{1,0:T(8,128)S(1)}, f32[64,512]{1,0:T(8,128)S(1)}, u32[]{:S(2)}, u32[]{:S(2)}) collective-permute-start(f32[64,512]{1,0:T(8,128)S(1)} %get-tuple-element.52), channel_id=1, source_target_pairs={{0,1},{1,0},{2,3},{3,2},{4,5},{5,4},{6,7},{7,6},{8,9},{9,8},{10,11... | collective-permute-start | bytes 393224 | tf_op jit(solution)/shard_map/ppermute | solution.py:135
  115.0 2.9 %collective-permute-done.24.refs_3_ = f32[64,512]{1,0:T(8,128)S(1)} collective-permute-done((f32[64,512]{1,0:T(8,128)S(1)}, f32[64,512]{1,0:T(8,128)S(1)}, u32[]{:S(2)}, u32[]{:S(2)}) %collective-permute-start.24) | collective-permute-done | bytes 131104 | tf_op jit(solution)/shard_map/ppermute | solution.py:135
  117.9 0.8 shard_map.53
  (25 shorter events, 1.9 us)
Async XLA Ops:
  0.0 11.9 %collective-permute-start = (f32[512,128]{1,0:T(8,128)}, f32[512,128]{1,0:T(8,128)S(1)}, u32[]{:S(2)}, u32[]{:S(2)}) collective-permute-start(f32[512,128]{1,0:T(8,128)} %refs_0_.1), channel_id=1, source_target_pairs={{0,1},{1,0},{2,3},{3,2},{4,5},{5,4},{6,7},{7,6},{8,9},{9,8},{10,11... | collective-permute-start | bytes 786440 | tf_op jit(solution)/shard_map/ppermute | solution.py:135
  2.9 1.9 %copy-start = (f32[1,1,48,128,128]{4,3,2,1,0:T(8,128)S(1)}, f32[1,1,48,128,128]{4,3,2,1,0:T(8,128)}, u32[]{:S(2)}) copy-start(f32[1,1,48,128,128]{4,3,2,1,0:T(8,128)} %param.4) | copy-start | bytes 9437188
  4.8 0.7 copy-start.2
  5.5 6.4 %copy-start.1 = (f32[512,128]{1,0:T(8,128)S(1)}, f32[512,128]{1,0:T(8,128)}, u32[]{:S(2)}) copy-start(f32[512,128]{1,0:T(8,128)} %refs_0_.1) | copy-start | bytes 786436
  13.5 2.7 %collective-permute-start.2 = (f32[64,1024]{1,0:T(8,128)S(1)}, f32[64,1024]{1,0:T(8,128)S(1)}, u32[]{:S(2)}, u32[]{:S(2)}) collective-permute-start(f32[64,1024]{1,0:T(8,128)S(1)} %get-tuple-element.32), channel_id=1, source_target_pairs={{0,0},{1,3},{2,2},{3,5},{4,4},{5,7},{6,6},{7,9},{8,8},{9,11},{10,1... | collective-permute-start | bytes 786440 | tf_op jit(solution)/shard_map/ppermute | solution.py:148
  14.2 2.1 %collective-permute-start.1 = (f32[64,1024]{1,0:T(8,128)S(1)}, f32[64,1024]{1,0:T(8,128)S(1)}, u32[]{:S(2)}, u32[]{:S(2)}) collective-permute-start(f32[64,1024]{1,0:T(8,128)S(1)} %get-tuple-element.31.refs_2_), channel_id=1, source_target_pairs={{0,0},{1,31},{2,2},{3,1},{4,4},{5,3},{6,6},{7,5},{8,8},{9,7},{10,1... | collective-permute-start | bytes 786440 | tf_op jit(solution)/shard_map/ppermute | solution.py:145
  14.9 16.1 %collective-permute-start.14 = (f32[64,1024]{1,0:T(8,128)S(1)}, f32[64,1024]{1,0:T(8,128)S(1)}, u32[]{:S(2)}, u32[]{:S(2)}) collective-permute-start(f32[64,1024]{1,0:T(8,128)S(1)} %get-tuple-element.44), channel_id=1, source_target_pairs={{0,0},{1,3},{2,2},{3,5},{4,4},{5,7},{6,6},{7,9},{8,8},{9,11},{10,1... | collective-permute-start | bytes 786440 | tf_op jit(solution)/shard_map/ppermute | solution.py:148
  15.6 15.4 %collective-permute-start.13 = (f32[64,1024]{1,0:T(8,128)S(1)}, f32[64,1024]{1,0:T(8,128)S(1)}, u32[]{:S(2)}, u32[]{:S(2)}) collective-permute-start(f32[64,1024]{1,0:T(8,128)S(1)} %get-tuple-element.43.refs_2_), channel_id=1, source_target_pairs={{0,0},{1,31},{2,2},{3,1},{4,4},{5,3},{6,6},{7,5},{8,8},{9,7},{10,1... | collective-permute-start | bytes 786440 | tf_op jit(solution)/shard_map/ppermute | solution.py:145
  17.1 18.2 %collective-permute-start.3 = (f32[64,1024]{1,0:T(8,128)S(1)}, f32[64,1024]{1,0:T(8,128)S(1)}, u32[]{:S(2)}, u32[]{:S(2)}) collective-permute-start(f32[64,1024]{1,0:T(8,128)S(1)} %shard_map.39.refs_0_), channel_id=1, source_target_pairs={{0,1},{1,0},{2,3},{3,2},{4,5},{5,4},{6,7},{7,6},{8,9},{9,8},{10,11... | collective-permute-start | bytes 786440 | tf_op jit(solution)/shard_map/ppermute | solution.py:135
  31.8 9.2 %collective-permute-start.15 = (f32[64,1024]{1,0:T(8,128)S(1)}, f32[64,1024]{1,0:T(8,128)S(1)}, u32[]{:S(2)}, u32[]{:S(2)}) collective-permute-start(f32[64,1024]{1,0:T(8,128)S(1)} %shard_map.46.refs_0_), channel_id=1, source_target_pairs={{0,1},{1,0},{2,3},{3,2},{4,5},{5,4},{6,7},{7,6},{8,9},{9,8},{10,11... | collective-permute-start | bytes 786440 | tf_op jit(solution)/shard_map/ppermute | solution.py:135
  36.2 7.1 %collective-permute-start.5 = (f32[64,1024]{1,0:T(8,128)S(1)}, f32[64,1024]{1,0:T(8,128)S(1)}, u32[]{:S(2)}, u32[]{:S(2)}) collective-permute-start(f32[64,1024]{1,0:T(8,128)S(1)} %get-tuple-element.36), channel_id=1, source_target_pairs={{0,0},{1,3},{2,2},{3,5},{4,4},{5,7},{6,6},{7,9},{8,8},{9,11},{10,1... | collective-permute-start | bytes 786440 | tf_op jit(solution)/shard_map/ppermute | solution.py:148
  36.8 6.4 %collective-permute-start.4 = (f32[64,1024]{1,0:T(8,128)S(1)}, f32[64,1024]{1,0:T(8,128)S(1)}, u32[]{:S(2)}, u32[]{:S(2)}) collective-permute-start(f32[64,1024]{1,0:T(8,128)S(1)} %get-tuple-element.35.refs_2_), channel_id=1, source_target_pairs={{0,0},{1,31},{2,2},{3,1},{4,4},{5,3},{6,6},{7,5},{8,8},{9,7},{10,1... | collective-permute-start | bytes 786440 | tf_op jit(solution)/shard_map/ppermute | solution.py:145
  41.9 14.7 %collective-permute-start.17 = (f32[64,1024]{1,0:T(8,128)S(1)}, f32[64,1024]{1,0:T(8,128)S(1)}, u32[]{:S(2)}, u32[]{:S(2)}) collective-permute-start(f32[64,1024]{1,0:T(8,128)S(1)} %get-tuple-element.46), channel_id=1, source_target_pairs={{0,0},{1,3},{2,2},{3,5},{4,4},{5,7},{6,6},{7,9},{8,8},{9,11},{10,1... | collective-permute-start | bytes 786440 | tf_op jit(solution)/shard_map/ppermute | solution.py:148
  42.6 14.0 %collective-permute-start.16 = (f32[64,1024]{1,0:T(8,128)S(1)}, f32[64,1024]{1,0:T(8,128)S(1)}, u32[]{:S(2)}, u32[]{:S(2)}) collective-permute-start(f32[64,1024]{1,0:T(8,128)S(1)} %get-tuple-element.45.refs_2_), channel_id=1, source_target_pairs={{0,0},{1,31},{2,2},{3,1},{4,4},{5,3},{6,6},{7,5},{8,8},{9,7},{10,1... | collective-permute-start | bytes 786440 | tf_op jit(solution)/shard_map/ppermute | solution.py:145
  44.1 17.9 %collective-permute-start.6 = (f32[64,1024]{1,0:T(8,128)S(1)}, f32[64,1024]{1,0:T(8,128)S(1)}, u32[]{:S(2)}, u32[]{:S(2)}) collective-permute-start(f32[64,1024]{1,0:T(8,128)S(1)} %shard_map.41.refs_0_), channel_id=1, source_target_pairs={{0,1},{1,0},{2,3},{3,2},{4,5},{5,4},{6,7},{7,6},{8,9},{9,8},{10,11... | collective-permute-start | bytes 786440 | tf_op jit(solution)/shard_map/ppermute | solution.py:135
  57.4 7.4 %collective-permute-start.18 = (f32[64,1024]{1,0:T(8,128)S(1)}, f32[64,1024]{1,0:T(8,128)S(1)}, u32[]{:S(2)}, u32[]{:S(2)}) collective-permute-start(f32[64,1024]{1,0:T(8,128)S(1)} %shard_map.48.refs_0_), channel_id=1, source_target_pairs={{0,1},{1,0},{2,3},{3,2},{4,5},{5,4},{6,7},{7,6},{8,9},{9,8},{10,11... | collective-permute-start | bytes 786440 | tf_op jit(solution)/shard_map/ppermute | solution.py:135
  62.7 4.2 %collective-permute-start.8 = (f32[64,1024]{1,0:T(8,128)S(1)}, f32[64,1024]{1,0:T(8,128)S(1)}, u32[]{:S(2)}, u32[]{:S(2)}) collective-permute-start(f32[64,1024]{1,0:T(8,128)S(1)} %get-tuple-element.38), channel_id=1, source_target_pairs={{0,0},{1,3},{2,2},{3,5},{4,4},{5,7},{6,6},{7,9},{8,8},{9,11},{10,1... | collective-permute-start | bytes 786440 | tf_op jit(solution)/shard_map/ppermute | solution.py:148
  63.4 3.5 %collective-permute-start.7 = (f32[64,1024]{1,0:T(8,128)S(1)}, f32[64,1024]{1,0:T(8,128)S(1)}, u32[]{:S(2)}, u32[]{:S(2)}) collective-permute-start(f32[64,1024]{1,0:T(8,128)S(1)} %get-tuple-element.37.refs_4_), channel_id=1, source_target_pairs={{0,0},{1,31},{2,2},{3,1},{4,4},{5,3},{6,6},{7,5},{8,8},{9,7},{10,1... | collective-permute-start | bytes 786440 | tf_op jit(solution)/shard_map/ppermute | solution.py:145
  65.6 17.2 %collective-permute-start.20 = (f32[64,1024]{1,0:T(8,128)S(1)}, f32[64,1024]{1,0:T(8,128)S(1)}, u32[]{:S(2)}, u32[]{:S(2)}) collective-permute-start(f32[64,1024]{1,0:T(8,128)S(1)} %get-tuple-element.48), channel_id=1, source_target_pairs={{0,0},{1,3},{2,2},{3,5},{4,4},{5,7},{6,6},{7,9},{8,8},{9,11},{10,1... | collective-permute-start | bytes 786440 | tf_op jit(solution)/shard_map/ppermute | solution.py:148
  66.3 16.5 %collective-permute-start.19 = (f32[64,1024]{1,0:T(8,128)S(1)}, f32[64,1024]{1,0:T(8,128)S(1)}, u32[]{:S(2)}, u32[]{:S(2)}) collective-permute-start(f32[64,1024]{1,0:T(8,128)S(1)} %get-tuple-element.47.refs_5_), channel_id=1, source_target_pairs={{0,0},{1,31},{2,2},{3,1},{4,4},{5,3},{6,6},{7,5},{8,8},{9,7},{10,1... | collective-permute-start | bytes 786440 | tf_op jit(solution)/shard_map/ppermute | solution.py:145
  67.8 20.3 %collective-permute-start.9 = (f32[64,1024]{1,0:T(8,128)S(1)}, f32[64,1024]{1,0:T(8,128)S(1)}, u32[]{:S(2)}, u32[]{:S(2)}) collective-permute-start(f32[64,1024]{1,0:T(8,128)S(1)} %shard_map.43.refs_0_), channel_id=1, source_target_pairs={{0,1},{1,0},{2,3},{3,2},{4,5},{5,4},{6,7},{7,6},{8,9},{9,8},{10,11... | collective-permute-start | bytes 786440 | tf_op jit(solution)/shard_map/ppermute | solution.py:135
  83.6 7.4 %collective-permute-start.21 = (f32[64,1024]{1,0:T(8,128)S(1)}, f32[64,1024]{1,0:T(8,128)S(1)}, u32[]{:S(2)}, u32[]{:S(2)}) collective-permute-start(f32[64,1024]{1,0:T(8,128)S(1)} %shard_map.50.refs_0_), channel_id=1, source_target_pairs={{0,1},{1,0},{2,3},{3,2},{4,5},{5,4},{6,7},{7,6},{8,9},{9,8},{10,11... | collective-permute-start | bytes 786440 | tf_op jit(solution)/shard_map/ppermute | solution.py:135
  88.9 4.2 %collective-permute-start.10 = (f32[64,1024]{1,0:T(8,128)S(1)}, f32[64,1024]{1,0:T(8,128)S(1)}, u32[]{:S(2)}, u32[]{:S(2)}) collective-permute-start(f32[64,1024]{1,0:T(8,128)S(1)} %get-tuple-element.39), channel_id=1, source_target_pairs={{0,0},{1,31},{2,2},{3,1},{4,4},{5,3},{6,6},{7,5},{8,8},{9,7},{10,1... | collective-permute-start | bytes 786440 | tf_op jit(solution)/shard_map/ppermute | solution.py:145
  89.6 3.5 %collective-permute-start.11 = (f32[64,1024]{1,0:T(8,128)S(1)}, f32[64,1024]{1,0:T(8,128)S(1)}, u32[]{:S(2)}, u32[]{:S(2)}) collective-permute-start(f32[64,1024]{1,0:T(8,128)S(1)} %get-tuple-element.40), channel_id=1, source_target_pairs={{0,0},{1,3},{2,2},{3,5},{4,4},{5,7},{6,6},{7,9},{8,8},{9,11},{10,1... | collective-permute-start | bytes 786440 | tf_op jit(solution)/shard_map/ppermute | solution.py:148
  91.8 14.8 %collective-permute-start.22 = (f32[64,1024]{1,0:T(8,128)S(1)}, f32[64,1024]{1,0:T(8,128)S(1)}, u32[]{:S(2)}, u32[]{:S(2)}) collective-permute-start(f32[64,1024]{1,0:T(8,128)S(1)} %get-tuple-element.49), channel_id=1, source_target_pairs={{0,0},{1,31},{2,2},{3,1},{4,4},{5,3},{6,6},{7,5},{8,8},{9,7},{10,1... | collective-permute-start | bytes 786440 | tf_op jit(solution)/shard_map/ppermute | solution.py:145
  92.5 14.1 %collective-permute-start.23 = (f32[64,1024]{1,0:T(8,128)S(1)}, f32[64,1024]{1,0:T(8,128)S(1)}, u32[]{:S(2)}, u32[]{:S(2)}) collective-permute-start(f32[64,1024]{1,0:T(8,128)S(1)} %get-tuple-element.50), channel_id=1, source_target_pairs={{0,0},{1,3},{2,2},{3,5},{4,4},{5,7},{6,6},{7,9},{8,8},{9,11},{10,1... | collective-permute-start | bytes 786440 | tf_op jit(solution)/shard_map/ppermute | solution.py:148
  94.7 20.3 %collective-permute-start.12 = (f32[64,512]{1,0:T(8,128)S(1)}, f32[64,512]{1,0:T(8,128)S(1)}, u32[]{:S(2)}, u32[]{:S(2)}) collective-permute-start(f32[64,512]{1,0:T(8,128)S(1)} %get-tuple-element.42), channel_id=1, source_target_pairs={{0,1},{1,0},{2,3},{3,2},{4,5},{5,4},{6,7},{7,6},{8,9},{9,8},{10,11... | collective-permute-start | bytes 393224 | tf_op jit(solution)/shard_map/ppermute | solution.py:135
  108.1 9.8 %collective-permute-start.24 = (f32[64,512]{1,0:T(8,128)S(1)}, f32[64,512]{1,0:T(8,128)S(1)}, u32[]{:S(2)}, u32[]{:S(2)}) collective-permute-start(f32[64,512]{1,0:T(8,128)S(1)} %get-tuple-element.52), channel_id=1, source_target_pairs={{0,1},{1,0},{2,3},{3,2},{4,5},{5,4},{6,7},{7,6},{8,9},{9,8},{10,11... | collective-permute-start | bytes 393224 | tf_op jit(solution)/shard_map/ppermute | solution.py:135
where the time goes:
time: 119 us
  starting transfers between devices  82.9 us (70%)
  Pallas kernels  21.5 us (18%)
  waiting for transfers between devices  11.4 us (10%)
  local copies, waits for them, and re-layouts  2.57 us (2%)
    ppermute x9, starting transfers between devices, shifted(): lax.ppermute(value, 'off', [(d, (d + distance) % n_off) for d in range(n_...  72.1 us
    ppermute x9, waiting for transfers between devices, shifted(): lax.ppermute(value, 'off', [(d, (d + distance) % n_off) for d in range(n_...  11.3 us
    pallas_call x1, Pallas kernels, per_device(): kernel_call(dense_kernel, [SMEM, VMEM], [bf16] * 4)  6.36 us
    ppermute x8, starting transfers between devices, pull(): return lax.ppermute(value, both, route(-1))  5.42 us
    ppermute x8, starting transfers between devices, push(): return lax.ppermute(value, both, route(1))  5.42 us
    pallas_call x6, Pallas kernels, per_device(): kernel_call(far_kernel, [VMEM] * 4, [group_shape], flops=flops)  4.84 us
    pallas_call x6, Pallas kernels, per_device(): kernel_call(functools.partial(step_kernel, n_off, scale), [VMEM] * (n_off...  4.78 us
    pallas_call x2, Pallas kernels, per_device(): kernel_call(functools.partial(last_far_kernel, n_off), [SMEM] + [VMEM] *...  3.07 us
  transfers between devices with their start and end apart: 25, of which 7 were waited for; matrix products, arithmetic and copies ran while one was open for 0% of the time, Pallas kernels for 16%

commit v1 on v0

v1 whole, which is shorter than its diff:
```python
import functools

import jax
import jax.numpy as jnp
from jax import lax
from jax.experimental import pallas as pl
from jax.experimental.pallas import tpu as pltpu
from jax.sharding import PartitionSpec as P

DEGREE = 4
GROUPS = 2

first_scale = 0.4
later_scale = 0.8

VMEM = pl.BlockSpec(memory_space=pltpu.VMEM)
SMEM = pl.BlockSpec(memory_space=pltpu.SMEM)


def halves(values):
    high = values.astype(jnp.bfloat16)
    low = (values - high.astype(jnp.float32)).astype(jnp.bfloat16)
    return high, low


def product(left, high_ref, low_ref, strip):
    rows, depth = left.shape
    high, low = halves(left)
    both = jnp.concatenate([high, low], axis=0)
    for start in range(0, high_ref.shape[1], strip):
        at = slice(start, start + strip)
        main = jnp.dot(both, high_ref[:, at], preferred_element_type=jnp.float32)
        rest = jnp.dot(high, low_ref[:, at], preferred_element_type=jnp.float32)
        yield at, main[:rows] + main[rows:] + rest


def dense_kernel(turned, which, lists_ref, blocks_ref, high_ref, low_ref):
    size = blocks_ref.shape[-1]
    high_ref[...] = jnp.zeros_like(high_ref)
    low_ref[...] = jnp.zeros_like(low_ref)

    @pl.loop(0, blocks_ref.shape[0])
    def _(k):
        row = pl.ds(pl.multiple_of(lists_ref[which, k] * size, size), size)
        col = pl.ds(pl.multiple_of(lists_ref[1 - which, k] * size, size), size)
        block = blocks_ref[k]
        high_ref[row, col], low_ref[row, col] = halves(block.T if turned else block)


def summed(terms):
    total = terms[0][...]
    for term in terms[1:]:
        total = total + term[...]
    return total


def chosen(refs, at):
    offset = lax.axis_index("off")
    value = refs[0][:, at]
    for distance in range(1, len(refs)):
        value = jnp.where(offset == distance, refs[distance][:, at], value)
    return value


def first_kernel(n_off, groups, *refs):
    pieces, (high_ref, low_ref), outs = refs[:n_off], refs[n_off : n_off + 2], refs[n_off + 2 :]
    rows = pieces[0].shape[0]
    width = pieces[0].shape[1] // groups
    offset = lax.axis_index("off")
    for step, piece in enumerate(pieces):
        owner = lax.rem(offset - step + n_off, n_off)
        at = pl.ds(pl.multiple_of(owner * rows, rows), rows)
        turned = piece[...].T
        for group in range(groups):
            outs[group][:, at] = turned[group * width : (group + 1) * width]
    for group in range(groups):
        for at, value in product(outs[group][...], high_ref, low_ref, 256):
            outs[groups + group][:, at] = value


def step_kernel(n_off, scale, *refs):
    high_ref, low_ref, vectors_ref, out_ref = refs[-4:]
    total = scale * summed(refs[:n_off])
    if len(refs) > n_off + 4:
        total = total - refs[n_off][...]
    vectors_ref[...] = total
    for at, value in product(total, high_ref, low_ref, 256):
        out_ref[:, at] = value


def far_kernel(n_off, *refs):
    fars, backs = refs[:n_off], refs[n_off : 2 * n_off]
    high_ref, low_ref = refs[2 * n_off : 2 * n_off + 2]
    total_ref, outs = refs[2 * n_off + 2], refs[2 * n_off + 3 :]
    everything = slice(None)
    for at, value in product(chosen(fars, everything), high_ref, low_ref, 256):
        total_ref[:, at] = value + chosen(backs, at)
    for step, out in enumerate(outs):
        rows = out.shape[1]
        owner = lax.rem(lax.axis_index("off") + step, n_off)
        out[...] = total_ref[:, pl.ds(pl.multiple_of(owner * rows, rows), rows)]


def last_kernel(n_off, groups, *refs):
    out_ref = refs[-1]
    rows = out_ref.shape[0]
    at = pl.ds(pl.multiple_of(lax.axis_index("off") * rows, rows), rows)
    result = []
    for group in range(groups):
        total = summed(refs[group * n_off : (group + 1) * n_off])
        result.append(later_scale * total - refs[groups * n_off + group][:, at])
    out_ref[...] = jnp.concatenate(result, axis=0).T


def kernel_call(body, in_specs, shapes, scratch=(), flops=0, limit=24):
    return pl.pallas_call(
        body,
        out_shape=shapes,
        in_specs=in_specs,
        out_specs=[VMEM] * len(shapes),
        scratch_shapes=list(scratch),
        compiler_params=pltpu.CompilerParams(vmem_limit_bytes=limit * 2**20),
        cost_estimate=pl.CostEstimate(flops=flops, bytes_accessed=0, transcendentals=0),
    )


def per_device(vectors, blocks, lists):
    n_off = lax.axis_size("off")
    n_row = lax.axis_size("row")
    piece_rows, width = vectors.shape
    tile_rows = piece_rows * n_off
    group_width = width // GROUPS

    def shifted(value, distance):
        return lax.ppermute(value, "off", [(d, (d + distance) % n_off) for d in range(n_off)])

    def passed(value, direction):
        route = [(i, (i + direction) % n_row) for i in range(n_row)]
        values = [value]
        for _ in range(1, n_off):
            values.append(lax.ppermute(values[-1], "row", route))
        return values

    f32 = lambda *shape: jax.ShapeDtypeStruct(shape, jnp.float32)
    bf16 = jax.ShapeDtypeStruct((tile_rows, tile_rows), jnp.bfloat16)
    group_shape = f32(group_width, tile_rows)
    piece_shape = f32(group_width, piece_rows)
    flops = 6 * group_width * tile_rows * tile_rows

    pieces = [vectors] + [shifted(vectors, s) for s in range(1, n_off)]
    high, low = kernel_call(
        functools.partial(dense_kernel, False, 0), [SMEM, VMEM], [bf16] * 2
    )(lists[0, 0], blocks[0, 0])
    outs = kernel_call(
        functools.partial(first_kernel, n_off, GROUPS),
        [VMEM] * (n_off + 2),
        [group_shape] * (2 * GROUPS),
        flops=flops * GROUPS,
    )(*pieces, high, low)
    high_t, low_t = kernel_call(
        functools.partial(dense_kernel, True, 1), [SMEM, VMEM], [bf16] * 2, flops=flops
    )(lists[0, 0], blocks[0, 0])

    current, products = list(outs[:GROUPS]), list(outs[GROUPS:])
    previous = [None] * GROUPS
    totals = [None] * GROUPS
    for degree in range(DEGREE):
        scale = first_scale if degree == 1 else later_scale
        fars, backs = [None] * GROUPS, [None] * GROUPS
        for g in range(GROUPS):
            if degree > 0:
                terms = [totals[g]] + [shifted(totals[g], s) for s in range(1, n_off)]
                older = [] if previous[g] is None else [previous[g]]
                following, products[g] = kernel_call(
                    functools.partial(step_kernel, n_off, scale),
                    [VMEM] * (n_off + len(older) + 2),
                    [group_shape] * 2,
                    flops=flops,
                )(*terms, *older, high, low)
                previous[g], current[g] = current[g], following
            backs[g] = passed(products[g], 1)
            fars[g] = passed(current[g], -1)
        for g in range(GROUPS):
            pieces_out = n_off if degree == DEGREE - 1 else 0
            outs = kernel_call(
                functools.partial(far_kernel, n_off),
                [VMEM] * (2 * n_off + 2),
                [group_shape] + [piece_shape] * pieces_out,
                flops=flops,
            )(*fars[g], *backs[g], high_t, low_t)
            totals[g] = outs[1:] if pieces_out else outs[0]
    terms = []
    for g in range(GROUPS):
        terms.append(totals[g][0])
        terms.extend(shifted(totals[g][s], s) for s in range(1, n_off))
    [result] = kernel_call(
        functools.partial(last_kernel, n_off, GROUPS),
        [VMEM] * (GROUPS * (n_off + 1)),
        [f32(piece_rows, width)],
    )(*terms, *previous)
    return result


def solution(mesh):
    in_specs = (
        P(("row", "off"), None),
        P("row", "off", None, None, None),
        P("row", "off", None, None),
    )
    out_specs = P(("row", "off"), None)
    return jax.shard_map(
        per_device, mesh=mesh, in_specs=in_specs, out_specs=out_specs, check_vma=False
    )
```

time: 119 us -> 98.7 us (0.83)
  starting transfers between devices: 82.9 us -> 42.2 us
  waiting for transfers between devices: 11.4 us -> 30.8 us
  Pallas kernels: 21.5 us -> 22.8 us
    ppermute x9, starting transfers between devices: 72.1 us -> 15.1 us  [shifted(): lax.ppermute(value, 'off', [(d, (d + distance) % n_off) for d in range(n_...]
    ppermute x16, waiting for transfers between devices: 0.04 us -> 18 us  [passed(): values.append(lax.ppermute(values[-1], 'row', route))]
    ppermute x16, starting transfers between devices: 10.8 us -> 27.1 us  [passed(): values.append(lax.ppermute(values[-1], 'row', route))]
    ppermute x9, waiting for transfers between devices: 11.3 us -> 12.8 us  [shifted(): lax.ppermute(value, 'off', [(d, (d + distance) % n_off) for d in range(n_...]
    pallas_call x11 -> x12, Pallas kernels: 16.7 us -> 18.1 us  [the longest x8 7.99 us: per_device(): kernel_call(functools.partial(far_kernel, n_off), [VMEM] * (2 * n_off + 2...]
  transfers between devices with their start and end apart: 25 -> 25, of which waited for: 7 -> 12; matrix products, arithmetic and copies ran while one was open for 0% -> 0% of each run, Pallas kernels for 16% -> 21%
where the time goes in v1:
time: 98.7 us; the launch traced here: 98.5 us
  starting transfers between devices  42.2 us (43%)
  waiting for transfers between devices  30.8 us (31%)
  Pallas kernels  22.8 us (23%)
  local copies, waits for them, and re-layouts  2.57 us (3%)
    ppermute x16, starting transfers between devices, passed(): values.append(lax.ppermute(values[-1], 'row', route))  27.1 us
    ppermute x16, waiting for transfers between devices, passed(): values.append(lax.ppermute(values[-1], 'row', route))  18 us
    ppermute x9, starting transfers between devices, shifted(): lax.ppermute(value, 'off', [(d, (d + distance) % n_off) for d in range(n_...  15.1 us
    ppermute x9, waiting for transfers between devices, shifted(): lax.ppermute(value, 'off', [(d, (d + distance) % n_off) for d in range(n_...  12.8 us
    pallas_call x8, Pallas kernels, per_device(): kernel_call(functools.partial(far_kernel, n_off), [VMEM] * (2 * n_off + 2...  7.99 us
    pallas_call x1, Pallas kernels, per_device(): kernel_call(functools.partial(dense_kernel, True, 1), [SMEM, VMEM], [bf16...  5.81 us
    pallas_call x6, Pallas kernels, per_device(): kernel_call(functools.partial(step_kernel, n_off, scale), [VMEM] * (n_off...  4.74 us
    unnamed x6, local copies, waits for them, and re-layouts  2.57 us
  transfers between devices with their start and end apart: 25, of which 12 were waited for; matrix products, arithmetic and copies ran while one was open for 0% of the time, Pallas kernels for 21%

profile of v1, /device:TPU:0, one launch (start us, length us, event | category | flops | bytes accessed | tf_op | source)
XLA Modules:
  0.0 98.5 jit_solution(13083449724895620309)
XLA Ops:
  0.0 2.9 %collective-permute-start = (f32[512,128]{1,0:T(8,128)}, f32[512,128]{1,0:T(8,128)S(1)}, u32[]{:S(2)}, u32[]{:S(2)}) collective-permute-start(f32[512,128]{1,0:T(8,128)} %refs_0_.1), channel_id=1, source_target_pairs={{0,1},{1,0},{2,3},{3,2},{4,5},{5,4},{6,7},{7,6},{8,9},{9,8},{10,11... | collective-permute-start | bytes 786440 | tf_op jit(solution)/shard_map/ppermute | solution.py:135
  2.9 1.9 %copy-done = f32[1,1,48,128,128]{4,3,2,1,0:T(8,128)S(1)} copy-done((f32[1,1,48,128,128]{4,3,2,1,0:T(8,128)S(1)}, f32[1,1,48,128,128]{4,3,2,1,0:T(8,128)}, u32[]{:S(2)}) %copy-start) | copy-done | bytes 3145752
  4.8 0.7 copy-done.2
  5.5 1.8 %shard_map.37 = (bf16[1024,1024]{1,0:T(8,128)(2,1)S(1)}, bf16[1024,1024]{1,0:T(8,128)(2,1)S(1)}) custom-call(s32[2,48]{1,0:T(2,128)S(1)} %bitcast.4, f32[48,128,128]{2,1,0:T(8,128)S(1)} %bitcast.2), custom_call_target="tpu_custom_call" | custom-call | tf_op jit(solution)/shard_map/pallas_call | solution.py:151
  7.3 2.1 %collective-permute-done.refs_1_ = f32[512,128]{1,0:T(8,128)S(1)} collective-permute-done((f32[512,128]{1,0:T(8,128)}, f32[512,128]{1,0:T(8,128)S(1)}, u32[]{:S(2)}, u32[]{:S(2)}) %collective-permute-start) | collective-permute-done | bytes 262176 | tf_op jit(solution)/shard_map/ppermute | solution.py:135
  9.5 1.6 %shard_map.38 = (f32[64,1024]{1,0:T(8,128)S(1)}, f32[64,1024]{1,0:T(8,128)S(1)}, f32[64,1024]{1,0:T(8,128)S(1)}, f32[64,1024]{1,0:T(8,128)S(1)}) custom-call(f32[512,128]{1,0:T(8,128)S(1)} %copy-done.1, f32[512,128]{1,0:T(8,128)S(1)} %collective-permute-done.refs_1_, bf16[1024,1024]{1,0:T(8,128)(2,1)S(1)} %get-tuple-element.29.refs_2_.refs_3_, ...), custom_call_target="tpu_custom_call" | custom-call | flops 805306368 | tf_op jit(solution)/shard_map/pallas_call | solution.py:154
  11.1 3.4 %collective-permute-start.13 = (f32[64,1024]{1,0:T(8,128)S(1)}, f32[64,1024]{1,0:T(8,128)S(1)}, u32[]{:S(2)}, u32[]{:S(2)}) collective-permute-start(f32[64,1024]{1,0:T(8,128)S(1)} %get-tuple-element.43.refs_0_.refs_2_), channel_id=1, source_target_pairs={{0,30},{2,0},{4,2},{6,4},{8,6},{10,8},{12,10},{14,12},{16,14},{18,... | collective-permute-start | bytes 786440 | tf_op jit(solution)/shard_map/ppermute | solution.py:141
  14.5 4.4 %collective-permute-start.1 = (f32[64,1024]{1,0:T(8,128)S(1)}, f32[64,1024]{1,0:T(8,128)S(1)}, u32[]{:S(2)}, u32[]{:S(2)}) collective-permute-start(f32[64,1024]{1,0:T(8,128)S(1)} %get-tuple-element.31.refs_0_.refs_2_), channel_id=1, source_target_pairs={{0,30},{2,0},{4,2},{6,4},{8,6},{10,8},{12,10},{14,12},{16,14},{18,... | collective-permute-start | bytes 786440 | tf_op jit(solution)/shard_map/ppermute | solution.py:141
  19.0 5.8 %shard_map.39 = (bf16[1024,1024]{1,0:T(8,128)(2,1)S(1)}, bf16[1024,1024]{1,0:T(8,128)(2,1)S(1)}) custom-call(s32[2,48]{1,0:T(2,128)S(1)} %bitcast.5, f32[48,128,128]{2,1,0:T(8,128)S(1)} %bitcast.3), custom_call_target="tpu_custom_call" | custom-call | flops 402653184 | tf_op jit(solution)/shard_map/pallas_call | solution.py:160
  24.8 0.8 shard_map.47.refs_0_
  25.6 1.5 %collective-permute-start.15 = (f32[64,1024]{1,0:T(8,128)S(1)}, f32[64,1024]{1,0:T(8,128)S(1)}, u32[]{:S(2)}, u32[]{:S(2)}) collective-permute-start(f32[64,1024]{1,0:T(8,128)S(1)} %shard_map.47.refs_0_), channel_id=1, source_target_pairs={{0,1},{1,0},{2,3},{3,2},{4,5},{5,4},{6,7},{7,6},{8,9},{9,8},{10,11... | collective-permute-start | bytes 786440 | tf_op jit(solution)/shard_map/ppermute | solution.py:135
  27.5 0.8 shard_map.40.refs_0_
  28.3 1.5 %collective-permute-start.3 = (f32[64,1024]{1,0:T(8,128)S(1)}, f32[64,1024]{1,0:T(8,128)S(1)}, u32[]{:S(2)}, u32[]{:S(2)}) collective-permute-start(f32[64,1024]{1,0:T(8,128)S(1)} %shard_map.40.refs_0_), channel_id=1, source_target_pairs={{0,1},{1,0},{2,3},{3,2},{4,5},{5,4},{6,7},{7,6},{8,9},{9,8},{10,11... | collective-permute-start | bytes 786440 | tf_op jit(solution)/shard_map/ppermute | solution.py:135
  29.8 4.1 %collective-permute-done.15.refs_1_ = f32[64,1024]{1,0:T(8,128)S(1)} collective-permute-done((f32[64,1024]{1,0:T(8,128)S(1)}, f32[64,1024]{1,0:T(8,128)S(1)}, u32[]{:S(2)}, u32[]{:S(2)}) %collective-permute-start.15) | collective-permute-done | bytes 262176 | tf_op jit(solution)/shard_map/ppermute | solution.py:135
  34.0 0.8 shard_map.48
  34.8 2.9 %collective-permute-start.16 = (f32[64,1024]{1,0:T(8,128)S(1)}, f32[64,1024]{1,0:T(8,128)S(1)}, u32[]{:S(2)}, u32[]{:S(2)}) collective-permute-start(f32[64,1024]{1,0:T(8,128)S(1)} %get-tuple-element.45.refs_0_.refs_2_), channel_id=1, source_target_pairs={{0,30},{2,0},{4,2},{6,4},{8,6},{10,8},{12,10},{14,12},{16,14},{18,... | collective-permute-start | bytes 786440 | tf_op jit(solution)/shard_map/ppermute | solution.py:141
  37.7 0.8 shard_map.41
  38.5 4.5 %collective-permute-start.4 = (f32[64,1024]{1,0:T(8,128)S(1)}, f32[64,1024]{1,0:T(8,128)S(1)}, u32[]{:S(2)}, u32[]{:S(2)}) collective-permute-start(f32[64,1024]{1,0:T(8,128)S(1)} %get-tuple-element.35.refs_0_.refs_2_), channel_id=1, source_target_pairs={{0,30},{2,0},{4,2},{6,4},{8,6},{10,8},{12,10},{14,12},{16,14},{18,... | collective-permute-start | bytes 786440 | tf_op jit(solution)/shard_map/ppermute | solution.py:141
  43.0 3.2 %collective-permute-done.17.refs_3_ = f32[64,1024]{1,0:T(8,128)S(1)} collective-permute-done((f32[64,1024]{1,0:T(8,128)S(1)}, f32[64,1024]{1,0:T(8,128)S(1)}, u32[]{:S(2)}, u32[]{:S(2)}) %collective-permute-start.17) | collective-permute-done | bytes 262176 | tf_op jit(solution)/shard_map/ppermute | solution.py:141
  46.2 0.8 shard_map.49.refs_0_
  47.0 1.5 %collective-permute-start.18 = (f32[64,1024]{1,0:T(8,128)S(1)}, f32[64,1024]{1,0:T(8,128)S(1)}, u32[]{:S(2)}, u32[]{:S(2)}) collective-permute-start(f32[64,1024]{1,0:T(8,128)S(1)} %shard_map.49.refs_0_), channel_id=1, source_target_pairs={{0,1},{1,0},{2,3},{3,2},{4,5},{5,4},{6,7},{7,6},{8,9},{9,8},{10,11... | collective-permute-start | bytes 786440 | tf_op jit(solution)/shard_map/ppermute | solution.py:135
  48.5 2.9 %collective-permute-done.5.refs_3_ = f32[64,1024]{1,0:T(8,128)S(1)} collective-permute-done((f32[64,1024]{1,0:T(8,128)S(1)}, f32[64,1024]{1,0:T(8,128)S(1)}, u32[]{:S(2)}, u32[]{:S(2)}) %collective-permute-start.5) | collective-permute-done | bytes 262176 | tf_op jit(solution)/shard_map/ppermute | solution.py:141
  51.5 0.8 shard_map.42.refs_0_
  52.3 1.6 %collective-permute-start.6 = (f32[64,1024]{1,0:T(8,128)S(1)}, f32[64,1024]{1,0:T(8,128)S(1)}, u32[]{:S(2)}, u32[]{:S(2)}) collective-permute-start(f32[64,1024]{1,0:T(8,128)S(1)} %shard_map.42.refs_0_), channel_id=1, source_target_pairs={{0,1},{1,0},{2,3},{3,2},{4,5},{5,4},{6,7},{7,6},{8,9},{9,8},{10,11... | collective-permute-start | bytes 786440 | tf_op jit(solution)/shard_map/ppermute | solution.py:135
  53.8 0.8 shard_map.50
  54.6 2.6 %collective-permute-start.19 = (f32[64,1024]{1,0:T(8,128)S(1)}, f32[64,1024]{1,0:T(8,128)S(1)}, u32[]{:S(2)}, u32[]{:S(2)}) collective-permute-start(f32[64,1024]{1,0:T(8,128)S(1)} %get-tuple-element.47.refs_0_.refs_5_), channel_id=1, source_target_pairs={{0,30},{2,0},{4,2},{6,4},{8,6},{10,8},{12,10},{14,12},{16,14},{18,... | collective-permute-start | bytes 786440 | tf_op jit(solution)/shard_map/ppermute | solution.py:141
  57.3 1.5 %collective-permute-done.6.refs_1_ = f32[64,1024]{1,0:T(8,128)S(1)} collective-permute-done((f32[64,1024]{1,0:T(8,128)S(1)}, f32[64,1024]{1,0:T(8,128)S(1)}, u32[]{:S(2)}, u32[]{:S(2)}) %collective-permute-start.6) | collective-permute-done | bytes 262176 | tf_op jit(solution)/shard_map/ppermute | solution.py:135
  58.7 0.8 shard_map.43
  59.5 3.4 %collective-permute-start.7 = (f32[64,1024]{1,0:T(8,128)S(1)}, f32[64,1024]{1,0:T(8,128)S(1)}, u32[]{:S(2)}, u32[]{:S(2)}) collective-permute-start(f32[64,1024]{1,0:T(8,128)S(1)} %get-tuple-element.37.refs_0_.refs_4_), channel_id=1, source_target_pairs={{0,30},{2,0},{4,2},{6,4},{8,6},{10,8},{12,10},{14,12},{16,14},{18,... | collective-permute-start | bytes 786440 | tf_op jit(solution)/shard_map/ppermute | solution.py:141
  62.9 2.9 %collective-permute-done.20.refs_3_ = f32[64,1024]{1,0:T(8,128)S(1)} collective-permute-done((f32[64,1024]{1,0:T(8,128)S(1)}, f32[64,1024]{1,0:T(8,128)S(1)}, u32[]{:S(2)}, u32[]{:S(2)}) %collective-permute-start.20) | collective-permute-done | bytes 262176 | tf_op jit(solution)/shard_map/ppermute | solution.py:141
  65.8 0.8 shard_map.51.refs_0_
  66.6 1.5 %collective-permute-start.21 = (f32[64,1024]{1,0:T(8,128)S(1)}, f32[64,1024]{1,0:T(8,128)S(1)}, u32[]{:S(2)}, u32[]{:S(2)}) collective-permute-start(f32[64,1024]{1,0:T(8,128)S(1)} %shard_map.51.refs_0_), channel_id=1, source_target_pairs={{0,1},{1,0},{2,3},{3,2},{4,5},{5,4},{6,7},{7,6},{8,9},{9,8},{10,11... | collective-permute-start | bytes 786440 | tf_op jit(solution)/shard_map/ppermute | solution.py:135
  68.1 3.2 %collective-permute-done.8.refs_3_ = f32[64,1024]{1,0:T(8,128)S(1)} collective-permute-done((f32[64,1024]{1,0:T(8,128)S(1)}, f32[64,1024]{1,0:T(8,128)S(1)}, u32[]{:S(2)}, u32[]{:S(2)}) %collective-permute-start.8) | collective-permute-done | bytes 262176 | tf_op jit(solution)/shard_map/ppermute | solution.py:141
  71.4 0.8 shard_map.44.refs_0_
  72.2 1.5 %collective-permute-start.9 = (f32[64,1024]{1,0:T(8,128)S(1)}, f32[64,1024]{1,0:T(8,128)S(1)}, u32[]{:S(2)}, u32[]{:S(2)}) collective-permute-start(f32[64,1024]{1,0:T(8,128)S(1)} %shard_map.44.refs_0_), channel_id=1, source_target_pairs={{0,1},{1,0},{2,3},{3,2},{4,5},{5,4},{6,7},{7,6},{8,9},{9,8},{10,11... | collective-permute-start | bytes 786440 | tf_op jit(solution)/shard_map/ppermute | solution.py:135
  73.7 0.8 shard_map.52
  74.6 2.6 %collective-permute-start.22 = (f32[64,1024]{1,0:T(8,128)S(1)}, f32[64,1024]{1,0:T(8,128)S(1)}, u32[]{:S(2)}, u32[]{:S(2)}) collective-permute-start(f32[64,1024]{1,0:T(8,128)S(1)} %get-tuple-element.49.refs_0_), channel_id=1, source_target_pairs={{0,30},{2,0},{4,2},{6,4},{8,6},{10,8},{12,10},{14,12},{16,14},{18,... | collective-permute-start | bytes 786440 | tf_op jit(solution)/shard_map/ppermute | solution.py:141
  77.1 1.5 %collective-permute-done.9.refs_1_ = f32[64,1024]{1,0:T(8,128)S(1)} collective-permute-done((f32[64,1024]{1,0:T(8,128)S(1)}, f32[64,1024]{1,0:T(8,128)S(1)}, u32[]{:S(2)}, u32[]{:S(2)}) %collective-permute-start.9) | collective-permute-done | bytes 262176 | tf_op jit(solution)/shard_map/ppermute | solution.py:135
  78.6 0.8 shard_map.45
  79.4 3.2 %collective-permute-start.10 = (f32[64,1024]{1,0:T(8,128)S(1)}, f32[64,1024]{1,0:T(8,128)S(1)}, u32[]{:S(2)}, u32[]{:S(2)}) collective-permute-start(f32[64,1024]{1,0:T(8,128)S(1)} %get-tuple-element.39.refs_0_), channel_id=1, source_target_pairs={{0,30},{2,0},{4,2},{6,4},{8,6},{10,8},{12,10},{14,12},{16,14},{18,... | collective-permute-start | bytes 786440 | tf_op jit(solution)/shard_map/ppermute | solution.py:141
  82.7 2.9 %collective-permute-done.23.refs_3_ = f32[64,1024]{1,0:T(8,128)S(1)} collective-permute-done((f32[64,1024]{1,0:T(8,128)S(1)}, f32[64,1024]{1,0:T(8,128)S(1)}, u32[]{:S(2)}, u32[]{:S(2)}) %collective-permute-start.23) | collective-permute-done | bytes 262176 | tf_op jit(solution)/shard_map/ppermute | solution.py:141
  85.6 1.6 %shard_map.53 = (f32[64,1024]{1,0:T(8,128)}, f32[64,512]{1,0:T(8,128)S(1)}, f32[64,512]{1,0:T(8,128)S(1)}) custom-call(f32[64,1024]{1,0:T(8,128)S(1)} %get-tuple-element.49.refs_0_, f32[64,1024]{1,0:T(8,128)S(1)} %collective-permute-done.22.refs_1_, f32[64,1024]{1,0:T(8,128)S(1)} %get-tuple-element.50.refs_2_, ...), custom_call_target="tpu_custom_call" | custom-call | flops 402653184 | tf_op jit(solution)/shard_map/pallas_call | solution.py:185
  87.2 1.4 %collective-permute-start.24 = (f32[64,512]{1,0:T(8,128)S(1)}, f32[64,512]{1,0:T(8,128)S(1)}, u32[]{:S(2)}, u32[]{:S(2)}) collective-permute-start(f32[64,512]{1,0:T(8,128)S(1)} %get-tuple-element.52), channel_id=1, source_target_pairs={{0,1},{1,0},{2,3},{3,2},{4,5},{5,4},{6,7},{7,6},{8,9},{9,8},{10,11... | collective-permute-start | bytes 393224 | tf_op jit(solution)/shard_map/ppermute | solution.py:135
  88.6 2.5 %collective-permute-done.11.refs_3_ = f32[64,1024]{1,0:T(8,128)S(1)} collective-permute-done((f32[64,1024]{1,0:T(8,128)S(1)}, f32[64,1024]{1,0:T(8,128)S(1)}, u32[]{:S(2)}, u32[]{:S(2)}) %collective-permute-start.11) | collective-permute-done | bytes 262176 | tf_op jit(solution)/shard_map/ppermute | solution.py:141
  91.2 1.5 %shard_map.46 = (f32[64,1024]{1,0:T(8,128)}, f32[64,512]{1,0:T(8,128)S(1)}, f32[64,512]{1,0:T(8,128)S(1)}) custom-call(f32[64,1024]{1,0:T(8,128)S(1)} %get-tuple-element.39.refs_0_, f32[64,1024]{1,0:T(8,128)S(1)} %collective-permute-done.10.refs_1_, f32[64,1024]{1,0:T(8,128)S(1)} %get-tuple-element.40.refs_2_, ...), custom_call_target="tpu_custom_call" | custom-call | flops 402653184 | tf_op jit(solution)/shard_map/pallas_call | solution.py:185
  92.7 1.5 %collective-permute-start.12 = (f32[64,512]{1,0:T(8,128)S(1)}, f32[64,512]{1,0:T(8,128)S(1)}, u32[]{:S(2)}, u32[]{:S(2)}) collective-permute-start(f32[64,512]{1,0:T(8,128)S(1)} %get-tuple-element.42), channel_id=1, source_target_pairs={{0,1},{1,0},{2,3},{3,2},{4,5},{5,4},{6,7},{7,6},{8,9},{9,8},{10,11... | collective-permute-start | bytes 393224 | tf_op jit(solution)/shard_map/ppermute | solution.py:135
  94.2 3.5 %collective-permute-done.12.refs_1_ = f32[64,512]{1,0:T(8,128)S(1)} collective-permute-done((f32[64,512]{1,0:T(8,128)S(1)}, f32[64,512]{1,0:T(8,128)S(1)}, u32[]{:S(2)}, u32[]{:S(2)}) %collective-permute-start.12) | collective-permute-done | bytes 131104 | tf_op jit(solution)/shard_map/ppermute | solution.py:135
  97.7 0.8 shard_map.54
  (26 shorter events, 0.3 us)
Async XLA Ops:
  0.0 9.5 %collective-permute-start = (f32[512,128]{1,0:T(8,128)}, f32[512,128]{1,0:T(8,128)S(1)}, u32[]{:S(2)}, u32[]{:S(2)}) collective-permute-start(f32[512,128]{1,0:T(8,128)} %refs_0_.1), channel_id=1, source_target_pairs={{0,1},{1,0},{2,3},{3,2},{4,5},{5,4},{6,7},{7,6},{8,9},{9,8},{10,11... | collective-permute-start | bytes 786440 | tf_op jit(solution)/shard_map/ppermute | solution.py:135
  2.9 1.9 %copy-start = (f32[1,1,48,128,128]{4,3,2,1,0:T(8,128)S(1)}, f32[1,1,48,128,128]{4,3,2,1,0:T(8,128)}, u32[]{:S(2)}) copy-start(f32[1,1,48,128,128]{4,3,2,1,0:T(8,128)} %param.4) | copy-start | bytes 9437188
  4.8 0.7 copy-start.2
  5.5 3.9 %copy-start.1 = (f32[512,128]{1,0:T(8,128)S(1)}, f32[512,128]{1,0:T(8,128)}, u32[]{:S(2)}) copy-start(f32[512,128]{1,0:T(8,128)} %refs_0_.1) | copy-start | bytes 786436
  11.1 13.7 %collective-permute-start.13 = (f32[64,1024]{1,0:T(8,128)S(1)}, f32[64,1024]{1,0:T(8,128)S(1)}, u32[]{:S(2)}, u32[]{:S(2)}) collective-permute-start(f32[64,1024]{1,0:T(8,128)S(1)} %get-tuple-element.43.refs_0_.refs_2_), channel_id=1, source_target_pairs={{0,30},{2,0},{4,2},{6,4},{8,6},{10,8},{12,10},{14,12},{16,14},{18,... | collective-permute-start | bytes 786440 | tf_op jit(solution)/shard_map/ppermute | solution.py:141
  14.5 10.3 %collective-permute-start.14 = (f32[64,1024]{1,0:T(8,128)S(1)}, f32[64,1024]{1,0:T(8,128)S(1)}, u32[]{:S(2)}, u32[]{:S(2)}) collective-permute-start(f32[64,1024]{1,0:T(8,128)S(1)} %get-tuple-element.44.refs_2_), channel_id=1, source_target_pairs={{0,2},{2,4},{4,6},{6,8},{8,10},{10,12},{12,14},{14,16},{16,18},{18... | collective-permute-start | bytes 786440 | tf_op jit(solution)/shard_map/ppermute | solution.py:141
  14.5 12.7 %collective-permute-start.1 = (f32[64,1024]{1,0:T(8,128)S(1)}, f32[64,1024]{1,0:T(8,128)S(1)}, u32[]{:S(2)}, u32[]{:S(2)}) collective-permute-start(f32[64,1024]{1,0:T(8,128)S(1)} %get-tuple-element.31.refs_0_.refs_2_), channel_id=1, source_target_pairs={{0,30},{2,0},{4,2},{6,4},{8,6},{10,8},{12,10},{14,12},{16,14},{18,... | collective-permute-start | bytes 786440 | tf_op jit(solution)/shard_map/ppermute | solution.py:141
  19.0 8.5 %collective-permute-start.2 = (f32[64,1024]{1,0:T(8,128)S(1)}, f32[64,1024]{1,0:T(8,128)S(1)}, u32[]{:S(2)}, u32[]{:S(2)}) collective-permute-start(f32[64,1024]{1,0:T(8,128)S(1)} %get-tuple-element.32.refs_2_), channel_id=1, source_target_pairs={{0,2},{2,4},{4,6},{6,8},{8,10},{10,12},{12,14},{14,16},{16,18},{18... | collective-permute-start | bytes 786440 | tf_op jit(solution)/shard_map/ppermute | solution.py:141
  25.6 8.3 %collective-permute-start.15 = (f32[64,1024]{1,0:T(8,128)S(1)}, f32[64,1024]{1,0:T(8,128)S(1)}, u32[]{:S(2)}, u32[]{:S(2)}) collective-permute-start(f32[64,1024]{1,0:T(8,128)S(1)} %shard_map.47.refs_0_), channel_id=1, source_target_pairs={{0,1},{1,0},{2,3},{3,2},{4,5},{5,4},{6,7},{7,6},{8,9},{9,8},{10,11... | collective-permute-start | bytes 786440 | tf_op jit(solution)/shard_map/ppermute | solution.py:135
  28.3 9.4 %collective-permute-start.3 = (f32[64,1024]{1,0:T(8,128)S(1)}, f32[64,1024]{1,0:T(8,128)S(1)}, u32[]{:S(2)}, u32[]{:S(2)}) collective-permute-start(f32[64,1024]{1,0:T(8,128)S(1)} %shard_map.40.refs_0_), channel_id=1, source_target_pairs={{0,1},{1,0},{2,3},{3,2},{4,5},{5,4},{6,7},{7,6},{8,9},{9,8},{10,11... | collective-permute-start | bytes 786440 | tf_op jit(solution)/shard_map/ppermute | solution.py:135
  34.8 8.2 %collective-permute-start.16 = (f32[64,1024]{1,0:T(8,128)S(1)}, f32[64,1024]{1,0:T(8,128)S(1)}, u32[]{:S(2)}, u32[]{:S(2)}) collective-permute-start(f32[64,1024]{1,0:T(8,128)S(1)} %get-tuple-element.45.refs_0_.refs_2_), channel_id=1, source_target_pairs={{0,30},{2,0},{4,2},{6,4},{8,6},{10,8},{12,10},{14,12},{16,14},{18,... | collective-permute-start | bytes 786440 | tf_op jit(solution)/shard_map/ppermute | solution.py:141
  37.7 8.5 %collective-permute-start.17 = (f32[64,1024]{1,0:T(8,128)S(1)}, f32[64,1024]{1,0:T(8,128)S(1)}, u32[]{:S(2)}, u32[]{:S(2)}) collective-permute-start(f32[64,1024]{1,0:T(8,128)S(1)} %get-tuple-element.46.refs_2_), channel_id=1, source_target_pairs={{0,2},{2,4},{4,6},{6,8},{8,10},{10,12},{12,14},{14,16},{16,18},{18... | collective-permute-start | bytes 786440 | tf_op jit(solution)/shard_map/ppermute | solution.py:141
  38.5 10.1 %collective-permute-start.4 = (f32[64,1024]{1,0:T(8,128)S(1)}, f32[64,1024]{1,0:T(8,128)S(1)}, u32[]{:S(2)}, u32[]{:S(2)}) collective-permute-start(f32[64,1024]{1,0:T(8,128)S(1)} %get-tuple-element.35.refs_0_.refs_2_), channel_id=1, source_target_pairs={{0,30},{2,0},{4,2},{6,4},{8,6},{10,8},{12,10},{14,12},{16,14},{18,... | collective-permute-start | bytes 786440 | tf_op jit(solution)/shard_map/ppermute | solution.py:141
  43.0 8.5 %collective-permute-start.5 = (f32[64,1024]{1,0:T(8,128)S(1)}, f32[64,1024]{1,0:T(8,128)S(1)}, u32[]{:S(2)}, u32[]{:S(2)}) collective-permute-start(f32[64,1024]{1,0:T(8,128)S(1)} %get-tuple-element.36.refs_2_), channel_id=1, source_target_pairs={{0,2},{2,4},{4,6},{6,8},{8,10},{10,12},{12,14},{14,16},{16,18},{18... | collective-permute-start | bytes 786440 | tf_op jit(solution)/shard_map/ppermute | solution.py:141
  47.0 6.9 %collective-permute-start.18 = (f32[64,1024]{1,0:T(8,128)S(1)}, f32[64,1024]{1,0:T(8,128)S(1)}, u32[]{:S(2)}, u32[]{:S(2)}) collective-permute-start(f32[64,1024]{1,0:T(8,128)S(1)} %shard_map.49.refs_0_), channel_id=1, source_target_pairs={{0,1},{1,0},{2,3},{3,2},{4,5},{5,4},{6,7},{7,6},{8,9},{9,8},{10,11... | collective-permute-start | bytes 786440 | tf_op jit(solution)/shard_map/ppermute | solution.py:135
  52.3 6.4 %collective-permute-start.6 = (f32[64,1024]{1,0:T(8,128)S(1)}, f32[64,1024]{1,0:T(8,128)S(1)}, u32[]{:S(2)}, u32[]{:S(2)}) collective-permute-start(f32[64,1024]{1,0:T(8,128)S(1)} %shard_map.42.refs_0_), channel_id=1, source_target_pairs={{0,1},{1,0},{2,3},{3,2},{4,5},{5,4},{6,7},{7,6},{8,9},{9,8},{10,11... | collective-permute-start | bytes 786440 | tf_op jit(solution)/shard_map/ppermute | solution.py:135
  54.6 8.2 %collective-permute-start.19 = (f32[64,1024]{1,0:T(8,128)S(1)}, f32[64,1024]{1,0:T(8,128)S(1)}, u32[]{:S(2)}, u32[]{:S(2)}) collective-permute-start(f32[64,1024]{1,0:T(8,128)S(1)} %get-tuple-element.47.refs_0_.refs_5_), channel_id=1, source_target_pairs={{0,30},{2,0},{4,2},{6,4},{8,6},{10,8},{12,10},{14,12},{16,14},{18,... | collective-permute-start | bytes 786440 | tf_op jit(solution)/shard_map/ppermute | solution.py:141
  57.3 8.5 %collective-permute-start.20 = (f32[64,1024]{1,0:T(8,128)S(1)}, f32[64,1024]{1,0:T(8,128)S(1)}, u32[]{:S(2)}, u32[]{:S(2)}) collective-permute-start(f32[64,1024]{1,0:T(8,128)S(1)} %get-tuple-element.48.refs_2_), channel_id=1, source_target_pairs={{0,2},{2,4},{4,6},{6,8},{8,10},{10,12},{12,14},{14,16},{16,18},{18... | collective-permute-start | bytes 786440 | tf_op jit(solution)/shard_map/ppermute | solution.py:141
  59.5 8.6 %collective-permute-start.7 = (f32[64,1024]{1,0:T(8,128)S(1)}, f32[64,1024]{1,0:T(8,128)S(1)}, u32[]{:S(2)}, u32[]{:S(2)}) collective-permute-start(f32[64,1024]{1,0:T(8,128)S(1)} %get-tuple-element.37.refs_0_.refs_4_), channel_id=1, source_target_pairs={{0,30},{2,0},{4,2},{6,4},{8,6},{10,8},{12,10},{14,12},{16,14},{18,... | collective-permute-start | bytes 786440 | tf_op jit(solution)/shard_map/ppermute | solution.py:141
  62.9 8.5 %collective-permute-start.8 = (f32[64,1024]{1,0:T(8,128)S(1)}, f32[64,1024]{1,0:T(8,128)S(1)}, u32[]{:S(2)}, u32[]{:S(2)}) collective-permute-start(f32[64,1024]{1,0:T(8,128)S(1)} %get-tuple-element.38.refs_2_), channel_id=1, source_target_pairs={{0,2},{2,4},{4,6},{6,8},{8,10},{10,12},{12,14},{14,16},{16,18},{18... | collective-permute-start | bytes 786440 | tf_op jit(solution)/shard_map/ppermute | solution.py:141
  66.6 7.2 %collective-permute-start.21 = (f32[64,1024]{1,0:T(8,128)S(1)}, f32[64,1024]{1,0:T(8,128)S(1)}, u32[]{:S(2)}, u32[]{:S(2)}) collective-permute-start(f32[64,1024]{1,0:T(8,128)S(1)} %shard_map.51.refs_0_), channel_id=1, source_target_pairs={{0,1},{1,0},{2,3},{3,2},{4,5},{5,4},{6,7},{7,6},{8,9},{9,8},{10,11... | collective-permute-start | bytes 786440 | tf_op jit(solution)/shard_map/ppermute | solution.py:135
  72.2 6.4 %collective-permute-start.9 = (f32[64,1024]{1,0:T(8,128)S(1)}, f32[64,1024]{1,0:T(8,128)S(1)}, u32[]{:S(2)}, u32[]{:S(2)}) collective-permute-start(f32[64,1024]{1,0:T(8,128)S(1)} %shard_map.44.refs_0_), channel_id=1, source_target_pairs={{0,1},{1,0},{2,3},{3,2},{4,5},{5,4},{6,7},{7,6},{8,9},{9,8},{10,11... | collective-permute-start | bytes 786440 | tf_op jit(solution)/shard_map/ppermute | solution.py:135
  74.6 8.1 %collective-permute-start.22 = (f32[64,1024]{1,0:T(8,128)S(1)}, f32[64,1024]{1,0:T(8,128)S(1)}, u32[]{:S(2)}, u32[]{:S(2)}) collective-permute-start(f32[64,1024]{1,0:T(8,128)S(1)} %get-tuple-element.49.refs_0_), channel_id=1, source_target_pairs={{0,30},{2,0},{4,2},{6,4},{8,6},{10,8},{12,10},{14,12},{16,14},{18,... | collective-permute-start | bytes 786440 | tf_op jit(solution)/shard_map/ppermute | solution.py:141
  77.1 8.5 %collective-permute-start.23 = (f32[64,1024]{1,0:T(8,128)S(1)}, f32[64,1024]{1,0:T(8,128)S(1)}, u32[]{:S(2)}, u32[]{:S(2)}) collective-permute-start(f32[64,1024]{1,0:T(8,128)S(1)} %get-tuple-element.50.refs_2_), channel_id=1, source_target_pairs={{0,2},{2,4},{4,6},{6,8},{8,10},{10,12},{12,14},{14,16},{16,18},{18... | collective-permute-start | bytes 786440 | tf_op jit(solution)/shard_map/ppermute | solution.py:141
  79.4 9.2 %collective-permute-start.10 = (f32[64,1024]{1,0:T(8,128)S(1)}, f32[64,1024]{1,0:T(8,128)S(1)}, u32[]{:S(2)}, u32[]{:S(2)}) collective-permute-start(f32[64,1024]{1,0:T(8,128)S(1)} %get-tuple-element.39.refs_0_), channel_id=1, source_target_pairs={{0,30},{2,0},{4,2},{6,4},{8,6},{10,8},{12,10},{14,12},{16,14},{18,... | collective-permute-start | bytes 786440 | tf_op jit(solution)/shard_map/ppermute | solution.py:141
  82.7 8.5 %collective-permute-start.11 = (f32[64,1024]{1,0:T(8,128)S(1)}, f32[64,1024]{1,0:T(8,128)S(1)}, u32[]{:S(2)}, u32[]{:S(2)}) collective-permute-start(f32[64,1024]{1,0:T(8,128)S(1)} %get-tuple-element.40.refs_2_), channel_id=1, source_target_pairs={{0,2},{2,4},{4,6},{6,8},{8,10},{10,12},{12,14},{14,16},{16,18},{18... | collective-permute-start | bytes 786440 | tf_op jit(solution)/shard_map/ppermute | solution.py:141
  87.2 7.0 %collective-permute-start.24 = (f32[64,512]{1,0:T(8,128)S(1)}, f32[64,512]{1,0:T(8,128)S(1)}, u32[]{:S(2)}, u32[]{:S(2)}) collective-permute-start(f32[64,512]{1,0:T(8,128)S(1)} %get-tuple-element.52), channel_id=1, source_target_pairs={{0,1},{1,0},{2,3},{3,2},{4,5},{5,4},{6,7},{7,6},{8,9},{9,8},{10,11... | collective-permute-start | bytes 393224 | tf_op jit(solution)/shard_map/ppermute | solution.py:135
  92.7 5.0 %collective-permute-start.12 = (f32[64,512]{1,0:T(8,128)S(1)}, f32[64,512]{1,0:T(8,128)S(1)}, u32[]{:S(2)}, u32[]{:S(2)}) collective-permute-start(f32[64,512]{1,0:T(8,128)S(1)} %get-tuple-element.42), channel_id=1, source_target_pairs={{0,1},{1,0},{2,3},{3,2},{4,5},{5,4},{6,7},{7,6},{8,9},{9,8},{10,11... | collective-permute-start | bytes 393224 | tf_op jit(solution)/shard_map/ppermute | solution.py:135

commit v2 on v1

v2 whole, which is shorter than its diff:
```python
import functools
import math

import jax
import jax.numpy as jnp
from jax import lax
from jax.experimental import pallas as pl
from jax.experimental.pallas import tpu as pltpu
from jax.sharding import PartitionSpec as P

DEGREE = 4
GROUPS = 2
UNROLL = 4

first_scale = 0.4
later_scale = 0.8

VMEM = pl.BlockSpec(memory_space=pltpu.VMEM)
SMEM = pl.BlockSpec(memory_space=pltpu.SMEM)


def halves(values):
    high = values.astype(jnp.bfloat16)
    low = (values - high.astype(jnp.float32)).astype(jnp.bfloat16)
    return high, low


def product(left, high_ref, low_ref, strip):
    rows, depth = left.shape
    high, low = halves(left)
    both = jnp.concatenate([high, low], axis=0)
    for start in range(0, high_ref.shape[1], strip):
        at = slice(start, start + strip)
        main = jnp.dot(both, high_ref[:, at], preferred_element_type=jnp.float32)
        rest = jnp.dot(high, low_ref[:, at], preferred_element_type=jnp.float32)
        yield at, main[:rows] + main[rows:] + rest


def dense_kernel(lists_ref, blocks_ref, high_ref, low_ref, high_t_ref, low_t_ref):
    size = blocks_ref.shape[-1]
    for ref in (high_ref, low_ref, high_t_ref, low_t_ref):
        ref[...] = jnp.zeros_like(ref)

    @pl.loop(0, blocks_ref.shape[0], unroll=UNROLL)
    def _(k):
        row = pl.ds(pl.multiple_of(lists_ref[0, k] * size, size), size)
        col = pl.ds(pl.multiple_of(lists_ref[1, k] * size, size), size)
        block = blocks_ref[k]
        high_ref[row, col], low_ref[row, col] = halves(block)
        high_t_ref[col, row], low_t_ref[col, row] = halves(block.T)


def summed(terms):
    total = terms[0][...]
    for term in terms[1:]:
        total = total + term[...]
    return total


def partner_order(n_off, n_row):
    offset, row = lax.axis_index("off"), lax.axis_index("row")
    ahead_first = offset >= 0
    for distance in range(1, n_off):
        parity = lax.rem(lax.div(row, math.gcd(distance, n_row)), 2)
        ahead_first = jnp.where(offset == distance, parity == 0, ahead_first)
    return ahead_first


def write_products(ahead_first, total, high_ref, low_ref, first_ref, second_ref):
    for at, value in product(total, high_ref, low_ref, 256):
        first_ref[:, at] = jnp.where(ahead_first, value, total[:, at])
        second_ref[:, at] = jnp.where(ahead_first, total[:, at], value)


def turn_kernel(groups, piece_ref, *outs):
    turned = piece_ref[...].T
    width = turned.shape[0] // groups
    for group, out in enumerate(outs):
        out[...] = turned[group * width : (group + 1) * width]


def first_kernel(n_off, n_row, *refs):
    pieces, (high_ref, low_ref, vectors_ref, first_ref, second_ref) = refs[:n_off], refs[n_off:]
    rows = pieces[0].shape[1]
    for step, piece in enumerate(pieces):
        owner = lax.rem(lax.axis_index("off") - step + n_off, n_off)
        vectors_ref[:, pl.ds(pl.multiple_of(owner * rows, rows), rows)] = piece[...]
    write_products(
        partner_order(n_off, n_row), vectors_ref[...], high_ref, low_ref, first_ref, second_ref
    )


def step_kernel(n_off, n_row, scale, *refs):
    high_ref, low_ref, vectors_ref, first_ref, second_ref = refs[-5:]
    total = scale * summed(refs[:n_off])
    if len(refs) > n_off + 5:
        total = total - refs[n_off][...]
    vectors_ref[...] = total
    write_products(partner_order(n_off, n_row), total, high_ref, low_ref, first_ref, second_ref)


def far_kernel(n_off, n_row, *refs):
    seconds, firsts = refs[:n_off], refs[n_off : 2 * n_off]
    high_ref, low_ref, total_ref, *outs = refs[2 * n_off :]
    offset = lax.axis_index("off")
    ahead_first = partner_order(n_off, n_row)

    def chosen(own, if_ahead, if_not, at):
        value = own[:, at]
        for distance in range(1, n_off):
            swapped = jnp.where(ahead_first, if_ahead[distance][:, at], if_not[distance][:, at])
            value = jnp.where(offset == distance, swapped, value)
        return value

    far = chosen(seconds[0], firsts, seconds, slice(None))
    for at, value in product(far, high_ref, low_ref, 256):
        total_ref[:, at] = value + chosen(firsts[0], seconds, firsts, at)
    for step, out in enumerate(outs):
        rows = out.shape[1]
        owner = lax.rem(offset + step, n_off)
        out[...] = total_ref[:, pl.ds(pl.multiple_of(owner * rows, rows), rows)]


def last_kernel(n_off, groups, *refs):
    out_ref = refs[-1]
    rows = out_ref.shape[0]
    at = pl.ds(pl.multiple_of(lax.axis_index("off") * rows, rows), rows)
    result = []
    for group in range(groups):
        total = summed(refs[group * n_off : (group + 1) * n_off])
        result.append(later_scale * total - refs[groups * n_off + group][:, at])
    out_ref[...] = jnp.concatenate(result, axis=0).T


def kernel_call(body, in_specs, shapes, scratch=(), flops=0, limit=24):
    return pl.pallas_call(
        body,
        out_shape=shapes,
        in_specs=in_specs,
        out_specs=[VMEM] * len(shapes),
        scratch_shapes=list(scratch),
        compiler_params=pltpu.CompilerParams(vmem_limit_bytes=limit * 2**20),
        cost_estimate=pl.CostEstimate(flops=flops, bytes_accessed=0, transcendentals=0),
    )


def per_device(vectors, blocks, lists):
    n_off = lax.axis_size("off")
    n_row = lax.axis_size("row")
    piece_rows, width = vectors.shape
    tile_rows = piece_rows * n_off
    group_width = width // GROUPS

    def shifted(value, distance):
        return lax.ppermute(value, "off", [(d, (d + distance) % n_off) for d in range(n_off)])

    def swapped(value, ahead):
        values = [value]
        for distance in range(1, n_off):
            step = math.gcd(distance, n_row)
            assert n_row // step % 2 == 0
            route = [
                (i, (i + (distance if (i // step + ahead) % 2 else -distance)) % n_row)
                for i in range(n_row)
            ]
            values.append(lax.ppermute(value, "row", route))
        return values

    f32 = lambda *shape: jax.ShapeDtypeStruct(shape, jnp.float32)
    bf16 = jax.ShapeDtypeStruct((tile_rows, tile_rows), jnp.bfloat16)
    group_shape = f32(group_width, tile_rows)
    piece_shape = f32(group_width, piece_rows)
    flops = 6 * group_width * tile_rows * tile_rows

    pieces = kernel_call(functools.partial(turn_kernel, GROUPS), [VMEM], [piece_shape] * GROUPS)(
        vectors
    )
    pieces = [[piece] + [shifted(piece, s) for s in range(1, n_off)] for piece in pieces]
    high, low, high_t, low_t = kernel_call(
        dense_kernel, [SMEM, VMEM], [bf16] * 4, flops=flops
    )(lists[0, 0], blocks[0, 0])

    older, newer = [None] * GROUPS, [None] * GROUPS
    totals = [None] * GROUPS
    for degree in range(DEGREE):
        scale = first_scale if degree == 1 else later_scale
        firsts, seconds = [None] * GROUPS, [None] * GROUPS
        for g in range(GROUPS):
            if degree == 0:
                body = functools.partial(first_kernel, n_off, n_row)
                terms = pieces[g]
            else:
                body = functools.partial(step_kernel, n_off, n_row, scale)
                terms = [totals[g]] + [shifted(totals[g], s) for s in range(1, n_off)]
                terms += [older[g]] if degree > 1 else []
            older[g] = newer[g]
            newer[g], first, second = kernel_call(
                body, [VMEM] * (len(terms) + 2), [group_shape] * 3, flops=flops
            )(*terms, high, low)
            seconds[g] = swapped(second, 0)
            firsts[g] = swapped(first, 1)
        for g in range(GROUPS):
            pieces_out = n_off if degree == DEGREE - 1 else 0
            outs = kernel_call(
                functools.partial(far_kernel, n_off, n_row),
                [VMEM] * (2 * n_off + 2),
                [group_shape] + [piece_shape] * pieces_out,
                flops=flops,
            )(*seconds[g], *firsts[g], high_t, low_t)
            totals[g] = outs[1:] if pieces_out else outs[0]
    terms = []
    for g in range(GROUPS):
        terms.append(totals[g][0])
        terms.extend(shifted(totals[g][s], s) for s in range(1, n_off))
    [result] = kernel_call(
        functools.partial(last_kernel, n_off, GROUPS),
        [VMEM] * (GROUPS * (n_off + 1)),
        [f32(piece_rows, width)],
    )(*terms, *older)
    return result


def solution(mesh):
    in_specs = (
        P(("row", "off"), None),
        P("row", "off", None, None, None),
        P("row", "off", None, None),
    )
    out_specs = P(("row", "off"), None)
    return jax.shard_map(
        per_device, mesh=mesh, in_specs=in_specs, out_specs=out_specs, check_vma=False
    )
```

time: 98.7 us -> 89.7 us (0.909)
  waiting for transfers between devices: 30.8 us -> 22.6 us
  Pallas kernels: 22.8 us -> 19.9 us
    ppermute x16, waiting for transfers between devices: 18 us -> 12.5 us  [swapped(): values.append(lax.ppermute(value, 'row', route))]
    ppermute x9 -> x10, starting transfers between devices: 15.1 us -> 19.6 us  [shifted(): lax.ppermute(value, 'off', [(d, (d + distance) % n_off) for d in range(n_...]
    ppermute x16, starting transfers between devices: 27.1 us -> 23.4 us  [swapped(): values.append(lax.ppermute(value, 'row', route))]
    pallas_call x17 -> x18, Pallas kernels: 22 us -> 19 us  [the longest x8 8.05 us: per_device(): kernel_call(functools.partial(far_kernel, n_off, n_row), [VMEM] * (2 * n_...]
    ppermute x9 -> x10, waiting for transfers between devices: 12.8 us -> 10.1 us  [shifted(): lax.ppermute(value, 'off', [(d, (d + distance) % n_off) for d in range(n_...]
  transfers between devices with their start and end apart: 25 -> 26, of which waited for: 12 -> 13; matrix products, arithmetic and copies ran while one was open for 0% -> 0% of each run, Pallas kernels for 21% -> 21%
where the time goes in v2:
time: 89.7 us; the launch traced here: 89.2 us
  starting transfers between devices  43.1 us (48%)
  waiting for transfers between devices  22.6 us (25%)
  Pallas kernels  19.9 us (22%)
  local copies, waits for them, and re-layouts  3.52 us (4%)
    ppermute x16, starting transfers between devices, swapped(): values.append(lax.ppermute(value, 'row', route))  23.4 us
    ppermute x10, starting transfers between devices, shifted(): lax.ppermute(value, 'off', [(d, (d + distance) % n_off) for d in range(n_...  19.6 us
    ppermute x16, waiting for transfers between devices, swapped(): values.append(lax.ppermute(value, 'row', route))  12.5 us
    ppermute x10, waiting for transfers between devices, shifted(): lax.ppermute(value, 'off', [(d, (d + distance) % n_off) for d in range(n_...  10.1 us
    pallas_call x8, Pallas kernels, per_device(): kernel_call(functools.partial(far_kernel, n_off, n_row), [VMEM] * (2 * n_...  8.05 us
    pallas_call x8, Pallas kernels, per_device(): kernel_call(body, [VMEM] * (len(terms) + 2), [group_shape] * 3, flops=flops)  7.63 us
    unnamed x6, local copies, waits for them, and re-layouts  3.52 us
    pallas_call x1, Pallas kernels, per_device(): kernel_call(dense_kernel, [SMEM, VMEM], [bf16] * 4, flops=flops)  3.23 us
  transfers between devices with their start and end apart: 26, of which 13 were waited for; matrix products, arithmetic and copies ran while one was open for 0% of the time, Pallas kernels for 21%

profile of v2, /device:TPU:0, one launch (start us, length us, event | category | flops | bytes accessed | tf_op | source)
XLA Modules:
  0.0 89.2 jit_solution(2043963442837023085)
XLA Ops:
  0.0 0.9 %copy-done.1 = f32[512,128]{1,0:T(8,128)S(1)} copy-done((f32[512,128]{1,0:T(8,128)S(1)}, f32[512,128]{1,0:T(8,128)}, u32[]{:S(2)}) %copy-start.1) | copy-done | bytes 262168
  1.1 3.0 %collective-permute-start.13 = (f32[64,512]{1,0:T(8,128)S(1)}, f32[64,512]{1,0:T(8,128)S(1)}, u32[]{:S(2)}, u32[]{:S(2)}) collective-permute-start(f32[64,512]{1,0:T(8,128)S(1)} %get-tuple-element.54.refs_0_), channel_id=1, source_target_pairs={{0,1},{1,0},{2,3},{3,2},{4,5},{5,4},{6,7},{7,6},{8,9},{9,8},{10,11... | collective-permute-start | bytes 393224 | tf_op jit(solution)/shard_map/ppermute | solution.py:155
  4.2 1.9 %copy-done = f32[1,1,48,128,128]{4,3,2,1,0:T(8,128)S(1)} copy-done((f32[1,1,48,128,128]{4,3,2,1,0:T(8,128)S(1)}, f32[1,1,48,128,128]{4,3,2,1,0:T(8,128)}, u32[]{:S(2)}) %copy-start) | copy-done | bytes 3145752
  6.7 3.2 %shard_map.38 = (bf16[1024,1024]{1,0:T(8,128)(2,1)S(1)}, bf16[1024,1024]{1,0:T(8,128)(2,1)S(1)}, bf16[1024,1024]{1,0:T(8,128)(2,1)S(1)}, bf16[1024,1024]{1,0:T(8,128)(2,1)S(1)}) custom-call(s32[2,48]{1,0:T(2,128)S(1)} %bitcast.3, f32[48,128,128]{2,1,0:T(8,128)S(1)} %bitcast.2), custom_call_target="tpu_custom_call" | custom-call | flops 402653184 | tf_op jit(solution)/shard_map/pallas_call | solution.py:179
  10.0 0.8 shard_map.47
  10.8 4.0 %collective-permute-start.14 = (f32[64,1024]{1,0:T(8,128)S(1)}, f32[64,1024]{1,0:T(8,128)S(1)}, u32[]{:S(2)}, u32[]{:S(2)}) collective-permute-start(f32[64,1024]{1,0:T(8,128)S(1)} %get-tuple-element.55.refs_0_), channel_id=1, source_target_pairs={{0,30},{2,4},{4,2},{6,8},{8,6},{10,12},{12,10},{14,16},{16,14},{18... | collective-permute-start | bytes 786440 | tf_op jit(solution)/shard_map/ppermute | solution.py:166
  14.8 0.8 shard_map.39
  15.6 1.4 %collective-permute-start.1 = (f32[64,1024]{1,0:T(8,128)S(1)}, f32[64,1024]{1,0:T(8,128)S(1)}, u32[]{:S(2)}, u32[]{:S(2)}) collective-permute-start(f32[64,1024]{1,0:T(8,128)S(1)} %get-tuple-element.40.refs_0_), channel_id=1, source_target_pairs={{0,30},{2,4},{4,2},{6,8},{8,6},{10,12},{12,10},{14,16},{16,14},{18... | collective-permute-start | bytes 786440 | tf_op jit(solution)/shard_map/ppermute | solution.py:166
  17.0 2.5 %collective-permute-done.14.refs_1_ = f32[64,1024]{1,0:T(8,128)S(1)} collective-permute-done((f32[64,1024]{1,0:T(8,128)S(1)}, f32[64,1024]{1,0:T(8,128)S(1)}, u32[]{:S(2)}, u32[]{:S(2)}) %collective-permute-start.14) | collective-permute-done | bytes 262176 | tf_op jit(solution)/shard_map/ppermute | solution.py:166
  19.5 0.8 shard_map.48.refs_0_
  20.3 2.0 %collective-permute-start.16 = (f32[64,1024]{1,0:T(8,128)S(1)}, f32[64,1024]{1,0:T(8,128)S(1)}, u32[]{:S(2)}, u32[]{:S(2)}) collective-permute-start(f32[64,1024]{1,0:T(8,128)S(1)} %shard_map.48.refs_0_), channel_id=1, source_target_pairs={{0,1},{1,0},{2,3},{3,2},{4,5},{5,4},{6,7},{7,6},{8,9},{9,8},{10,11... | collective-permute-start | bytes 786440 | tf_op jit(solution)/shard_map/ppermute | solution.py:155
  22.3 1.9 %collective-permute-done.1.refs_1_ = f32[64,1024]{1,0:T(8,128)S(1)} collective-permute-done((f32[64,1024]{1,0:T(8,128)S(1)}, f32[64,1024]{1,0:T(8,128)S(1)}, u32[]{:S(2)}, u32[]{:S(2)}) %collective-permute-start.1) | collective-permute-done | bytes 262176 | tf_op jit(solution)/shard_map/ppermute | solution.py:166
  24.3 0.8 shard_map.40.refs_0_
  25.1 1.5 %collective-permute-start.3 = (f32[64,1024]{1,0:T(8,128)S(1)}, f32[64,1024]{1,0:T(8,128)S(1)}, u32[]{:S(2)}, u32[]{:S(2)}) collective-permute-start(f32[64,1024]{1,0:T(8,128)S(1)} %shard_map.40.refs_0_), channel_id=1, source_target_pairs={{0,1},{1,0},{2,3},{3,2},{4,5},{5,4},{6,7},{7,6},{8,9},{9,8},{10,11... | collective-permute-start | bytes 786440 | tf_op jit(solution)/shard_map/ppermute | solution.py:155
  26.6 1.4 %collective-permute-done.16.refs_1_ = f32[64,1024]{1,0:T(8,128)S(1)} collective-permute-done((f32[64,1024]{1,0:T(8,128)S(1)}, f32[64,1024]{1,0:T(8,128)S(1)}, u32[]{:S(2)}, u32[]{:S(2)}) %collective-permute-start.16) | collective-permute-done | bytes 262176 | tf_op jit(solution)/shard_map/ppermute | solution.py:155
  28.9 1.8 %collective-permute-start.17 = (f32[64,1024]{1,0:T(8,128)S(1)}, f32[64,1024]{1,0:T(8,128)S(1)}, u32[]{:S(2)}, u32[]{:S(2)}) collective-permute-start(f32[64,1024]{1,0:T(8,128)S(1)} %get-tuple-element.57.refs_0_), channel_id=1, source_target_pairs={{0,30},{2,4},{4,2},{6,8},{8,6},{10,12},{12,10},{14,16},{16,14},{18... | collective-permute-start | bytes 786440 | tf_op jit(solution)/shard_map/ppermute | solution.py:166
  30.7 1.9 %collective-permute-start.18 = (f32[64,1024]{1,0:T(8,128)S(1)}, f32[64,1024]{1,0:T(8,128)S(1)}, u32[]{:S(2)}, u32[]{:S(2)}) collective-permute-start(f32[64,1024]{1,0:T(8,128)S(1)} %get-tuple-element.58.refs_2_), channel_id=1, source_target_pairs={{0,2},{2,0},{4,6},{6,4},{8,10},{10,8},{12,14},{14,12},{16,18},{18,... | collective-permute-start | bytes 786440 | tf_op jit(solution)/shard_map/ppermute | solution.py:166
  32.5 1.9 %collective-permute-done.3.refs_1_ = f32[64,1024]{1,0:T(8,128)S(1)} collective-permute-done((f32[64,1024]{1,0:T(8,128)S(1)}, f32[64,1024]{1,0:T(8,128)S(1)}, u32[]{:S(2)}, u32[]{:S(2)}) %collective-permute-start.3) | collective-permute-done | bytes 262176 | tf_op jit(solution)/shard_map/ppermute | solution.py:155
  35.2 2.4 %collective-permute-start.4 = (f32[64,1024]{1,0:T(8,128)S(1)}, f32[64,1024]{1,0:T(8,128)S(1)}, u32[]{:S(2)}, u32[]{:S(2)}) collective-permute-start(f32[64,1024]{1,0:T(8,128)S(1)} %get-tuple-element.44.refs_0_), channel_id=1, source_target_pairs={{0,30},{2,4},{4,2},{6,8},{8,6},{10,12},{12,10},{14,16},{16,14},{18... | collective-permute-start | bytes 786440 | tf_op jit(solution)/shard_map/ppermute | solution.py:166
  37.7 0.8 shard_map.50.refs_0_
  38.5 2.4 %collective-permute-start.19 = (f32[64,1024]{1,0:T(8,128)S(1)}, f32[64,1024]{1,0:T(8,128)S(1)}, u32[]{:S(2)}, u32[]{:S(2)}) collective-permute-start(f32[64,1024]{1,0:T(8,128)S(1)} %shard_map.50.refs_0_), channel_id=1, source_target_pairs={{0,1},{1,0},{2,3},{3,2},{4,5},{5,4},{6,7},{7,6},{8,9},{9,8},{10,11... | collective-permute-start | bytes 786440 | tf_op jit(solution)/shard_map/ppermute | solution.py:155
  40.9 3.0 %collective-permute-done.4.refs_1_ = f32[64,1024]{1,0:T(8,128)S(1)} collective-permute-done((f32[64,1024]{1,0:T(8,128)S(1)}, f32[64,1024]{1,0:T(8,128)S(1)}, u32[]{:S(2)}, u32[]{:S(2)}) %collective-permute-start.4) | collective-permute-done | bytes 262176 | tf_op jit(solution)/shard_map/ppermute | solution.py:166
  43.9 0.8 shard_map.42.refs_0_
  44.7 1.8 %collective-permute-start.6 = (f32[64,1024]{1,0:T(8,128)S(1)}, f32[64,1024]{1,0:T(8,128)S(1)}, u32[]{:S(2)}, u32[]{:S(2)}) collective-permute-start(f32[64,1024]{1,0:T(8,128)S(1)} %shard_map.42.refs_0_), channel_id=1, source_target_pairs={{0,1},{1,0},{2,3},{3,2},{4,5},{5,4},{6,7},{7,6},{8,9},{9,8},{10,11... | collective-permute-start | bytes 786440 | tf_op jit(solution)/shard_map/ppermute | solution.py:155
  46.6 0.8 shard_map.51
  47.4 1.9 %collective-permute-start.20 = (f32[64,1024]{1,0:T(8,128)S(1)}, f32[64,1024]{1,0:T(8,128)S(1)}, u32[]{:S(2)}, u32[]{:S(2)}) collective-permute-start(f32[64,1024]{1,0:T(8,128)S(1)} %get-tuple-element.60.refs_0_), channel_id=1, source_target_pairs={{0,30},{2,4},{4,2},{6,8},{8,6},{10,12},{12,10},{14,16},{16,14},{18... | collective-permute-start | bytes 786440 | tf_op jit(solution)/shard_map/ppermute | solution.py:166
  49.3 1.7 %collective-permute-start.21 = (f32[64,1024]{1,0:T(8,128)S(1)}, f32[64,1024]{1,0:T(8,128)S(1)}, u32[]{:S(2)}, u32[]{:S(2)}) collective-permute-start(f32[64,1024]{1,0:T(8,128)S(1)} %get-tuple-element.61.refs_2_), channel_id=1, source_target_pairs={{0,2},{2,0},{4,6},{6,4},{8,10},{10,8},{12,14},{14,12},{16,18},{18,... | collective-permute-start | bytes 786440 | tf_op jit(solution)/shard_map/ppermute | solution.py:166
  50.9 1.6 %collective-permute-done.6.refs_1_ = f32[64,1024]{1,0:T(8,128)S(1)} collective-permute-done((f32[64,1024]{1,0:T(8,128)S(1)}, f32[64,1024]{1,0:T(8,128)S(1)}, u32[]{:S(2)}, u32[]{:S(2)}) %collective-permute-start.6) | collective-permute-done | bytes 262176 | tf_op jit(solution)/shard_map/ppermute | solution.py:155
  52.5 0.8 shard_map.43
  53.8 1.2 %collective-permute-start.8 = (f32[64,1024]{1,0:T(8,128)S(1)}, f32[64,1024]{1,0:T(8,128)S(1)}, u32[]{:S(2)}, u32[]{:S(2)}) collective-permute-start(f32[64,1024]{1,0:T(8,128)S(1)} %get-tuple-element.48.refs_2_), channel_id=1, source_target_pairs={{0,2},{2,0},{4,6},{6,4},{8,10},{10,8},{12,14},{14,12},{16,18},{18,... | collective-permute-start | bytes 786440 | tf_op jit(solution)/shard_map/ppermute | solution.py:166
  55.0 1.1 %collective-permute-done.20.refs_1_ = f32[64,1024]{1,0:T(8,128)S(1)} collective-permute-done((f32[64,1024]{1,0:T(8,128)S(1)}, f32[64,1024]{1,0:T(8,128)S(1)}, u32[]{:S(2)}, u32[]{:S(2)}) %collective-permute-start.20) | collective-permute-done | bytes 262176 | tf_op jit(solution)/shard_map/ppermute | solution.py:166
  56.1 0.8 shard_map.52.refs_0_
  56.9 2.4 %collective-permute-start.22 = (f32[64,1024]{1,0:T(8,128)S(1)}, f32[64,1024]{1,0:T(8,128)S(1)}, u32[]{:S(2)}, u32[]{:S(2)}) collective-permute-start(f32[64,1024]{1,0:T(8,128)S(1)} %shard_map.52.refs_0_), channel_id=1, source_target_pairs={{0,1},{1,0},{2,3},{3,2},{4,5},{5,4},{6,7},{7,6},{8,9},{9,8},{10,11... | collective-permute-start | bytes 786440 | tf_op jit(solution)/shard_map/ppermute | solution.py:155
  59.3 2.7 %collective-permute-done.7.refs_1_ = f32[64,1024]{1,0:T(8,128)S(1)} collective-permute-done((f32[64,1024]{1,0:T(8,128)S(1)}, f32[64,1024]{1,0:T(8,128)S(1)}, u32[]{:S(2)}, u32[]{:S(2)}) %collective-permute-start.7) | collective-permute-done | bytes 262176 | tf_op jit(solution)/shard_map/ppermute | solution.py:166
  62.0 0.8 shard_map.44.refs_0_
  62.8 1.8 %collective-permute-start.9 = (f32[64,1024]{1,0:T(8,128)S(1)}, f32[64,1024]{1,0:T(8,128)S(1)}, u32[]{:S(2)}, u32[]{:S(2)}) collective-permute-start(f32[64,1024]{1,0:T(8,128)S(1)} %shard_map.44.refs_0_), channel_id=1, source_target_pairs={{0,1},{1,0},{2,3},{3,2},{4,5},{5,4},{6,7},{7,6},{8,9},{9,8},{10,11... | collective-permute-start | bytes 786440 | tf_op jit(solution)/shard_map/ppermute | solution.py:155
  64.6 1.2 %collective-permute-done.22.refs_1_ = f32[64,1024]{1,0:T(8,128)S(1)} collective-permute-done((f32[64,1024]{1,0:T(8,128)S(1)}, f32[64,1024]{1,0:T(8,128)S(1)}, u32[]{:S(2)}, u32[]{:S(2)}) %collective-permute-start.22) | collective-permute-done | bytes 262176 | tf_op jit(solution)/shard_map/ppermute | solution.py:155
  65.8 1.4 %shard_map.53 = (f32[64,1024]{1,0:T(8,128)}, f32[64,1024]{1,0:T(8,128)S(1)}, f32[64,1024]{1,0:T(8,128)S(1)}) custom-call(f32[64,1024]{1,0:T(8,128)S(1)} %shard_map.52.refs_0_, f32[64,1024]{1,0:T(8,128)S(1)} %collective-permute-done.22.refs_1_, f32[64,1024]{1,0:T(8,128)S(1)} %get-tuple-element.62.refs_2_, ...), custom_call_target="tpu_custom_call" | custom-call | flops 402653184 | tf_op jit(solution)/shard_map/pallas_call | solution.py:197
  67.2 3.3 %collective-permute-start.24 = (f32[64,1024]{1,0:T(8,128)S(1)}, f32[64,1024]{1,0:T(8,128)S(1)}, u32[]{:S(2)}, u32[]{:S(2)}) collective-permute-start(f32[64,1024]{1,0:T(8,128)S(1)} %get-tuple-element.64.refs_2_), channel_id=1, source_target_pairs={{0,2},{2,0},{4,6},{6,4},{8,10},{10,8},{12,14},{14,12},{16,18},{18,... | collective-permute-start | bytes 786440 | tf_op jit(solution)/shard_map/ppermute | solution.py:166
  71.1 1.4 %shard_map.45 = (f32[64,1024]{1,0:T(8,128)}, f32[64,1024]{1,0:T(8,128)S(1)}, f32[64,1024]{1,0:T(8,128)S(1)}) custom-call(f32[64,1024]{1,0:T(8,128)S(1)} %shard_map.44.refs_0_, f32[64,1024]{1,0:T(8,128)S(1)} %collective-permute-done.9.refs_1_, f32[64,1024]{1,0:T(8,128)S(1)} %get-tuple-element.49.refs_2_, ...), custom_call_target="tpu_custom_call" | custom-call | flops 402653184 | tf_op jit(solution)/shard_map/pallas_call | solution.py:197
  72.5 3.4 %collective-permute-start.10 = (f32[64,1024]{1,0:T(8,128)S(1)}, f32[64,1024]{1,0:T(8,128)S(1)}, u32[]{:S(2)}, u32[]{:S(2)}) collective-permute-start(f32[64,1024]{1,0:T(8,128)S(1)} %get-tuple-element.50.refs_0_), channel_id=1, source_target_pairs={{0,30},{2,4},{4,2},{6,8},{8,6},{10,12},{12,10},{14,16},{16,14},{18... | collective-permute-start | bytes 786440 | tf_op jit(solution)/shard_map/ppermute | solution.py:166
  75.9 1.6 %shard_map.54 = (f32[64,1024]{1,0:T(8,128)}, f32[64,512]{1,0:T(8,128)S(1)}, f32[64,512]{1,0:T(8,128)S(1)}) custom-call(f32[64,1024]{1,0:T(8,128)S(1)} %get-tuple-element.63.refs_0_, f32[64,1024]{1,0:T(8,128)S(1)} %collective-permute-done.23.refs_1_, f32[64,1024]{1,0:T(8,128)S(1)} %get-tuple-element.64.refs_2_, ...), custom_call_target="tpu_custom_call" | custom-call | flops 402653184 | tf_op jit(solution)/shard_map/pallas_call | solution.py:204
  77.5 2.3 %collective-permute-start.25 = (f32[64,512]{1,0:T(8,128)S(1)}, f32[64,512]{1,0:T(8,128)S(1)}, u32[]{:S(2)}, u32[]{:S(2)}) collective-permute-start(f32[64,512]{1,0:T(8,128)S(1)} %get-tuple-element.66), channel_id=1, source_target_pairs={{0,1},{1,0},{2,3},{3,2},{4,5},{5,4},{6,7},{7,6},{8,9},{9,8},{10,11... | collective-permute-start | bytes 393224 | tf_op jit(solution)/shard_map/ppermute | solution.py:155
  79.7 1.3 %collective-permute-done.10.refs_1_ = f32[64,1024]{1,0:T(8,128)S(1)} collective-permute-done((f32[64,1024]{1,0:T(8,128)S(1)}, f32[64,1024]{1,0:T(8,128)S(1)}, u32[]{:S(2)}, u32[]{:S(2)}) %collective-permute-start.10) | collective-permute-done | bytes 262176 | tf_op jit(solution)/shard_map/ppermute | solution.py:166
  81.1 1.6 %shard_map.46 = (f32[64,1024]{1,0:T(8,128)}, f32[64,512]{1,0:T(8,128)S(1)}, f32[64,512]{1,0:T(8,128)S(1)}) custom-call(f32[64,1024]{1,0:T(8,128)S(1)} %get-tuple-element.50.refs_0_, f32[64,1024]{1,0:T(8,128)S(1)} %collective-permute-done.10.refs_1_, f32[64,1024]{1,0:T(8,128)S(1)} %get-tuple-element.51.refs_2_, ...), custom_call_target="tpu_custom_call" | custom-call | flops 402653184 | tf_op jit(solution)/shard_map/pallas_call | solution.py:204
  82.6 2.3 %collective-permute-start.12 = (f32[64,512]{1,0:T(8,128)S(1)}, f32[64,512]{1,0:T(8,128)S(1)}, u32[]{:S(2)}, u32[]{:S(2)}) collective-permute-start(f32[64,512]{1,0:T(8,128)S(1)} %get-tuple-element.53), channel_id=1, source_target_pairs={{0,1},{1,0},{2,3},{3,2},{4,5},{5,4},{6,7},{7,6},{8,9},{9,8},{10,11... | collective-permute-start | bytes 393224 | tf_op jit(solution)/shard_map/ppermute | solution.py:155
  85.0 3.4 %collective-permute-done.12.refs_1_ = f32[64,512]{1,0:T(8,128)S(1)} collective-permute-done((f32[64,512]{1,0:T(8,128)S(1)}, f32[64,512]{1,0:T(8,128)S(1)}, u32[]{:S(2)}, u32[]{:S(2)}) %collective-permute-start.12) | collective-permute-done | bytes 131104 | tf_op jit(solution)/shard_map/ppermute | solution.py:155
  88.4 0.8 shard_map.55
  (29 shorter events, 3.7 us)
Async XLA Ops:
  0.0 0.9 %copy-start.1 = (f32[512,128]{1,0:T(8,128)S(1)}, f32[512,128]{1,0:T(8,128)}, u32[]{:S(2)}) copy-start(f32[512,128]{1,0:T(8,128)} %piece_ref.1) | copy-start | bytes 786436
  1.1 8.9 %collective-permute-start.13 = (f32[64,512]{1,0:T(8,128)S(1)}, f32[64,512]{1,0:T(8,128)S(1)}, u32[]{:S(2)}, u32[]{:S(2)}) collective-permute-start(f32[64,512]{1,0:T(8,128)S(1)} %get-tuple-element.54.refs_0_), channel_id=1, source_target_pairs={{0,1},{1,0},{2,3},{3,2},{4,5},{5,4},{6,7},{7,6},{8,9},{9,8},{10,11... | collective-permute-start | bytes 393224 | tf_op jit(solution)/shard_map/ppermute | solution.py:155
  4.1 10.7 %collective-permute-start = (f32[64,512]{1,0:T(8,128)S(1)}, f32[64,512]{1,0:T(8,128)S(1)}, u32[]{:S(2)}, u32[]{:S(2)}) collective-permute-start(f32[64,512]{1,0:T(8,128)S(1)} %get-tuple-element.37.refs_0_), channel_id=1, source_target_pairs={{0,1},{1,0},{2,3},{3,2},{4,5},{5,4},{6,7},{7,6},{8,9},{9,8},{10,11... | collective-permute-start | bytes 393224 | tf_op jit(solution)/shard_map/ppermute | solution.py:155
  4.2 1.9 %copy-start = (f32[1,1,48,128,128]{4,3,2,1,0:T(8,128)S(1)}, f32[1,1,48,128,128]{4,3,2,1,0:T(8,128)}, u32[]{:S(2)}) copy-start(f32[1,1,48,128,128]{4,3,2,1,0:T(8,128)} %param.4) | copy-start | bytes 9437188
  6.1 0.7 copy-start.2
  10.8 8.7 %collective-permute-start.14 = (f32[64,1024]{1,0:T(8,128)S(1)}, f32[64,1024]{1,0:T(8,128)S(1)}, u32[]{:S(2)}, u32[]{:S(2)}) collective-permute-start(f32[64,1024]{1,0:T(8,128)S(1)} %get-tuple-element.55.refs_0_), channel_id=1, source_target_pairs={{0,30},{2,4},{4,2},{6,8},{8,6},{10,12},{12,10},{14,16},{16,14},{18... | collective-permute-start | bytes 786440 | tf_op jit(solution)/shard_map/ppermute | solution.py:166
  14.8 4.7 %collective-permute-start.15 = (f32[64,1024]{1,0:T(8,128)S(1)}, f32[64,1024]{1,0:T(8,128)S(1)}, u32[]{:S(2)}, u32[]{:S(2)}) collective-permute-start(f32[64,1024]{1,0:T(8,128)S(1)} %get-tuple-element.56.refs_2_), channel_id=1, source_target_pairs={{0,2},{2,0},{4,6},{6,4},{8,10},{10,8},{12,14},{14,12},{16,18},{18,... | collective-permute-start | bytes 786440 | tf_op jit(solution)/shard_map/ppermute | solution.py:166
  15.6 8.7 %collective-permute-start.1 = (f32[64,1024]{1,0:T(8,128)S(1)}, f32[64,1024]{1,0:T(8,128)S(1)}, u32[]{:S(2)}, u32[]{:S(2)}) collective-permute-start(f32[64,1024]{1,0:T(8,128)S(1)} %get-tuple-element.40.refs_0_), channel_id=1, source_target_pairs={{0,30},{2,4},{4,2},{6,8},{8,6},{10,12},{12,10},{14,16},{16,14},{18... | collective-permute-start | bytes 786440 | tf_op jit(solution)/shard_map/ppermute | solution.py:166
  17.0 7.3 %collective-permute-start.2 = (f32[64,1024]{1,0:T(8,128)S(1)}, f32[64,1024]{1,0:T(8,128)S(1)}, u32[]{:S(2)}, u32[]{:S(2)}) collective-permute-start(f32[64,1024]{1,0:T(8,128)S(1)} %get-tuple-element.41.refs_2_), channel_id=1, source_target_pairs={{0,2},{2,0},{4,6},{6,4},{8,10},{10,8},{12,14},{14,12},{16,18},{18,... | collective-permute-start | bytes 786440 | tf_op jit(solution)/shard_map/ppermute | solution.py:166
  20.3 7.7 %collective-permute-start.16 = (f32[64,1024]{1,0:T(8,128)S(1)}, f32[64,1024]{1,0:T(8,128)S(1)}, u32[]{:S(2)}, u32[]{:S(2)}) collective-permute-start(f32[64,1024]{1,0:T(8,128)S(1)} %shard_map.48.refs_0_), channel_id=1, source_target_pairs={{0,1},{1,0},{2,3},{3,2},{4,5},{5,4},{6,7},{7,6},{8,9},{9,8},{10,11... | collective-permute-start | bytes 786440 | tf_op jit(solution)/shard_map/ppermute | solution.py:155
  25.1 9.3 %collective-permute-start.3 = (f32[64,1024]{1,0:T(8,128)S(1)}, f32[64,1024]{1,0:T(8,128)S(1)}, u32[]{:S(2)}, u32[]{:S(2)}) collective-permute-start(f32[64,1024]{1,0:T(8,128)S(1)} %shard_map.40.refs_0_), channel_id=1, source_target_pairs={{0,1},{1,0},{2,3},{3,2},{4,5},{5,4},{6,7},{7,6},{8,9},{9,8},{10,11... | collective-permute-start | bytes 786440 | tf_op jit(solution)/shard_map/ppermute | solution.py:155
  28.9 8.8 %collective-permute-start.17 = (f32[64,1024]{1,0:T(8,128)S(1)}, f32[64,1024]{1,0:T(8,128)S(1)}, u32[]{:S(2)}, u32[]{:S(2)}) collective-permute-start(f32[64,1024]{1,0:T(8,128)S(1)} %get-tuple-element.57.refs_0_), channel_id=1, source_target_pairs={{0,30},{2,4},{4,2},{6,8},{8,6},{10,12},{12,10},{14,16},{16,14},{18... | collective-permute-start | bytes 786440 | tf_op jit(solution)/shard_map/ppermute | solution.py:166
  30.7 7.0 %collective-permute-start.18 = (f32[64,1024]{1,0:T(8,128)S(1)}, f32[64,1024]{1,0:T(8,128)S(1)}, u32[]{:S(2)}, u32[]{:S(2)}) collective-permute-start(f32[64,1024]{1,0:T(8,128)S(1)} %get-tuple-element.58.refs_2_), channel_id=1, source_target_pairs={{0,2},{2,0},{4,6},{6,4},{8,10},{10,8},{12,14},{14,12},{16,18},{18,... | collective-permute-start | bytes 786440 | tf_op jit(solution)/shard_map/ppermute | solution.py:166
  35.2 8.7 %collective-permute-start.4 = (f32[64,1024]{1,0:T(8,128)S(1)}, f32[64,1024]{1,0:T(8,128)S(1)}, u32[]{:S(2)}, u32[]{:S(2)}) collective-permute-start(f32[64,1024]{1,0:T(8,128)S(1)} %get-tuple-element.44.refs_0_), channel_id=1, source_target_pairs={{0,30},{2,4},{4,2},{6,8},{8,6},{10,12},{12,10},{14,16},{16,14},{18... | collective-permute-start | bytes 786440 | tf_op jit(solution)/shard_map/ppermute | solution.py:166
  37.7 6.2 %collective-permute-start.5 = (f32[64,1024]{1,0:T(8,128)S(1)}, f32[64,1024]{1,0:T(8,128)S(1)}, u32[]{:S(2)}, u32[]{:S(2)}) collective-permute-start(f32[64,1024]{1,0:T(8,128)S(1)} %get-tuple-element.45.refs_2_), channel_id=1, source_target_pairs={{0,2},{2,0},{4,6},{6,4},{8,10},{10,8},{12,14},{14,12},{16,18},{18,... | collective-permute-start | bytes 786440 | tf_op jit(solution)/shard_map/ppermute | solution.py:166
  38.5 8.1 %collective-permute-start.19 = (f32[64,1024]{1,0:T(8,128)S(1)}, f32[64,1024]{1,0:T(8,128)S(1)}, u32[]{:S(2)}, u32[]{:S(2)}) collective-permute-start(f32[64,1024]{1,0:T(8,128)S(1)} %shard_map.50.refs_0_), channel_id=1, source_target_pairs={{0,1},{1,0},{2,3},{3,2},{4,5},{5,4},{6,7},{7,6},{8,9},{9,8},{10,11... | collective-permute-start | bytes 786440 | tf_op jit(solution)/shard_map/ppermute | solution.py:155
  44.7 7.8 %collective-permute-start.6 = (f32[64,1024]{1,0:T(8,128)S(1)}, f32[64,1024]{1,0:T(8,128)S(1)}, u32[]{:S(2)}, u32[]{:S(2)}) collective-permute-start(f32[64,1024]{1,0:T(8,128)S(1)} %shard_map.42.refs_0_), channel_id=1, source_target_pairs={{0,1},{1,0},{2,3},{3,2},{4,5},{5,4},{6,7},{7,6},{8,9},{9,8},{10,11... | collective-permute-start | bytes 786440 | tf_op jit(solution)/shard_map/ppermute | solution.py:155
  47.4 8.7 %collective-permute-start.20 = (f32[64,1024]{1,0:T(8,128)S(1)}, f32[64,1024]{1,0:T(8,128)S(1)}, u32[]{:S(2)}, u32[]{:S(2)}) collective-permute-start(f32[64,1024]{1,0:T(8,128)S(1)} %get-tuple-element.60.refs_0_), channel_id=1, source_target_pairs={{0,30},{2,4},{4,2},{6,8},{8,6},{10,12},{12,10},{14,16},{16,14},{18... | collective-permute-start | bytes 786440 | tf_op jit(solution)/shard_map/ppermute | solution.py:166
  49.3 6.8 %collective-permute-start.21 = (f32[64,1024]{1,0:T(8,128)S(1)}, f32[64,1024]{1,0:T(8,128)S(1)}, u32[]{:S(2)}, u32[]{:S(2)}) collective-permute-start(f32[64,1024]{1,0:T(8,128)S(1)} %get-tuple-element.61.refs_2_), channel_id=1, source_target_pairs={{0,2},{2,0},{4,6},{6,4},{8,10},{10,8},{12,14},{14,12},{16,18},{18,... | collective-permute-start | bytes 786440 | tf_op jit(solution)/shard_map/ppermute | solution.py:166
  53.3 8.7 %collective-permute-start.7 = (f32[64,1024]{1,0:T(8,128)S(1)}, f32[64,1024]{1,0:T(8,128)S(1)}, u32[]{:S(2)}, u32[]{:S(2)}) collective-permute-start(f32[64,1024]{1,0:T(8,128)S(1)} %get-tuple-element.47.refs_0_), channel_id=1, source_target_pairs={{0,30},{2,4},{4,2},{6,8},{8,6},{10,12},{12,10},{14,16},{16,14},{18... | collective-permute-start | bytes 786440 | tf_op jit(solution)/shard_map/ppermute | solution.py:166
  53.8 8.2 %collective-permute-start.8 = (f32[64,1024]{1,0:T(8,128)S(1)}, f32[64,1024]{1,0:T(8,128)S(1)}, u32[]{:S(2)}, u32[]{:S(2)}) collective-permute-start(f32[64,1024]{1,0:T(8,128)S(1)} %get-tuple-element.48.refs_2_), channel_id=1, source_target_pairs={{0,2},{2,0},{4,6},{6,4},{8,10},{10,8},{12,14},{14,12},{16,18},{18,... | collective-permute-start | bytes 786440 | tf_op jit(solution)/shard_map/ppermute | solution.py:166
  56.9 8.9 %collective-permute-start.22 = (f32[64,1024]{1,0:T(8,128)S(1)}, f32[64,1024]{1,0:T(8,128)S(1)}, u32[]{:S(2)}, u32[]{:S(2)}) collective-permute-start(f32[64,1024]{1,0:T(8,128)S(1)} %shard_map.52.refs_0_), channel_id=1, source_target_pairs={{0,1},{1,0},{2,3},{3,2},{4,5},{5,4},{6,7},{7,6},{8,9},{9,8},{10,11... | collective-permute-start | bytes 786440 | tf_op jit(solution)/shard_map/ppermute | solution.py:155
  62.8 8.3 %collective-permute-start.9 = (f32[64,1024]{1,0:T(8,128)S(1)}, f32[64,1024]{1,0:T(8,128)S(1)}, u32[]{:S(2)}, u32[]{:S(2)}) collective-permute-start(f32[64,1024]{1,0:T(8,128)S(1)} %shard_map.44.refs_0_), channel_id=1, source_target_pairs={{0,1},{1,0},{2,3},{3,2},{4,5},{5,4},{6,7},{7,6},{8,9},{9,8},{10,11... | collective-permute-start | bytes 786440 | tf_op jit(solution)/shard_map/ppermute | solution.py:155
  67.2 8.7 %collective-permute-start.23 = (f32[64,1024]{1,0:T(8,128)S(1)}, f32[64,1024]{1,0:T(8,128)S(1)}, u32[]{:S(2)}, u32[]{:S(2)}) collective-permute-start(f32[64,1024]{1,0:T(8,128)S(1)} %get-tuple-element.63.refs_0_), channel_id=1, source_target_pairs={{0,30},{2,4},{4,2},{6,8},{8,6},{10,12},{12,10},{14,16},{16,14},{18... | collective-permute-start | bytes 786440 | tf_op jit(solution)/shard_map/ppermute | solution.py:166
  67.2 8.7 %collective-permute-start.24 = (f32[64,1024]{1,0:T(8,128)S(1)}, f32[64,1024]{1,0:T(8,128)S(1)}, u32[]{:S(2)}, u32[]{:S(2)}) collective-permute-start(f32[64,1024]{1,0:T(8,128)S(1)} %get-tuple-element.64.refs_2_), channel_id=1, source_target_pairs={{0,2},{2,0},{4,6},{6,4},{8,10},{10,8},{12,14},{14,12},{16,18},{18,... | collective-permute-start | bytes 786440 | tf_op jit(solution)/shard_map/ppermute | solution.py:166
  72.5 8.6 %collective-permute-start.10 = (f32[64,1024]{1,0:T(8,128)S(1)}, f32[64,1024]{1,0:T(8,128)S(1)}, u32[]{:S(2)}, u32[]{:S(2)}) collective-permute-start(f32[64,1024]{1,0:T(8,128)S(1)} %get-tuple-element.50.refs_0_), channel_id=1, source_target_pairs={{0,30},{2,4},{4,2},{6,8},{8,6},{10,12},{12,10},{14,16},{16,14},{18... | collective-permute-start | bytes 786440 | tf_op jit(solution)/shard_map/ppermute | solution.py:166
  75.9 5.2 %collective-permute-start.11 = (f32[64,1024]{1,0:T(8,128)S(1)}, f32[64,1024]{1,0:T(8,128)S(1)}, u32[]{:S(2)}, u32[]{:S(2)}) collective-permute-start(f32[64,1024]{1,0:T(8,128)S(1)} %get-tuple-element.51.refs_2_), channel_id=1, source_target_pairs={{0,2},{2,0},{4,6},{6,4},{8,10},{10,8},{12,14},{14,12},{16,18},{18,... | collective-permute-start | bytes 786440 | tf_op jit(solution)/shard_map/ppermute | solution.py:166
  77.5 7.5 %collective-permute-start.25 = (f32[64,512]{1,0:T(8,128)S(1)}, f32[64,512]{1,0:T(8,128)S(1)}, u32[]{:S(2)}, u32[]{:S(2)}) collective-permute-start(f32[64,512]{1,0:T(8,128)S(1)} %get-tuple-element.66), channel_id=1, source_target_pairs={{0,1},{1,0},{2,3},{3,2},{4,5},{5,4},{6,7},{7,6},{8,9},{9,8},{10,11... | collective-permute-start | bytes 393224 | tf_op jit(solution)/shard_map/ppermute | solution.py:155
  82.6 5.7 %collective-permute-start.12 = (f32[64,512]{1,0:T(8,128)S(1)}, f32[64,512]{1,0:T(8,128)S(1)}, u32[]{:S(2)}, u32[]{:S(2)}) collective-permute-start(f32[64,512]{1,0:T(8,128)S(1)} %get-tuple-element.53), channel_id=1, source_target_pairs={{0,1},{1,0},{2,3},{3,2},{4,5},{5,4},{6,7},{7,6},{8,9},{9,8},{10,11... | collective-permute-start | bytes 393224 | tf_op jit(solution)/shard_map/ppermute | solution.py:155

commit v3 on v2

--- a/solution.py
+++ b/solution.py
@@ -11,12 +11,13 @@
 DEGREE = 4
 GROUPS = 2
 UNROLL = 4
+CHUNKS = 4
 
 first_scale = 0.4
 later_scale = 0.8
 
 VMEM = pl.BlockSpec(memory_space=pltpu.VMEM)
-SMEM = pl.BlockSpec(memory_space=pltpu.SMEM)
+HBM = pl.BlockSpec(memory_space=pltpu.HBM)
 
 
 def halves(values):
@@ -36,18 +37,37 @@
         yield at, main[:rows] + main[rows:] + rest
 
 
-def dense_kernel(lists_ref, blocks_ref, high_ref, low_ref, high_t_ref, low_t_ref):
-    size = blocks_ref.shape[-1]
-    for ref in (high_ref, low_ref, high_t_ref, low_t_ref):
-        ref[...] = jnp.zeros_like(ref)
-
-    @pl.loop(0, blocks_ref.shape[0], unroll=UNROLL)
-    def _(k):
-        row = pl.ds(pl.multiple_of(lists_ref[0, k] * size, size), size)
-        col = pl.ds(pl.multiple_of(lists_ref[1, k] * size, size), size)
-        block = blocks_ref[k]
-        high_ref[row, col], low_ref[row, col] = halves(block)
-        high_t_ref[col, row], low_t_ref[col, row] = halves(block.T)
+def dense_kernel(lists_hbm, blocks_hbm, high_ref, low_ref, lists_ref, blocks_ref, semaphores):
+    count, size = blocks_ref.shape[0], blocks_ref.shape[-1]
+    chunk = count // math.gcd(count, CHUNKS)
+    copies = [pltpu.make_async_copy(lists_hbm.at[0, 0], lists_ref, semaphores.at[0])]
+    for at, start in enumerate(range(0, count, chunk)):
+        part = pl.ds(start, chunk)
+        copies.append(
+            pltpu.make_async_copy(
+                blocks_hbm.at[0, 0, part], blocks_ref.at[part], semaphores.at[1 + at]
+            )
+        )
+    for copy in copies:
+        copy.start()
+    high_ref[...] = jnp.zeros_like(high_ref)
+    low_ref[...] = jnp.zeros_like(low_ref)
+    copies[0].wait()
+    for at, copy in enumerate(copies[1:]):
+        copy.wait()
+
+        @pl.loop(at * chunk, (at + 1) * chunk, unroll=UNROLL)
+        def _(k):
+            row = pl.ds(pl.multiple_of(lists_ref[0, k] * size, size), size)
+            col = pl.ds(pl.multiple_of(lists_ref[1, k] * size, size), size)
+            high_ref[row, col], low_ref[row, col] = halves(blocks_ref[k])
+
+
+def transpose_kernel(high_ref, low_ref, high_t_ref, low_t_ref):
+    for start in range(0, high_ref.shape[0], 128):
+        at = slice(start, start + 128)
+        high_t_ref[at, :] = high_ref[:, at].T
+        low_t_ref[at, :] = low_ref[:, at].T
 
 
 def summed(terms):
@@ -68,8 +88,8 @@
 
 def write_products(ahead_first, total, high_ref, low_ref, first_ref, second_ref):
     for at, value in product(total, high_ref, low_ref, 256):
+        second_ref[:, at] = jnp.where(ahead_first, total[:, at], value)
         first_ref[:, at] = jnp.where(ahead_first, value, total[:, at])
-        second_ref[:, at] = jnp.where(ahead_first, total[:, at], value)
 
 
 def turn_kernel(groups, piece_ref, *outs):
@@ -80,45 +100,62 @@
 
 
 def first_kernel(n_off, n_row, *refs):
-    pieces, (high_ref, low_ref, vectors_ref, first_ref, second_ref) = refs[:n_off], refs[n_off:]
+    pieces, (high_ref, low_ref) = refs[:n_off], refs[n_off : n_off + 2]
+    vectors_ref, second_ref, first_ref = refs[-3:]
     rows = pieces[0].shape[1]
     for step, piece in enumerate(pieces):
         owner = lax.rem(lax.axis_index("off") - step + n_off, n_off)
         vectors_ref[:, pl.ds(pl.multiple_of(owner * rows, rows), rows)] = piece[...]
     write_products(
-        partner_order(n_off, n_row), vectors_ref[...], high_ref, low_ref, first_ref, second_ref
-    )
-
-
-def step_kernel(n_off, n_row, scale, *refs):
-    high_ref, low_ref, vectors_ref, first_ref, second_ref = refs[-5:]
+        partner_order(n_off, n_row),
+        vectors_ref[...],
+        high_ref,
+        low_ref,
+        first_ref,
+        second_ref,
+    )
+
+
+def step_kernel(n_off, n_row, scale, has_older, keeps, *refs):
     total = scale * summed(refs[:n_off])
-    if len(refs) > n_off + 5:
+    if has_older:
         total = total - refs[n_off][...]
-    vectors_ref[...] = total
-    write_products(partner_order(n_off, n_row), total, high_ref, low_ref, first_ref, second_ref)
+    if keeps:
+        refs[-3][...] = total
+    high_ref, low_ref = refs[n_off + has_older : n_off + has_older + 2]
+    second_ref, first_ref = refs[-2:]
+    write_products(
+        partner_order(n_off, n_row), total, high_ref, low_ref, first_ref, second_ref
+    )
 
 
 def far_kernel(n_off, n_row, *refs):
     seconds, firsts = refs[:n_off], refs[n_off : 2 * n_off]
-    high_ref, low_ref, total_ref, *outs = refs[2 * n_off :]
+    high_ref, low_ref, *outs = refs[2 * n_off :]
     offset = lax.axis_index("off")
     ahead_first = partner_order(n_off, n_row)
 
-    def chosen(own, if_ahead, if_not, at):
-        value = own[:, at]
+    def far(at):
+        value = seconds[0][:, at]
         for distance in range(1, n_off):
-            swapped = jnp.where(ahead_first, if_ahead[distance][:, at], if_not[distance][:, at])
+            swapped = jnp.where(ahead_first, firsts[distance][:, at], seconds[distance][:, at])
             value = jnp.where(offset == distance, swapped, value)
         return value
 
-    far = chosen(seconds[0], firsts, seconds, slice(None))
-    for at, value in product(far, high_ref, low_ref, 256):
-        total_ref[:, at] = value + chosen(firsts[0], seconds, firsts, at)
-    for step, out in enumerate(outs):
-        rows = out.shape[1]
+    def back(at):
+        value = firsts[0][:, at]
+        for distance in range(1, n_off):
+            swapped = jnp.where(ahead_first, seconds[distance][:, at], firsts[distance][:, at])
+            value = jnp.where(offset == distance, swapped, value)
+        return value
+
+    total_ref = outs[-1]
+    for at, value in product(far(slice(None)), high_ref, low_ref, 256):
+        total_ref[:, at] = value + back(at)
+    for step, out in enumerate(outs[:-1]):
+        rows_out = out.shape[1]
         owner = lax.rem(offset + step, n_off)
-        out[...] = total_ref[:, pl.ds(pl.multiple_of(owner * rows, rows), rows)]
+        out[...] = total_ref[:, pl.ds(pl.multiple_of(owner * rows_out, rows_out), rows_out)]
 
 
 def last_kernel(n_off, groups, *refs):
@@ -132,14 +169,14 @@
     out_ref[...] = jnp.concatenate(result, axis=0).T
 
 
-def kernel_call(body, in_specs, shapes, scratch=(), flops=0, limit=24):
+def kernel_call(body, in_specs, shapes, scratch=(), flops=0):
     return pl.pallas_call(
         body,
         out_shape=shapes,
         in_specs=in_specs,
         out_specs=[VMEM] * len(shapes),
         scratch_shapes=list(scratch),
-        compiler_params=pltpu.CompilerParams(vmem_limit_bytes=limit * 2**20),
+        compiler_params=pltpu.CompilerParams(vmem_limit_bytes=24 * 2**20),
         cost_estimate=pl.CostEstimate(flops=flops, bytes_accessed=0, transcendentals=0),
     )
 
@@ -176,38 +213,52 @@
         vectors
     )
     pieces = [[piece] + [shifted(piece, s) for s in range(1, n_off)] for piece in pieces]
-    high, low, high_t, low_t = kernel_call(
-        dense_kernel, [SMEM, VMEM], [bf16] * 4, flops=flops
-    )(lists[0, 0], blocks[0, 0])
+    count = blocks.shape[2]
+    high, low = kernel_call(
+        dense_kernel,
+        [HBM, HBM],
+        [bf16] * 2,
+        [
+            pltpu.SMEM(lists.shape[2:], lists.dtype),
+            pltpu.VMEM(blocks.shape[2:], blocks.dtype),
+            pltpu.SemaphoreType.DMA((1 + math.gcd(count, CHUNKS),)),
+        ],
+    )(*(pltpu.with_memory_space_constraint(x, pltpu.HBM) for x in (lists, blocks)))
+    high_t, low_t = kernel_call(transpose_kernel, [VMEM] * 2, [bf16] * 2, flops=flops)(high, low)
 
     older, newer = [None] * GROUPS, [None] * GROUPS
     totals = [None] * GROUPS
     for degree in range(DEGREE):
         scale = first_scale if degree == 1 else later_scale
-        firsts, seconds = [None] * GROUPS, [None] * GROUPS
+        last = degree == DEGREE - 1
+        seconds = []
+        firsts = []
         for g in range(GROUPS):
             if degree == 0:
                 body = functools.partial(first_kernel, n_off, n_row)
                 terms = pieces[g]
             else:
-                body = functools.partial(step_kernel, n_off, n_row, scale)
+                body = functools.partial(
+                    step_kernel, n_off, n_row, scale, int(degree > 1), not last
+                )
                 terms = [totals[g]] + [shifted(totals[g], s) for s in range(1, n_off)]
                 terms += [older[g]] if degree > 1 else []
-            older[g] = newer[g]
-            newer[g], first, second = kernel_call(
-                body, [VMEM] * (len(terms) + 2), [group_shape] * 3, flops=flops
+            kept = [] if last else [group_shape]
+            *kept, second, first = kernel_call(
+                body, [VMEM] * (len(terms) + 2), kept + [group_shape] * 2, flops=flops
             )(*terms, high, low)
-            seconds[g] = swapped(second, 0)
-            firsts[g] = swapped(first, 1)
+            older[g], newer[g] = newer[g], kept[0] if kept else None
+            seconds.append(swapped(second, 0))
+            firsts.append(swapped(first, 1))
         for g in range(GROUPS):
-            pieces_out = n_off if degree == DEGREE - 1 else 0
             outs = kernel_call(
                 functools.partial(far_kernel, n_off, n_row),
                 [VMEM] * (2 * n_off + 2),
-                [group_shape] + [piece_shape] * pieces_out,
+                [piece_shape] * n_off if last else [group_shape],
+                [pltpu.VMEM(group_shape.shape, jnp.float32)] if last else [],
                 flops=flops,
             )(*seconds[g], *firsts[g], high_t, low_t)
-            totals[g] = outs[1:] if pieces_out else outs[0]
+            totals[g] = outs if last else outs[0]
     terms = []
     for g in range(GROUPS):
         terms.append(totals[g][0])

time: 89.7 us -> 85.9 us (0.958)
  Pallas kernels: 19.9 us -> 17.1 us
  local copies, waits for them, and re-layouts: 3.52 us -> 0.95 us
  starting transfers between devices: 43.1 us -> 44.8 us
    ppermute x16, starting transfers between devices: 23.4 us -> 27.5 us  [swapped(): values.append(lax.ppermute(value, 'row', route))]
    ppermute x16, waiting for transfers between devices: 12.5 us -> 9.32 us  [swapped(): values.append(lax.ppermute(value, 'row', route))]
    ppermute x10, waiting for transfers between devices: 10.1 us -> 13 us  [shifted(): lax.ppermute(value, 'off', [(d, (d + distance) % n_off) for d in range(n_...]
    unnamed x6 -> x2, local copies, waits for them, and re-layouts: 3.52 us -> 0.95 us
    ppermute x10, starting transfers between devices: 19.6 us -> 17.4 us  [shifted(): lax.ppermute(value, 'off', [(d, (d + distance) % n_off) for d in range(n_...]
    pallas_call x8, Pallas kernels: 8.05 us -> 6.51 us  [per_device(): kernel_call(functools.partial(far_kernel, n_off, n_row), [VMEM] * (2 * n_...]
    pallas_call x9 -> x10, Pallas kernels: 10.9 us -> 9.59 us  [the longest x8 6.35 us: per_device(): kernel_call(body, [VMEM] * (len(terms) + 2), kept + [group_shape] * 2, fl...]
  transfers between devices with their start and end apart: 26 -> 26, of which waited for: 13 -> 13; matrix products, arithmetic and copies ran while one was open for 0% -> 0% of each run, Pallas kernels for 21% -> 19%
where the time goes in v3:
time: 85.9 us; the launch traced here: 85.3 us
  starting transfers between devices  44.8 us (52%)
  waiting for transfers between devices  22.3 us (26%)
  Pallas kernels  17.1 us (20%)
  local copies, waits for them, and re-layouts  0.95 us (1%)
    ppermute x16, starting transfers between devices, swapped(): values.append(lax.ppermute(value, 'row', route))  27.5 us
    ppermute x10, starting transfers between devices, shifted(): lax.ppermute(value, 'off', [(d, (d + distance) % n_off) for d in range(n_...  17.4 us
    ppermute x10, waiting for transfers between devices, shifted(): lax.ppermute(value, 'off', [(d, (d + distance) % n_off) for d in range(n_...  13 us
    ppermute x16, waiting for transfers between devices, swapped(): values.append(lax.ppermute(value, 'row', route))  9.32 us
    pallas_call x8, Pallas kernels, per_device(): kernel_call(functools.partial(far_kernel, n_off, n_row), [VMEM] * (2 * n_...  6.51 us
    pallas_call x8, Pallas kernels, per_device(): kernel_call(body, [VMEM] * (len(terms) + 2), kept + [group_shape] * 2, fl...  6.35 us
    pallas_call x1, Pallas kernels, per_device(): kernel_call(dense_kernel, [HBM, HBM], [bf16] * 2, [pltpu.SMEM(lists.shape...  2.1 us
  transfers between devices with their start and end apart: 26, of which 13 were waited for; matrix products, arithmetic and copies ran while one was open for 0% of the time, Pallas kernels for 19%

profile of v3, /device:TPU:0, one launch (start us, length us, event | category | flops | bytes accessed | tf_op | source)
XLA Modules:
  0.0 85.3 jit_solution(11348456633276382765)
XLA Ops:
  0.0 0.9 %copy-done = f32[512,128]{1,0:T(8,128)S(1)} copy-done((f32[512,128]{1,0:T(8,128)S(1)}, f32[512,128]{1,0:T(8,128)}, u32[]{:S(2)}) %copy-start) | copy-done | bytes 262168
  1.1 3.0 %collective-permute-start.13 = (f32[64,512]{1,0:T(8,128)S(1)}, f32[64,512]{1,0:T(8,128)S(1)}, u32[]{:S(2)}, u32[]{:S(2)}) collective-permute-start(f32[64,512]{1,0:T(8,128)S(1)} %get-tuple-element.54.refs_0_), channel_id=1, source_target_pairs={{0,1},{1,0},{2,3},{3,2},{4,5},{5,4},{6,7},{7,6},{8,9},{9,8},{10,11... | collective-permute-start | bytes 393224 | tf_op jit(solution)/shard_map/ppermute | solution.py:192
  4.2 2.1 %shard_map.38 = (bf16[1024,1024]{1,0:T(8,128)(2,1)S(1)}, bf16[1024,1024]{1,0:T(8,128)(2,1)S(1)}) custom-call(s32[1,1,2,48]{3,2,1,0:T(2,128)} %lists_hbm.1, f32[1,1,48,128,128]{4,3,2,1,0:T(8,128)} %blocks_hbm.1), custom_call_target="tpu_custom_call" | custom-call | tf_op jit(solution)/shard_map/pallas_call | solution.py:217
  6.3 2.1 %collective-permute-done.13.refs_1_ = f32[64,512]{1,0:T(8,128)S(1)} collective-permute-done((f32[64,512]{1,0:T(8,128)S(1)}, f32[64,512]{1,0:T(8,128)S(1)}, u32[]{:S(2)}, u32[]{:S(2)}) %collective-permute-start.13) | collective-permute-done | bytes 131104 | tf_op jit(solution)/shard_map/ppermute | solution.py:192
  8.4 0.8 shard_map.48
  9.2 2.6 %collective-permute-start.14 = (f32[64,1024]{1,0:T(8,128)S(1)}, f32[64,1024]{1,0:T(8,128)S(1)}, u32[]{:S(2)}, u32[]{:S(2)}) collective-permute-start(f32[64,1024]{1,0:T(8,128)S(1)} %get-tuple-element.55.refs_0_), channel_id=1, source_target_pairs={{0,30},{2,4},{4,2},{6,8},{8,6},{10,12},{12,10},{14,16},{16,14},{18... | collective-permute-start | bytes 786440 | tf_op jit(solution)/shard_map/ppermute | solution.py:203
  12.6 2.8 %collective-permute-start.1 = (f32[64,1024]{1,0:T(8,128)S(1)}, f32[64,1024]{1,0:T(8,128)S(1)}, u32[]{:S(2)}, u32[]{:S(2)}) collective-permute-start(f32[64,1024]{1,0:T(8,128)S(1)} %get-tuple-element.40.refs_0_), channel_id=1, source_target_pairs={{0,30},{2,4},{4,2},{6,8},{8,6},{10,12},{12,10},{14,16},{16,14},{18... | collective-permute-start | bytes 786440 | tf_op jit(solution)/shard_map/ppermute | solution.py:203
  15.5 1.1 %shard_map.40 = (bf16[1024,1024]{1,0:T(8,128)(2,1)S(1)}, bf16[1024,1024]{1,0:T(8,128)(2,1)S(1)}) custom-call(bf16[1024,1024]{1,0:T(8,128)(2,1)S(1)} %get-tuple-element.38.refs_2_.high_ref.refs_3_, bf16[1024,1024]{1,0:T(8,128)(2,1)S(1)} %get-tuple-element.39.refs_3_.low_ref.refs_4_), custom_call_target="tpu_custom_call" | custom-call | flops 402653184 | tf_op jit(solution)/shard_map/pallas_call | solution.py:227
  16.6 1.3 %collective-permute-done.14.refs_1_ = f32[64,1024]{1,0:T(8,128)S(1)} collective-permute-done((f32[64,1024]{1,0:T(8,128)S(1)}, f32[64,1024]{1,0:T(8,128)S(1)}, u32[]{:S(2)}, u32[]{:S(2)}) %collective-permute-start.14) | collective-permute-done | bytes 262176 | tf_op jit(solution)/shard_map/ppermute | solution.py:203
  17.9 0.8 shard_map.49.refs_0_
  18.7 2.1 %collective-permute-start.16 = (f32[64,1024]{1,0:T(8,128)S(1)}, f32[64,1024]{1,0:T(8,128)S(1)}, u32[]{:S(2)}, u32[]{:S(2)}) collective-permute-start(f32[64,1024]{1,0:T(8,128)S(1)} %shard_map.49.refs_0_), channel_id=1, source_target_pairs={{0,1},{1,0},{2,3},{3,2},{4,5},{5,4},{6,7},{7,6},{8,9},{9,8},{10,11... | collective-permute-start | bytes 786440 | tf_op jit(solution)/shard_map/ppermute | solution.py:192
  21.3 0.8 shard_map.41.refs_0_
  22.1 1.5 %collective-permute-start.3 = (f32[64,1024]{1,0:T(8,128)S(1)}, f32[64,1024]{1,0:T(8,128)S(1)}, u32[]{:S(2)}, u32[]{:S(2)}) collective-permute-start(f32[64,1024]{1,0:T(8,128)S(1)} %shard_map.41.refs_0_), channel_id=1, source_target_pairs={{0,1},{1,0},{2,3},{3,2},{4,5},{5,4},{6,7},{7,6},{8,9},{9,8},{10,11... | collective-permute-start | bytes 786440 | tf_op jit(solution)/shard_map/ppermute | solution.py:192
  23.6 1.9 %collective-permute-done.16.refs_1_ = f32[64,1024]{1,0:T(8,128)S(1)} collective-permute-done((f32[64,1024]{1,0:T(8,128)S(1)}, f32[64,1024]{1,0:T(8,128)S(1)}, u32[]{:S(2)}, u32[]{:S(2)}) %collective-permute-start.16) | collective-permute-done | bytes 262176 | tf_op jit(solution)/shard_map/ppermute | solution.py:192
  26.3 1.4 %collective-permute-start.17 = (f32[64,1024]{1,0:T(8,128)S(1)}, f32[64,1024]{1,0:T(8,128)S(1)}, u32[]{:S(2)}, u32[]{:S(2)}) collective-permute-start(f32[64,1024]{1,0:T(8,128)S(1)} %get-tuple-element.57.refs_0_), channel_id=1, source_target_pairs={{0,30},{2,4},{4,2},{6,8},{8,6},{10,12},{12,10},{14,16},{16,14},{18... | collective-permute-start | bytes 786440 | tf_op jit(solution)/shard_map/ppermute | solution.py:203
  27.7 3.6 %collective-permute-start.18 = (f32[64,1024]{1,0:T(8,128)S(1)}, f32[64,1024]{1,0:T(8,128)S(1)}, u32[]{:S(2)}, u32[]{:S(2)}) collective-permute-start(f32[64,1024]{1,0:T(8,128)S(1)} %get-tuple-element.58.refs_2_), channel_id=1, source_target_pairs={{0,2},{2,0},{4,6},{6,4},{8,10},{10,8},{12,14},{14,12},{16,18},{18,... | collective-permute-start | bytes 786440 | tf_op jit(solution)/shard_map/ppermute | solution.py:203
  31.4 0.8 shard_map.42
  32.2 4.0 %collective-permute-start.4 = (f32[64,1024]{1,0:T(8,128)S(1)}, f32[64,1024]{1,0:T(8,128)S(1)}, u32[]{:S(2)}, u32[]{:S(2)}) collective-permute-start(f32[64,1024]{1,0:T(8,128)S(1)} %get-tuple-element.44.refs_0_), channel_id=1, source_target_pairs={{0,30},{2,4},{4,2},{6,8},{8,6},{10,12},{12,10},{14,16},{16,14},{18... | collective-permute-start | bytes 786440 | tf_op jit(solution)/shard_map/ppermute | solution.py:203
  36.2 0.8 shard_map.51.refs_0_
  37.0 1.6 %collective-permute-start.19 = (f32[64,1024]{1,0:T(8,128)S(1)}, f32[64,1024]{1,0:T(8,128)S(1)}, u32[]{:S(2)}, u32[]{:S(2)}) collective-permute-start(f32[64,1024]{1,0:T(8,128)S(1)} %shard_map.51.refs_0_), channel_id=1, source_target_pairs={{0,1},{1,0},{2,3},{3,2},{4,5},{5,4},{6,7},{7,6},{8,9},{9,8},{10,11... | collective-permute-start | bytes 786440 | tf_op jit(solution)/shard_map/ppermute | solution.py:192
  38.5 2.3 %collective-permute-done.4.refs_1_ = f32[64,1024]{1,0:T(8,128)S(1)} collective-permute-done((f32[64,1024]{1,0:T(8,128)S(1)}, f32[64,1024]{1,0:T(8,128)S(1)}, u32[]{:S(2)}, u32[]{:S(2)}) %collective-permute-start.4) | collective-permute-done | bytes 262176 | tf_op jit(solution)/shard_map/ppermute | solution.py:203
  40.8 0.8 shard_map.43.refs_0_
  41.6 2.3 %collective-permute-start.6 = (f32[64,1024]{1,0:T(8,128)S(1)}, f32[64,1024]{1,0:T(8,128)S(1)}, u32[]{:S(2)}, u32[]{:S(2)}) collective-permute-start(f32[64,1024]{1,0:T(8,128)S(1)} %shard_map.43.refs_0_), channel_id=1, source_target_pairs={{0,1},{1,0},{2,3},{3,2},{4,5},{5,4},{6,7},{7,6},{8,9},{9,8},{10,11... | collective-permute-start | bytes 786440 | tf_op jit(solution)/shard_map/ppermute | solution.py:192
  44.7 0.8 shard_map.52
  45.5 2.2 %collective-permute-start.20 = (f32[64,1024]{1,0:T(8,128)S(1)}, f32[64,1024]{1,0:T(8,128)S(1)}, u32[]{:S(2)}, u32[]{:S(2)}) collective-permute-start(f32[64,1024]{1,0:T(8,128)S(1)} %get-tuple-element.60.refs_0_), channel_id=1, source_target_pairs={{0,30},{2,4},{4,2},{6,8},{8,6},{10,12},{12,10},{14,16},{16,14},{18... | collective-permute-start | bytes 786440 | tf_op jit(solution)/shard_map/ppermute | solution.py:203
  47.7 0.9 %collective-permute-start.21 = (f32[64,1024]{1,0:T(8,128)S(1)}, f32[64,1024]{1,0:T(8,128)S(1)}, u32[]{:S(2)}, u32[]{:S(2)}) collective-permute-start(f32[64,1024]{1,0:T(8,128)S(1)} %get-tuple-element.61.refs_2_), channel_id=1, source_target_pairs={{0,2},{2,0},{4,6},{6,4},{8,10},{10,8},{12,14},{14,12},{16,18},{18,... | collective-permute-start | bytes 786440 | tf_op jit(solution)/shard_map/ppermute | solution.py:203
  48.6 1.8 %collective-permute-done.6.refs_1_ = f32[64,1024]{1,0:T(8,128)S(1)} collective-permute-done((f32[64,1024]{1,0:T(8,128)S(1)}, f32[64,1024]{1,0:T(8,128)S(1)}, u32[]{:S(2)}, u32[]{:S(2)}) %collective-permute-start.6) | collective-permute-done | bytes 262176 | tf_op jit(solution)/shard_map/ppermute | solution.py:192
  50.4 0.8 shard_map.44
  51.2 3.3 %collective-permute-start.7 = (f32[64,1024]{1,0:T(8,128)S(1)}, f32[64,1024]{1,0:T(8,128)S(1)}, u32[]{:S(2)}, u32[]{:S(2)}) collective-permute-start(f32[64,1024]{1,0:T(8,128)S(1)} %get-tuple-element.47.refs_0_), channel_id=1, source_target_pairs={{0,30},{2,4},{4,2},{6,8},{8,6},{10,12},{12,10},{14,16},{16,14},{18... | collective-permute-start | bytes 786440 | tf_op jit(solution)/shard_map/ppermute | solution.py:203
  54.5 0.8 shard_map.53.refs_0_
  55.3 1.6 %collective-permute-start.22 = (f32[64,1024]{1,0:T(8,128)S(1)}, f32[64,1024]{1,0:T(8,128)S(1)}, u32[]{:S(2)}, u32[]{:S(2)}) collective-permute-start(f32[64,1024]{1,0:T(8,128)S(1)} %shard_map.53.refs_0_), channel_id=1, source_target_pairs={{0,1},{1,0},{2,3},{3,2},{4,5},{5,4},{6,7},{7,6},{8,9},{9,8},{10,11... | collective-permute-start | bytes 786440 | tf_op jit(solution)/shard_map/ppermute | solution.py:192
  56.8 3.0 %collective-permute-done.7.refs_1_ = f32[64,1024]{1,0:T(8,128)S(1)} collective-permute-done((f32[64,1024]{1,0:T(8,128)S(1)}, f32[64,1024]{1,0:T(8,128)S(1)}, u32[]{:S(2)}, u32[]{:S(2)}) %collective-permute-start.7) | collective-permute-done | bytes 262176 | tf_op jit(solution)/shard_map/ppermute | solution.py:203
  59.8 0.8 shard_map.45.refs_0_
  60.6 1.3 %collective-permute-start.9 = (f32[64,1024]{1,0:T(8,128)S(1)}, f32[64,1024]{1,0:T(8,128)S(1)}, u32[]{:S(2)}, u32[]{:S(2)}) collective-permute-start(f32[64,1024]{1,0:T(8,128)S(1)} %shard_map.45.refs_0_), channel_id=1, source_target_pairs={{0,1},{1,0},{2,3},{3,2},{4,5},{5,4},{6,7},{7,6},{8,9},{9,8},{10,11... | collective-permute-start | bytes 786440 | tf_op jit(solution)/shard_map/ppermute | solution.py:192
  61.9 1.5 %collective-permute-done.22.refs_1_ = f32[64,1024]{1,0:T(8,128)S(1)} collective-permute-done((f32[64,1024]{1,0:T(8,128)S(1)}, f32[64,1024]{1,0:T(8,128)S(1)}, u32[]{:S(2)}, u32[]{:S(2)}) %collective-permute-start.22) | collective-permute-done | bytes 262176 | tf_op jit(solution)/shard_map/ppermute | solution.py:192
  63.5 0.8 shard_map.54
  64.3 1.7 %collective-permute-start.23 = (f32[64,1024]{1,0:T(8,128)S(1)}, f32[64,1024]{1,0:T(8,128)S(1)}, u32[]{:S(2)}, u32[]{:S(2)}) collective-permute-start(f32[64,1024]{1,0:T(8,128)S(1)} %get-tuple-element.63.refs_0_), channel_id=1, source_target_pairs={{0,30},{2,4},{4,2},{6,8},{8,6},{10,12},{12,10},{14,16},{16,14},{18... | collective-permute-start | bytes 786440 | tf_op jit(solution)/shard_map/ppermute | solution.py:203
  66.0 1.3 %collective-permute-start.24 = (f32[64,1024]{1,0:T(8,128)S(1)}, f32[64,1024]{1,0:T(8,128)S(1)}, u32[]{:S(2)}, u32[]{:S(2)}) collective-permute-start(f32[64,1024]{1,0:T(8,128)S(1)} %get-tuple-element.64.refs_2_), channel_id=1, source_target_pairs={{0,2},{2,0},{4,6},{6,4},{8,10},{10,8},{12,14},{14,12},{16,18},{18,... | collective-permute-start | bytes 786440 | tf_op jit(solution)/shard_map/ppermute | solution.py:203
  67.3 1.4 %collective-permute-done.9.refs_1_ = f32[64,1024]{1,0:T(8,128)S(1)} collective-permute-done((f32[64,1024]{1,0:T(8,128)S(1)}, f32[64,1024]{1,0:T(8,128)S(1)}, u32[]{:S(2)}, u32[]{:S(2)}) %collective-permute-start.9) | collective-permute-done | bytes 262176 | tf_op jit(solution)/shard_map/ppermute | solution.py:192
  68.7 0.8 shard_map.46
  69.5 3.8 %collective-permute-start.10 = (f32[64,1024]{1,0:T(8,128)S(1)}, f32[64,1024]{1,0:T(8,128)S(1)}, u32[]{:S(2)}, u32[]{:S(2)}) collective-permute-start(f32[64,1024]{1,0:T(8,128)S(1)} %get-tuple-element.50.refs_0_), channel_id=1, source_target_pairs={{0,30},{2,4},{4,2},{6,8},{8,6},{10,12},{12,10},{14,16},{16,14},{18... | collective-permute-start | bytes 786440 | tf_op jit(solution)/shard_map/ppermute | solution.py:203
  73.3 0.8 shard_map.55
  74.2 1.8 %collective-permute-start.25 = (f32[64,512]{1,0:T(8,128)S(1)}, f32[64,512]{1,0:T(8,128)S(1)}, u32[]{:S(2)}, u32[]{:S(2)}) collective-permute-start(f32[64,512]{1,0:T(8,128)S(1)} %get-tuple-element.66), channel_id=1, source_target_pairs={{0,1},{1,0},{2,3},{3,2},{4,5},{5,4},{6,7},{7,6},{8,9},{9,8},{10,11... | collective-permute-start | bytes 393224 | tf_op jit(solution)/shard_map/ppermute | solution.py:192
  76.0 2.3 %collective-permute-done.10.refs_1_ = f32[64,1024]{1,0:T(8,128)S(1)} collective-permute-done((f32[64,1024]{1,0:T(8,128)S(1)}, f32[64,1024]{1,0:T(8,128)S(1)}, u32[]{:S(2)}, u32[]{:S(2)}) %collective-permute-start.10) | collective-permute-done | bytes 262176 | tf_op jit(solution)/shard_map/ppermute | solution.py:203
  78.2 0.8 shard_map.47
  79.1 2.1 %collective-permute-start.12 = (f32[64,512]{1,0:T(8,128)S(1)}, f32[64,512]{1,0:T(8,128)S(1)}, u32[]{:S(2)}, u32[]{:S(2)}) collective-permute-start(f32[64,512]{1,0:T(8,128)S(1)} %get-tuple-element.53), channel_id=1, source_target_pairs={{0,1},{1,0},{2,3},{3,2},{4,5},{5,4},{6,7},{7,6},{8,9},{9,8},{10,11... | collective-permute-start | bytes 393224 | tf_op jit(solution)/shard_map/ppermute | solution.py:192
  81.2 3.3 %collective-permute-done.12.refs_1_ = f32[64,512]{1,0:T(8,128)S(1)} collective-permute-done((f32[64,512]{1,0:T(8,128)S(1)}, f32[64,512]{1,0:T(8,128)S(1)}, u32[]{:S(2)}, u32[]{:S(2)}) %collective-permute-start.12) | collective-permute-done | bytes 131104 | tf_op jit(solution)/shard_map/ppermute | solution.py:192
  84.5 0.8 shard_map.56
  (26 shorter events, 3.2 us)
Async XLA Ops:
  0.0 0.9 %copy-start = (f32[512,128]{1,0:T(8,128)S(1)}, f32[512,128]{1,0:T(8,128)}, u32[]{:S(2)}) copy-start(f32[512,128]{1,0:T(8,128)} %piece_ref.1) | copy-start | bytes 786436
  1.1 7.3 %collective-permute-start.13 = (f32[64,512]{1,0:T(8,128)S(1)}, f32[64,512]{1,0:T(8,128)S(1)}, u32[]{:S(2)}, u32[]{:S(2)}) collective-permute-start(f32[64,512]{1,0:T(8,128)S(1)} %get-tuple-element.54.refs_0_), channel_id=1, source_target_pairs={{0,1},{1,0},{2,3},{3,2},{4,5},{5,4},{6,7},{7,6},{8,9},{9,8},{10,11... | collective-permute-start | bytes 393224 | tf_op jit(solution)/shard_map/ppermute | solution.py:192
  4.1 7.7 %collective-permute-start = (f32[64,512]{1,0:T(8,128)S(1)}, f32[64,512]{1,0:T(8,128)S(1)}, u32[]{:S(2)}, u32[]{:S(2)}) collective-permute-start(f32[64,512]{1,0:T(8,128)S(1)} %get-tuple-element.37.refs_0_), channel_id=1, source_target_pairs={{0,1},{1,0},{2,3},{3,2},{4,5},{5,4},{6,7},{7,6},{8,9},{9,8},{10,11... | collective-permute-start | bytes 393224 | tf_op jit(solution)/shard_map/ppermute | solution.py:192
  9.2 8.7 %collective-permute-start.14 = (f32[64,1024]{1,0:T(8,128)S(1)}, f32[64,1024]{1,0:T(8,128)S(1)}, u32[]{:S(2)}, u32[]{:S(2)}) collective-permute-start(f32[64,1024]{1,0:T(8,128)S(1)} %get-tuple-element.55.refs_0_), channel_id=1, source_target_pairs={{0,30},{2,4},{4,2},{6,8},{8,6},{10,12},{12,10},{14,16},{16,14},{18... | collective-permute-start | bytes 786440 | tf_op jit(solution)/shard_map/ppermute | solution.py:203
  11.8 6.1 %collective-permute-start.15 = (f32[64,1024]{1,0:T(8,128)S(1)}, f32[64,1024]{1,0:T(8,128)S(1)}, u32[]{:S(2)}, u32[]{:S(2)}) collective-permute-start(f32[64,1024]{1,0:T(8,128)S(1)} %get-tuple-element.56.refs_2_), channel_id=1, source_target_pairs={{0,2},{2,0},{4,6},{6,4},{8,10},{10,8},{12,14},{14,12},{16,18},{18,... | collective-permute-start | bytes 786440 | tf_op jit(solution)/shard_map/ppermute | solution.py:203
  12.6 8.7 %collective-permute-start.1 = (f32[64,1024]{1,0:T(8,128)S(1)}, f32[64,1024]{1,0:T(8,128)S(1)}, u32[]{:S(2)}, u32[]{:S(2)}) collective-permute-start(f32[64,1024]{1,0:T(8,128)S(1)} %get-tuple-element.40.refs_0_), channel_id=1, source_target_pairs={{0,30},{2,4},{4,2},{6,8},{8,6},{10,12},{12,10},{14,16},{16,14},{18... | collective-permute-start | bytes 786440 | tf_op jit(solution)/shard_map/ppermute | solution.py:203
  15.5 5.8 %collective-permute-start.2 = (f32[64,1024]{1,0:T(8,128)S(1)}, f32[64,1024]{1,0:T(8,128)S(1)}, u32[]{:S(2)}, u32[]{:S(2)}) collective-permute-start(f32[64,1024]{1,0:T(8,128)S(1)} %get-tuple-element.41.refs_2_), channel_id=1, source_target_pairs={{0,2},{2,0},{4,6},{6,4},{8,10},{10,8},{12,14},{14,12},{16,18},{18,... | collective-permute-start | bytes 786440 | tf_op jit(solution)/shard_map/ppermute | solution.py:203
  18.7 6.8 %collective-permute-start.16 = (f32[64,1024]{1,0:T(8,128)S(1)}, f32[64,1024]{1,0:T(8,128)S(1)}, u32[]{:S(2)}, u32[]{:S(2)}) collective-permute-start(f32[64,1024]{1,0:T(8,128)S(1)} %shard_map.49.refs_0_), channel_id=1, source_target_pairs={{0,1},{1,0},{2,3},{3,2},{4,5},{5,4},{6,7},{7,6},{8,9},{9,8},{10,11... | collective-permute-start | bytes 786440 | tf_op jit(solution)/shard_map/ppermute | solution.py:192
  22.1 9.2 %collective-permute-start.3 = (f32[64,1024]{1,0:T(8,128)S(1)}, f32[64,1024]{1,0:T(8,128)S(1)}, u32[]{:S(2)}, u32[]{:S(2)}) collective-permute-start(f32[64,1024]{1,0:T(8,128)S(1)} %shard_map.41.refs_0_), channel_id=1, source_target_pairs={{0,1},{1,0},{2,3},{3,2},{4,5},{5,4},{6,7},{7,6},{8,9},{9,8},{10,11... | collective-permute-start | bytes 786440 | tf_op jit(solution)/shard_map/ppermute | solution.py:192
  26.3 9.8 %collective-permute-start.17 = (f32[64,1024]{1,0:T(8,128)S(1)}, f32[64,1024]{1,0:T(8,128)S(1)}, u32[]{:S(2)}, u32[]{:S(2)}) collective-permute-start(f32[64,1024]{1,0:T(8,128)S(1)} %get-tuple-element.57.refs_0_), channel_id=1, source_target_pairs={{0,30},{2,4},{4,2},{6,8},{8,6},{10,12},{12,10},{14,16},{16,14},{18... | collective-permute-start | bytes 786440 | tf_op jit(solution)/shard_map/ppermute | solution.py:203
  27.7 8.5 %collective-permute-start.18 = (f32[64,1024]{1,0:T(8,128)S(1)}, f32[64,1024]{1,0:T(8,128)S(1)}, u32[]{:S(2)}, u32[]{:S(2)}) collective-permute-start(f32[64,1024]{1,0:T(8,128)S(1)} %get-tuple-element.58.refs_2_), channel_id=1, source_target_pairs={{0,2},{2,0},{4,6},{6,4},{8,10},{10,8},{12,14},{14,12},{16,18},{18,... | collective-permute-start | bytes 786440 | tf_op jit(solution)/shard_map/ppermute | solution.py:203
  32.2 8.7 %collective-permute-start.4 = (f32[64,1024]{1,0:T(8,128)S(1)}, f32[64,1024]{1,0:T(8,128)S(1)}, u32[]{:S(2)}, u32[]{:S(2)}) collective-permute-start(f32[64,1024]{1,0:T(8,128)S(1)} %get-tuple-element.44.refs_0_), channel_id=1, source_target_pairs={{0,30},{2,4},{4,2},{6,8},{8,6},{10,12},{12,10},{14,16},{16,14},{18... | collective-permute-start | bytes 786440 | tf_op jit(solution)/shard_map/ppermute | solution.py:203
  36.2 4.7 %collective-permute-start.5 = (f32[64,1024]{1,0:T(8,128)S(1)}, f32[64,1024]{1,0:T(8,128)S(1)}, u32[]{:S(2)}, u32[]{:S(2)}) collective-permute-start(f32[64,1024]{1,0:T(8,128)S(1)} %get-tuple-element.45.refs_2_), channel_id=1, source_target_pairs={{0,2},{2,0},{4,6},{6,4},{8,10},{10,8},{12,14},{14,12},{16,18},{18,... | collective-permute-start | bytes 786440 | tf_op jit(solution)/shard_map/ppermute | solution.py:203
  37.0 7.8 %collective-permute-start.19 = (f32[64,1024]{1,0:T(8,128)S(1)}, f32[64,1024]{1,0:T(8,128)S(1)}, u32[]{:S(2)}, u32[]{:S(2)}) collective-permute-start(f32[64,1024]{1,0:T(8,128)S(1)} %shard_map.51.refs_0_), channel_id=1, source_target_pairs={{0,1},{1,0},{2,3},{3,2},{4,5},{5,4},{6,7},{7,6},{8,9},{9,8},{10,11... | collective-permute-start | bytes 786440 | tf_op jit(solution)/shard_map/ppermute | solution.py:192
  41.6 8.7 %collective-permute-start.6 = (f32[64,1024]{1,0:T(8,128)S(1)}, f32[64,1024]{1,0:T(8,128)S(1)}, u32[]{:S(2)}, u32[]{:S(2)}) collective-permute-start(f32[64,1024]{1,0:T(8,128)S(1)} %shard_map.43.refs_0_), channel_id=1, source_target_pairs={{0,1},{1,0},{2,3},{3,2},{4,5},{5,4},{6,7},{7,6},{8,9},{9,8},{10,11... | collective-permute-start | bytes 786440 | tf_op jit(solution)/shard_map/ppermute | solution.py:192
  45.5 8.9 %collective-permute-start.20 = (f32[64,1024]{1,0:T(8,128)S(1)}, f32[64,1024]{1,0:T(8,128)S(1)}, u32[]{:S(2)}, u32[]{:S(2)}) collective-permute-start(f32[64,1024]{1,0:T(8,128)S(1)} %get-tuple-element.60.refs_0_), channel_id=1, source_target_pairs={{0,30},{2,4},{4,2},{6,8},{8,6},{10,12},{12,10},{14,16},{16,14},{18... | collective-permute-start | bytes 786440 | tf_op jit(solution)/shard_map/ppermute | solution.py:203
  47.7 6.7 %collective-permute-start.21 = (f32[64,1024]{1,0:T(8,128)S(1)}, f32[64,1024]{1,0:T(8,128)S(1)}, u32[]{:S(2)}, u32[]{:S(2)}) collective-permute-start(f32[64,1024]{1,0:T(8,128)S(1)} %get-tuple-element.61.refs_2_), channel_id=1, source_target_pairs={{0,2},{2,0},{4,6},{6,4},{8,10},{10,8},{12,14},{14,12},{16,18},{18,... | collective-permute-start | bytes 786440 | tf_op jit(solution)/shard_map/ppermute | solution.py:203
  51.2 8.7 %collective-permute-start.7 = (f32[64,1024]{1,0:T(8,128)S(1)}, f32[64,1024]{1,0:T(8,128)S(1)}, u32[]{:S(2)}, u32[]{:S(2)}) collective-permute-start(f32[64,1024]{1,0:T(8,128)S(1)} %get-tuple-element.47.refs_0_), channel_id=1, source_target_pairs={{0,30},{2,4},{4,2},{6,8},{8,6},{10,12},{12,10},{14,16},{16,14},{18... | collective-permute-start | bytes 786440 | tf_op jit(solution)/shard_map/ppermute | solution.py:203
  54.4 5.4 %collective-permute-start.8 = (f32[64,1024]{1,0:T(8,128)S(1)}, f32[64,1024]{1,0:T(8,128)S(1)}, u32[]{:S(2)}, u32[]{:S(2)}) collective-permute-start(f32[64,1024]{1,0:T(8,128)S(1)} %get-tuple-element.48.refs_2_), channel_id=1, source_target_pairs={{0,2},{2,0},{4,6},{6,4},{8,10},{10,8},{12,14},{14,12},{16,18},{18,... | collective-permute-start | bytes 786440 | tf_op jit(solution)/shard_map/ppermute | solution.py:203
  55.3 8.2 %collective-permute-start.22 = (f32[64,1024]{1,0:T(8,128)S(1)}, f32[64,1024]{1,0:T(8,128)S(1)}, u32[]{:S(2)}, u32[]{:S(2)}) collective-permute-start(f32[64,1024]{1,0:T(8,128)S(1)} %shard_map.53.refs_0_), channel_id=1, source_target_pairs={{0,1},{1,0},{2,3},{3,2},{4,5},{5,4},{6,7},{7,6},{8,9},{9,8},{10,11... | collective-permute-start | bytes 786440 | tf_op jit(solution)/shard_map/ppermute | solution.py:192
  60.6 8.1 %collective-permute-start.9 = (f32[64,1024]{1,0:T(8,128)S(1)}, f32[64,1024]{1,0:T(8,128)S(1)}, u32[]{:S(2)}, u32[]{:S(2)}) collective-permute-start(f32[64,1024]{1,0:T(8,128)S(1)} %shard_map.45.refs_0_), channel_id=1, source_target_pairs={{0,1},{1,0},{2,3},{3,2},{4,5},{5,4},{6,7},{7,6},{8,9},{9,8},{10,11... | collective-permute-start | bytes 786440 | tf_op jit(solution)/shard_map/ppermute | solution.py:192
  64.3 9.0 %collective-permute-start.23 = (f32[64,1024]{1,0:T(8,128)S(1)}, f32[64,1024]{1,0:T(8,128)S(1)}, u32[]{:S(2)}, u32[]{:S(2)}) collective-permute-start(f32[64,1024]{1,0:T(8,128)S(1)} %get-tuple-element.63.refs_0_), channel_id=1, source_target_pairs={{0,30},{2,4},{4,2},{6,8},{8,6},{10,12},{12,10},{14,16},{16,14},{18... | collective-permute-start | bytes 786440 | tf_op jit(solution)/shard_map/ppermute | solution.py:203
  66.0 7.3 %collective-permute-start.24 = (f32[64,1024]{1,0:T(8,128)S(1)}, f32[64,1024]{1,0:T(8,128)S(1)}, u32[]{:S(2)}, u32[]{:S(2)}) collective-permute-start(f32[64,1024]{1,0:T(8,128)S(1)} %get-tuple-element.64.refs_2_), channel_id=1, source_target_pairs={{0,2},{2,0},{4,6},{6,4},{8,10},{10,8},{12,14},{14,12},{16,18},{18,... | collective-permute-start | bytes 786440 | tf_op jit(solution)/shard_map/ppermute | solution.py:203
  69.5 8.7 %collective-permute-start.10 = (f32[64,1024]{1,0:T(8,128)S(1)}, f32[64,1024]{1,0:T(8,128)S(1)}, u32[]{:S(2)}, u32[]{:S(2)}) collective-permute-start(f32[64,1024]{1,0:T(8,128)S(1)} %get-tuple-element.50.refs_0_), channel_id=1, source_target_pairs={{0,30},{2,4},{4,2},{6,8},{8,6},{10,12},{12,10},{14,16},{16,14},{18... | collective-permute-start | bytes 786440 | tf_op jit(solution)/shard_map/ppermute | solution.py:203
  73.3 4.9 %collective-permute-start.11 = (f32[64,1024]{1,0:T(8,128)S(1)}, f32[64,1024]{1,0:T(8,128)S(1)}, u32[]{:S(2)}, u32[]{:S(2)}) collective-permute-start(f32[64,1024]{1,0:T(8,128)S(1)} %get-tuple-element.51.refs_2_), channel_id=1, source_target_pairs={{0,2},{2,0},{4,6},{6,4},{8,10},{10,8},{12,14},{14,12},{16,18},{18,... | collective-permute-start | bytes 786440 | tf_op jit(solution)/shard_map/ppermute | solution.py:203
  74.2 7.0 %collective-permute-start.25 = (f32[64,512]{1,0:T(8,128)S(1)}, f32[64,512]{1,0:T(8,128)S(1)}, u32[]{:S(2)}, u32[]{:S(2)}) collective-permute-start(f32[64,512]{1,0:T(8,128)S(1)} %get-tuple-element.66), channel_id=1, source_target_pairs={{0,1},{1,0},{2,3},{3,2},{4,5},{5,4},{6,7},{7,6},{8,9},{9,8},{10,11... | collective-permute-start | bytes 393224 | tf_op jit(solution)/shard_map/ppermute | solution.py:192
  79.1 5.4 %collective-permute-start.12 = (f32[64,512]{1,0:T(8,128)S(1)}, f32[64,512]{1,0:T(8,128)S(1)}, u32[]{:S(2)}, u32[]{:S(2)}) collective-permute-start(f32[64,512]{1,0:T(8,128)S(1)} %get-tuple-element.53), channel_id=1, source_target_pairs={{0,1},{1,0},{2,3},{3,2},{4,5},{5,4},{6,7},{7,6},{8,9},{9,8},{10,11... | collective-permute-start | bytes 393224 | tf_op jit(solution)/shard_map/ppermute | solution.py:192

commit v4 on v3

--- a/solution.py
+++ b/solution.py
@@ -130,32 +130,22 @@
 
 
 def far_kernel(n_off, n_row, *refs):
-    seconds, firsts = refs[:n_off], refs[n_off : 2 * n_off]
-    high_ref, low_ref, *outs = refs[2 * n_off :]
+    own_second, second, own_first, first, high_ref, low_ref, *outs = refs
     offset = lax.axis_index("off")
     ahead_first = partner_order(n_off, n_row)
 
-    def far(at):
-        value = seconds[0][:, at]
-        for distance in range(1, n_off):
-            swapped = jnp.where(ahead_first, firsts[distance][:, at], seconds[distance][:, at])
-            value = jnp.where(offset == distance, swapped, value)
-        return value
-
-    def back(at):
-        value = firsts[0][:, at]
-        for distance in range(1, n_off):
-            swapped = jnp.where(ahead_first, seconds[distance][:, at], firsts[distance][:, at])
-            value = jnp.where(offset == distance, swapped, value)
-        return value
+    def received(own, if_ahead, if_not, at):
+        value = jnp.where(ahead_first, if_ahead[:, at], if_not[:, at])
+        return jnp.where(offset == 0, own[:, at], value)
 
     total_ref = outs[-1]
-    for at, value in product(far(slice(None)), high_ref, low_ref, 256):
-        total_ref[:, at] = value + back(at)
+    far = received(own_second, first, second, slice(None))
+    for at, value in product(far, high_ref, low_ref, 256):
+        total_ref[:, at] = value + received(own_first, second, first, at)
     for step, out in enumerate(outs[:-1]):
-        rows_out = out.shape[1]
+        rows = out.shape[1]
         owner = lax.rem(offset + step, n_off)
-        out[...] = total_ref[:, pl.ds(pl.multiple_of(owner * rows_out, rows_out), rows_out)]
+        out[...] = total_ref[:, pl.ds(pl.multiple_of(owner * rows, rows), rows)]
 
 
 def last_kernel(n_off, groups, *refs):
@@ -192,16 +182,15 @@
         return lax.ppermute(value, "off", [(d, (d + distance) % n_off) for d in range(n_off)])
 
     def swapped(value, ahead):
-        values = [value]
-        for distance in range(1, n_off):
-            step = math.gcd(distance, n_row)
-            assert n_row // step % 2 == 0
-            route = [
-                (i, (i + (distance if (i // step + ahead) % 2 else -distance)) % n_row)
-                for i in range(n_row)
-            ]
-            values.append(lax.ppermute(value, "row", route))
-        return values
+        route = []
+        for i in range(n_row):
+            for d in range(n_off):
+                step = math.gcd(d, n_row) if d else 1
+                assert n_row // step % 2 == 0
+                forward = i // step % 2 == (1 - ahead if d else 0)
+                partner = (i + (d or 1) * (1 if forward else -1)) % n_row
+                route.append((i * n_off + d, partner * n_off + d))
+        return [value, lax.ppermute(value, ("row", "off"), route)]
 
     f32 = lambda *shape: jax.ShapeDtypeStruct(shape, jnp.float32)
     bf16 = jax.ShapeDtypeStruct((tile_rows, tile_rows), jnp.bfloat16)
@@ -253,7 +242,7 @@
         for g in range(GROUPS):
             outs = kernel_call(
                 functools.partial(far_kernel, n_off, n_row),
-                [VMEM] * (2 * n_off + 2),
+                [VMEM] * 6,
                 [piece_shape] * n_off if last else [group_shape],
                 [pltpu.VMEM(group_shape.shape, jnp.float32)] if last else [],
                 flops=flops,

time: 85.9 us -> 85.9 us (level)
  starting transfers between devices: 44.8 us -> 52.7 us
  waiting for transfers between devices: 22.3 us -> 14.4 us
    ppermute x10, starting transfers between devices: 17.4 us -> 37.4 us  [shifted(): lax.ppermute(value, 'off', [(d, (d + distance) % n_off) for d in range(n_...]
    ppermute x16, starting transfers between devices: 27.5 us -> 15.3 us  [swapped(): return [value, lax.ppermute(value, ('row', 'off'), route)]]
    ppermute x16, waiting for transfers between devices: 9.32 us -> 0.04 us  [swapped(): return [value, lax.ppermute(value, ('row', 'off'), route)]]
    ppermute x10, waiting for transfers between devices: 13 us -> 14.3 us  [shifted(): lax.ppermute(value, 'off', [(d, (d + distance) % n_off) for d in range(n_...]
  transfers between devices with their start and end apart: 26 -> 26, of which waited for: 13 -> 8; matrix products, arithmetic and copies ran while one was open for 0% -> 0% of each run, Pallas kernels for 19% -> 19%
where the time goes in v4:
time: 85.9 us; the launch traced here: 85.4 us
  starting transfers between devices  52.7 us (61%)
  Pallas kernels  17.1 us (20%)
  waiting for transfers between devices  14.4 us (17%)
  local copies, waits for them, and re-layouts  0.95 us (1%)
    ppermute x10, starting transfers between devices, shifted(): lax.ppermute(value, 'off', [(d, (d + distance) % n_off) for d in range(n_...  37.4 us
    ppermute x16, starting transfers between devices, swapped(): return [value, lax.ppermute(value, ('row', 'off'), route)]  15.3 us
    ppermute x10, waiting for transfers between devices, shifted(): lax.ppermute(value, 'off', [(d, (d + distance) % n_off) for d in range(n_...  14.3 us
    pallas_call x8, Pallas kernels, per_device(): kernel_call(functools.partial(far_kernel, n_off, n_row), [VMEM] * 6, [pie...  6.53 us
    pallas_call x8, Pallas kernels, per_device(): kernel_call(body, [VMEM] * (len(terms) + 2), kept + [group_shape] * 2, fl...  6.36 us
    pallas_call x1, Pallas kernels, per_device(): kernel_call(dense_kernel, [HBM, HBM], [bf16] * 2, [pltpu.SMEM(lists.shape...  2.1 us
  transfers between devices with their start and end apart: 26, of which 8 were waited for; matrix products, arithmetic and copies ran while one was open for 0% of the time, Pallas kernels for 19%

profile of v4, /device:TPU:0, one launch (start us, length us, event | category | flops | bytes accessed | tf_op | source)
XLA Modules:
  0.0 85.4 jit_solution(1290159198510828781)
XLA Ops:
  0.0 0.9 %copy-done = f32[512,128]{1,0:T(8,128)S(1)} copy-done((f32[512,128]{1,0:T(8,128)S(1)}, f32[512,128]{1,0:T(8,128)}, u32[]{:S(2)}) %copy-start) | copy-done | bytes 262168
  1.0 0.1 shard_map.37
  1.1 3.0 %collective-permute-start.13 = (f32[64,512]{1,0:T(8,128)S(1)}, f32[64,512]{1,0:T(8,128)S(1)}, u32[]{:S(2)}, u32[]{:S(2)}) collective-permute-start(f32[64,512]{1,0:T(8,128)S(1)} %get-tuple-element.54.refs_0_), channel_id=1, source_target_pairs={{0,1},{1,0},{2,3},{3,2},{4,5},{5,4},{6,7},{7,6},{8,9},{9,8},{10,11... | collective-permute-start | bytes 393224 | tf_op jit(solution)/shard_map/ppermute | solution.py:182
  4.1 0.1 collective-permute-start
  4.2 2.1 %shard_map.38 = (bf16[1024,1024]{1,0:T(8,128)(2,1)S(1)}, bf16[1024,1024]{1,0:T(8,128)(2,1)S(1)}) custom-call(s32[1,1,2,48]{3,2,1,0:T(2,128)} %lists_hbm.1, f32[1,1,48,128,128]{4,3,2,1,0:T(8,128)} %blocks_hbm.1), custom_call_target="tpu_custom_call" | custom-call | tf_op jit(solution)/shard_map/pallas_call | solution.py:206
  6.3 2.1 %collective-permute-done.13.refs_1_ = f32[64,512]{1,0:T(8,128)S(1)} collective-permute-done((f32[64,512]{1,0:T(8,128)S(1)}, f32[64,512]{1,0:T(8,128)S(1)}, u32[]{:S(2)}, u32[]{:S(2)}) %collective-permute-start.13) | collective-permute-done | bytes 131104 | tf_op jit(solution)/shard_map/ppermute | solution.py:182
  8.4 0.8 shard_map.48
  9.3 0.5 collective-permute-start.15
  9.8 0.6 collective-permute-done.refs_1_
  10.4 0.8 shard_map.39
  11.3 0.5 collective-permute-start.2
  11.8 1.1 %shard_map.40 = (bf16[1024,1024]{1,0:T(8,128)(2,1)S(1)}, bf16[1024,1024]{1,0:T(8,128)(2,1)S(1)}) custom-call(bf16[1024,1024]{1,0:T(8,128)(2,1)S(1)} %get-tuple-element.38.refs_2_.high_ref.refs_3_, bf16[1024,1024]{1,0:T(8,128)(2,1)S(1)} %get-tuple-element.39.refs_3_.low_ref.refs_4_), custom_call_target="tpu_custom_call" | custom-call | flops 402653184 | tf_op jit(solution)/shard_map/pallas_call | solution.py:216
  12.9 0.8 shard_map.49.refs_0_
  13.8 7.0 %collective-permute-start.16 = (f32[64,1024]{1,0:T(8,128)S(1)}, f32[64,1024]{1,0:T(8,128)S(1)}, u32[]{:S(2)}, u32[]{:S(2)}) collective-permute-start(f32[64,1024]{1,0:T(8,128)S(1)} %shard_map.49.refs_0_), channel_id=1, source_target_pairs={{0,1},{1,0},{2,3},{3,2},{4,5},{5,4},{6,7},{7,6},{8,9},{9,8},{10,11... | collective-permute-start | bytes 786440 | tf_op jit(solution)/shard_map/ppermute | solution.py:182
  20.8 0.8 shard_map.41.refs_0_
  21.6 2.0 %collective-permute-start.3 = (f32[64,1024]{1,0:T(8,128)S(1)}, f32[64,1024]{1,0:T(8,128)S(1)}, u32[]{:S(2)}, u32[]{:S(2)}) collective-permute-start(f32[64,1024]{1,0:T(8,128)S(1)} %shard_map.41.refs_0_), channel_id=1, source_target_pairs={{0,1},{1,0},{2,3},{3,2},{4,5},{5,4},{6,7},{7,6},{8,9},{9,8},{10,11... | collective-permute-start | bytes 786440 | tf_op jit(solution)/shard_map/ppermute | solution.py:182
  23.6 2.1 %collective-permute-done.16.refs_1_ = f32[64,1024]{1,0:T(8,128)S(1)} collective-permute-done((f32[64,1024]{1,0:T(8,128)S(1)}, f32[64,1024]{1,0:T(8,128)S(1)}, u32[]{:S(2)}, u32[]{:S(2)}) %collective-permute-start.16) | collective-permute-done | bytes 262176 | tf_op jit(solution)/shard_map/ppermute | solution.py:182
  25.7 0.8 shard_map.50
  26.5 4.7 %collective-permute-start.17 = (f32[64,1024]{1,0:T(8,128)S(1)}, f32[64,1024]{1,0:T(8,128)S(1)}, u32[]{:S(2)}, u32[]{:S(2)}) collective-permute-start(f32[64,1024]{1,0:T(8,128)S(1)} %get-tuple-element.57.refs_0_), channel_id=1, source_target_pairs={{0,2},{1,31},{2,0},{3,5},{4,6},{5,3},{6,4},{7,9},{8,10},{9,7},{10,... | collective-permute-start | bytes 786440 | tf_op jit(solution)/shard_map/ppermute | solution.py:193
  31.2 0.1 collective-permute-start.18
  31.3 0.8 shard_map.42
  32.1 2.1 %collective-permute-start.4 = (f32[64,1024]{1,0:T(8,128)S(1)}, f32[64,1024]{1,0:T(8,128)S(1)}, u32[]{:S(2)}, u32[]{:S(2)}) collective-permute-start(f32[64,1024]{1,0:T(8,128)S(1)} %get-tuple-element.44.refs_0_), channel_id=1, source_target_pairs={{0,2},{1,31},{2,0},{3,5},{4,6},{5,3},{6,4},{7,9},{8,10},{9,7},{10,... | collective-permute-start | bytes 786440 | tf_op jit(solution)/shard_map/ppermute | solution.py:193
  34.3 0.1 collective-permute-start.5
  34.4 0.8 shard_map.51.refs_0_
  35.2 3.4 %collective-permute-start.19 = (f32[64,1024]{1,0:T(8,128)S(1)}, f32[64,1024]{1,0:T(8,128)S(1)}, u32[]{:S(2)}, u32[]{:S(2)}) collective-permute-start(f32[64,1024]{1,0:T(8,128)S(1)} %shard_map.51.refs_0_), channel_id=1, source_target_pairs={{0,1},{1,0},{2,3},{3,2},{4,5},{5,4},{6,7},{7,6},{8,9},{9,8},{10,11... | collective-permute-start | bytes 786440 | tf_op jit(solution)/shard_map/ppermute | solution.py:182
  38.5 0.8 shard_map.43.refs_0_
  39.4 4.6 %collective-permute-start.6 = (f32[64,1024]{1,0:T(8,128)S(1)}, f32[64,1024]{1,0:T(8,128)S(1)}, u32[]{:S(2)}, u32[]{:S(2)}) collective-permute-start(f32[64,1024]{1,0:T(8,128)S(1)} %shard_map.43.refs_0_), channel_id=1, source_target_pairs={{0,1},{1,0},{2,3},{3,2},{4,5},{5,4},{6,7},{7,6},{8,9},{9,8},{10,11... | collective-permute-start | bytes 786440 | tf_op jit(solution)/shard_map/ppermute | solution.py:182
  44.0 0.8 shard_map.52
  44.8 2.6 %collective-permute-start.20 = (f32[64,1024]{1,0:T(8,128)S(1)}, f32[64,1024]{1,0:T(8,128)S(1)}, u32[]{:S(2)}, u32[]{:S(2)}) collective-permute-start(f32[64,1024]{1,0:T(8,128)S(1)} %get-tuple-element.60.refs_0_), channel_id=1, source_target_pairs={{0,2},{1,31},{2,0},{3,5},{4,6},{5,3},{6,4},{7,9},{8,10},{9,7},{10,... | collective-permute-start | bytes 786440 | tf_op jit(solution)/shard_map/ppermute | solution.py:193
  47.5 1.8 %collective-permute-done.6.refs_1_ = f32[64,1024]{1,0:T(8,128)S(1)} collective-permute-done((f32[64,1024]{1,0:T(8,128)S(1)}, f32[64,1024]{1,0:T(8,128)S(1)}, u32[]{:S(2)}, u32[]{:S(2)}) %collective-permute-start.6) | collective-permute-done | bytes 262176 | tf_op jit(solution)/shard_map/ppermute | solution.py:182
  49.3 0.8 shard_map.44
  50.1 1.9 %collective-permute-start.7 = (f32[64,1024]{1,0:T(8,128)S(1)}, f32[64,1024]{1,0:T(8,128)S(1)}, u32[]{:S(2)}, u32[]{:S(2)}) collective-permute-start(f32[64,1024]{1,0:T(8,128)S(1)} %get-tuple-element.47.refs_0_), channel_id=1, source_target_pairs={{0,2},{1,31},{2,0},{3,5},{4,6},{5,3},{6,4},{7,9},{8,10},{9,7},{10,... | collective-permute-start | bytes 786440 | tf_op jit(solution)/shard_map/ppermute | solution.py:193
  52.1 0.8 shard_map.53.refs_0_
  52.9 3.9 %collective-permute-start.22 = (f32[64,1024]{1,0:T(8,128)S(1)}, f32[64,1024]{1,0:T(8,128)S(1)}, u32[]{:S(2)}, u32[]{:S(2)}) collective-permute-start(f32[64,1024]{1,0:T(8,128)S(1)} %shard_map.53.refs_0_), channel_id=1, source_target_pairs={{0,1},{1,0},{2,3},{3,2},{4,5},{5,4},{6,7},{7,6},{8,9},{9,8},{10,11... | collective-permute-start | bytes 786440 | tf_op jit(solution)/shard_map/ppermute | solution.py:182
  56.8 0.8 shard_map.45.refs_0_
  57.7 4.3 %collective-permute-start.9 = (f32[64,1024]{1,0:T(8,128)S(1)}, f32[64,1024]{1,0:T(8,128)S(1)}, u32[]{:S(2)}, u32[]{:S(2)}) collective-permute-start(f32[64,1024]{1,0:T(8,128)S(1)} %shard_map.45.refs_0_), channel_id=1, source_target_pairs={{0,1},{1,0},{2,3},{3,2},{4,5},{5,4},{6,7},{7,6},{8,9},{9,8},{10,11... | collective-permute-start | bytes 786440 | tf_op jit(solution)/shard_map/ppermute | solution.py:182
  61.9 1.3 %collective-permute-done.22.refs_1_ = f32[64,1024]{1,0:T(8,128)S(1)} collective-permute-done((f32[64,1024]{1,0:T(8,128)S(1)}, f32[64,1024]{1,0:T(8,128)S(1)}, u32[]{:S(2)}, u32[]{:S(2)}) %collective-permute-start.22) | collective-permute-done | bytes 262176 | tf_op jit(solution)/shard_map/ppermute | solution.py:182
  63.2 0.8 shard_map.54
  64.1 1.4 %collective-permute-start.23 = (f32[64,1024]{1,0:T(8,128)S(1)}, f32[64,1024]{1,0:T(8,128)S(1)}, u32[]{:S(2)}, u32[]{:S(2)}) collective-permute-start(f32[64,1024]{1,0:T(8,128)S(1)} %get-tuple-element.63.refs_0_), channel_id=1, source_target_pairs={{0,2},{1,31},{2,0},{3,5},{4,6},{5,3},{6,4},{7,9},{8,10},{9,7},{10,... | collective-permute-start | bytes 786440 | tf_op jit(solution)/shard_map/ppermute | solution.py:193
  65.5 3.0 %collective-permute-done.9.refs_1_ = f32[64,1024]{1,0:T(8,128)S(1)} collective-permute-done((f32[64,1024]{1,0:T(8,128)S(1)}, f32[64,1024]{1,0:T(8,128)S(1)}, u32[]{:S(2)}, u32[]{:S(2)}) %collective-permute-start.9) | collective-permute-done | bytes 262176 | tf_op jit(solution)/shard_map/ppermute | solution.py:182
  68.5 0.8 shard_map.46
  69.3 1.0 %collective-permute-start.10 = (f32[64,1024]{1,0:T(8,128)S(1)}, f32[64,1024]{1,0:T(8,128)S(1)}, u32[]{:S(2)}, u32[]{:S(2)}) collective-permute-start(f32[64,1024]{1,0:T(8,128)S(1)} %get-tuple-element.50.refs_0_), channel_id=1, source_target_pairs={{0,2},{1,31},{2,0},{3,5},{4,6},{5,3},{6,4},{7,9},{8,10},{9,7},{10,... | collective-permute-start | bytes 786440 | tf_op jit(solution)/shard_map/ppermute | solution.py:193
  70.4 0.8 shard_map.55
  71.2 4.7 %collective-permute-start.25 = (f32[64,512]{1,0:T(8,128)S(1)}, f32[64,512]{1,0:T(8,128)S(1)}, u32[]{:S(2)}, u32[]{:S(2)}) collective-permute-start(f32[64,512]{1,0:T(8,128)S(1)} %get-tuple-element.66), channel_id=1, source_target_pairs={{0,1},{1,0},{2,3},{3,2},{4,5},{5,4},{6,7},{7,6},{8,9},{9,8},{10,11... | collective-permute-start | bytes 393224 | tf_op jit(solution)/shard_map/ppermute | solution.py:182
  76.0 0.8 shard_map.47
  76.8 4.3 %collective-permute-start.12 = (f32[64,512]{1,0:T(8,128)S(1)}, f32[64,512]{1,0:T(8,128)S(1)}, u32[]{:S(2)}, u32[]{:S(2)}) collective-permute-start(f32[64,512]{1,0:T(8,128)S(1)} %get-tuple-element.53), channel_id=1, source_target_pairs={{0,1},{1,0},{2,3},{3,2},{4,5},{5,4},{6,7},{7,6},{8,9},{9,8},{10,11... | collective-permute-start | bytes 393224 | tf_op jit(solution)/shard_map/ppermute | solution.py:182
  81.2 3.3 %collective-permute-done.12.refs_1_ = f32[64,512]{1,0:T(8,128)S(1)} collective-permute-done((f32[64,512]{1,0:T(8,128)S(1)}, f32[64,512]{1,0:T(8,128)S(1)}, u32[]{:S(2)}, u32[]{:S(2)}) %collective-permute-start.12) | collective-permute-done | bytes 131104 | tf_op jit(solution)/shard_map/ppermute | solution.py:182
  84.5 0.8 shard_map.56
  (26 shorter events, 0.6 us)
Async XLA Ops:
  0.0 0.9 %copy-start = (f32[512,128]{1,0:T(8,128)S(1)}, f32[512,128]{1,0:T(8,128)}, u32[]{:S(2)}) copy-start(f32[512,128]{1,0:T(8,128)} %piece_ref.1) | copy-start | bytes 786436
  1.1 7.3 %collective-permute-start.13 = (f32[64,512]{1,0:T(8,128)S(1)}, f32[64,512]{1,0:T(8,128)S(1)}, u32[]{:S(2)}, u32[]{:S(2)}) collective-permute-start(f32[64,512]{1,0:T(8,128)S(1)} %get-tuple-element.54.refs_0_), channel_id=1, source_target_pairs={{0,1},{1,0},{2,3},{3,2},{4,5},{5,4},{6,7},{7,6},{8,9},{9,8},{10,11... | collective-permute-start | bytes 393224 | tf_op jit(solution)/shard_map/ppermute | solution.py:182
  4.1 6.3 %collective-permute-start = (f32[64,512]{1,0:T(8,128)S(1)}, f32[64,512]{1,0:T(8,128)S(1)}, u32[]{:S(2)}, u32[]{:S(2)}) collective-permute-start(f32[64,512]{1,0:T(8,128)S(1)} %get-tuple-element.37.refs_0_), channel_id=1, source_target_pairs={{0,1},{1,0},{2,3},{3,2},{4,5},{5,4},{6,7},{7,6},{8,9},{9,8},{10,11... | collective-permute-start | bytes 393224 | tf_op jit(solution)/shard_map/ppermute | solution.py:182
  9.2 3.7 %collective-permute-start.14 = (f32[64,1024]{1,0:T(8,128)S(1)}, f32[64,1024]{1,0:T(8,128)S(1)}, u32[]{:S(2)}, u32[]{:S(2)}) collective-permute-start(f32[64,1024]{1,0:T(8,128)S(1)} %get-tuple-element.55.refs_0_), channel_id=1, source_target_pairs={{0,2},{1,31},{2,0},{3,5},{4,6},{5,3},{6,4},{7,9},{8,10},{9,7},{10,... | collective-permute-start | bytes 786440 | tf_op jit(solution)/shard_map/ppermute | solution.py:193
  9.3 3.6 %collective-permute-start.15 = (f32[64,1024]{1,0:T(8,128)S(1)}, f32[64,1024]{1,0:T(8,128)S(1)}, u32[]{:S(2)}, u32[]{:S(2)}) collective-permute-start(f32[64,1024]{1,0:T(8,128)S(1)} %get-tuple-element.56.refs_2_), channel_id=1, source_target_pairs={{0,2},{1,3},{2,0},{3,1},{4,6},{5,7},{6,4},{7,5},{8,10},{9,11},{10,... | collective-permute-start | bytes 786440 | tf_op jit(solution)/shard_map/ppermute | solution.py:193
  11.2 9.6 %collective-permute-start.1 = (f32[64,1024]{1,0:T(8,128)S(1)}, f32[64,1024]{1,0:T(8,128)S(1)}, u32[]{:S(2)}, u32[]{:S(2)}) collective-permute-start(f32[64,1024]{1,0:T(8,128)S(1)} %get-tuple-element.40.refs_0_), channel_id=1, source_target_pairs={{0,2},{1,31},{2,0},{3,5},{4,6},{5,3},{6,4},{7,9},{8,10},{9,7},{10,... | collective-permute-start | bytes 786440 | tf_op jit(solution)/shard_map/ppermute | solution.py:193
  11.3 9.5 %collective-permute-start.2 = (f32[64,1024]{1,0:T(8,128)S(1)}, f32[64,1024]{1,0:T(8,128)S(1)}, u32[]{:S(2)}, u32[]{:S(2)}) collective-permute-start(f32[64,1024]{1,0:T(8,128)S(1)} %get-tuple-element.41.refs_2_), channel_id=1, source_target_pairs={{0,2},{1,3},{2,0},{3,1},{4,6},{5,7},{6,4},{7,5},{8,10},{9,11},{10,... | collective-permute-start | bytes 786440 | tf_op jit(solution)/shard_map/ppermute | solution.py:193
  13.8 12.0 %collective-permute-start.16 = (f32[64,1024]{1,0:T(8,128)S(1)}, f32[64,1024]{1,0:T(8,128)S(1)}, u32[]{:S(2)}, u32[]{:S(2)}) collective-permute-start(f32[64,1024]{1,0:T(8,128)S(1)} %shard_map.49.refs_0_), channel_id=1, source_target_pairs={{0,1},{1,0},{2,3},{3,2},{4,5},{5,4},{6,7},{7,6},{8,9},{9,8},{10,11... | collective-permute-start | bytes 786440 | tf_op jit(solution)/shard_map/ppermute | solution.py:182
  21.6 9.7 %collective-permute-start.3 = (f32[64,1024]{1,0:T(8,128)S(1)}, f32[64,1024]{1,0:T(8,128)S(1)}, u32[]{:S(2)}, u32[]{:S(2)}) collective-permute-start(f32[64,1024]{1,0:T(8,128)S(1)} %shard_map.41.refs_0_), channel_id=1, source_target_pairs={{0,1},{1,0},{2,3},{3,2},{4,5},{5,4},{6,7},{7,6},{8,9},{9,8},{10,11... | collective-permute-start | bytes 786440 | tf_op jit(solution)/shard_map/ppermute | solution.py:182
  26.5 7.8 %collective-permute-start.17 = (f32[64,1024]{1,0:T(8,128)S(1)}, f32[64,1024]{1,0:T(8,128)S(1)}, u32[]{:S(2)}, u32[]{:S(2)}) collective-permute-start(f32[64,1024]{1,0:T(8,128)S(1)} %get-tuple-element.57.refs_0_), channel_id=1, source_target_pairs={{0,2},{1,31},{2,0},{3,5},{4,6},{5,3},{6,4},{7,9},{8,10},{9,7},{10,... | collective-permute-start | bytes 786440 | tf_op jit(solution)/shard_map/ppermute | solution.py:193
  31.2 3.2 %collective-permute-start.18 = (f32[64,1024]{1,0:T(8,128)S(1)}, f32[64,1024]{1,0:T(8,128)S(1)}, u32[]{:S(2)}, u32[]{:S(2)}) collective-permute-start(f32[64,1024]{1,0:T(8,128)S(1)} %get-tuple-element.58.refs_2_), channel_id=1, source_target_pairs={{0,2},{1,3},{2,0},{3,1},{4,6},{5,7},{6,4},{7,5},{8,10},{9,11},{10,... | collective-permute-start | bytes 786440 | tf_op jit(solution)/shard_map/ppermute | solution.py:193
  32.1 6.4 %collective-permute-start.4 = (f32[64,1024]{1,0:T(8,128)S(1)}, f32[64,1024]{1,0:T(8,128)S(1)}, u32[]{:S(2)}, u32[]{:S(2)}) collective-permute-start(f32[64,1024]{1,0:T(8,128)S(1)} %get-tuple-element.44.refs_0_), channel_id=1, source_target_pairs={{0,2},{1,31},{2,0},{3,5},{4,6},{5,3},{6,4},{7,9},{8,10},{9,7},{10,... | collective-permute-start | bytes 786440 | tf_op jit(solution)/shard_map/ppermute | solution.py:193
  34.3 4.3 %collective-permute-start.5 = (f32[64,1024]{1,0:T(8,128)S(1)}, f32[64,1024]{1,0:T(8,128)S(1)}, u32[]{:S(2)}, u32[]{:S(2)}) collective-permute-start(f32[64,1024]{1,0:T(8,128)S(1)} %get-tuple-element.45.refs_2_), channel_id=1, source_target_pairs={{0,2},{1,3},{2,0},{3,1},{4,6},{5,7},{6,4},{7,5},{8,10},{9,11},{10,... | collective-permute-start | bytes 786440 | tf_op jit(solution)/shard_map/ppermute | solution.py:193
  35.2 8.8 %collective-permute-start.19 = (f32[64,1024]{1,0:T(8,128)S(1)}, f32[64,1024]{1,0:T(8,128)S(1)}, u32[]{:S(2)}, u32[]{:S(2)}) collective-permute-start(f32[64,1024]{1,0:T(8,128)S(1)} %shard_map.51.refs_0_), channel_id=1, source_target_pairs={{0,1},{1,0},{2,3},{3,2},{4,5},{5,4},{6,7},{7,6},{8,9},{9,8},{10,11... | collective-permute-start | bytes 786440 | tf_op jit(solution)/shard_map/ppermute | solution.py:182
  39.4 9.9 %collective-permute-start.6 = (f32[64,1024]{1,0:T(8,128)S(1)}, f32[64,1024]{1,0:T(8,128)S(1)}, u32[]{:S(2)}, u32[]{:S(2)}) collective-permute-start(f32[64,1024]{1,0:T(8,128)S(1)} %shard_map.43.refs_0_), channel_id=1, source_target_pairs={{0,1},{1,0},{2,3},{3,2},{4,5},{5,4},{6,7},{7,6},{8,9},{9,8},{10,11... | collective-permute-start | bytes 786440 | tf_op jit(solution)/shard_map/ppermute | solution.py:182
  44.8 7.3 %collective-permute-start.20 = (f32[64,1024]{1,0:T(8,128)S(1)}, f32[64,1024]{1,0:T(8,128)S(1)}, u32[]{:S(2)}, u32[]{:S(2)}) collective-permute-start(f32[64,1024]{1,0:T(8,128)S(1)} %get-tuple-element.60.refs_0_), channel_id=1, source_target_pairs={{0,2},{1,31},{2,0},{3,5},{4,6},{5,3},{6,4},{7,9},{8,10},{9,7},{10,... | collective-permute-start | bytes 786440 | tf_op jit(solution)/shard_map/ppermute | solution.py:193
  47.4 4.7 %collective-permute-start.21 = (f32[64,1024]{1,0:T(8,128)S(1)}, f32[64,1024]{1,0:T(8,128)S(1)}, u32[]{:S(2)}, u32[]{:S(2)}) collective-permute-start(f32[64,1024]{1,0:T(8,128)S(1)} %get-tuple-element.61.refs_2_), channel_id=1, source_target_pairs={{0,2},{1,3},{2,0},{3,1},{4,6},{5,7},{6,4},{7,5},{8,10},{9,11},{10,... | collective-permute-start | bytes 786440 | tf_op jit(solution)/shard_map/ppermute | solution.py:193
  50.1 6.7 %collective-permute-start.7 = (f32[64,1024]{1,0:T(8,128)S(1)}, f32[64,1024]{1,0:T(8,128)S(1)}, u32[]{:S(2)}, u32[]{:S(2)}) collective-permute-start(f32[64,1024]{1,0:T(8,128)S(1)} %get-tuple-element.47.refs_0_), channel_id=1, source_target_pairs={{0,2},{1,31},{2,0},{3,5},{4,6},{5,3},{6,4},{7,9},{8,10},{9,7},{10,... | collective-permute-start | bytes 786440 | tf_op jit(solution)/shard_map/ppermute | solution.py:193
  52.0 4.8 %collective-permute-start.8 = (f32[64,1024]{1,0:T(8,128)S(1)}, f32[64,1024]{1,0:T(8,128)S(1)}, u32[]{:S(2)}, u32[]{:S(2)}) collective-permute-start(f32[64,1024]{1,0:T(8,128)S(1)} %get-tuple-element.48.refs_2_), channel_id=1, source_target_pairs={{0,2},{1,3},{2,0},{3,1},{4,6},{5,7},{6,4},{7,5},{8,10},{9,11},{10,... | collective-permute-start | bytes 786440 | tf_op jit(solution)/shard_map/ppermute | solution.py:193
  52.9 10.3 %collective-permute-start.22 = (f32[64,1024]{1,0:T(8,128)S(1)}, f32[64,1024]{1,0:T(8,128)S(1)}, u32[]{:S(2)}, u32[]{:S(2)}) collective-permute-start(f32[64,1024]{1,0:T(8,128)S(1)} %shard_map.53.refs_0_), channel_id=1, source_target_pairs={{0,1},{1,0},{2,3},{3,2},{4,5},{5,4},{6,7},{7,6},{8,9},{9,8},{10,11... | collective-permute-start | bytes 786440 | tf_op jit(solution)/shard_map/ppermute | solution.py:182
  57.7 10.8 %collective-permute-start.9 = (f32[64,1024]{1,0:T(8,128)S(1)}, f32[64,1024]{1,0:T(8,128)S(1)}, u32[]{:S(2)}, u32[]{:S(2)}) collective-permute-start(f32[64,1024]{1,0:T(8,128)S(1)} %shard_map.45.refs_0_), channel_id=1, source_target_pairs={{0,1},{1,0},{2,3},{3,2},{4,5},{5,4},{6,7},{7,6},{8,9},{9,8},{10,11... | collective-permute-start | bytes 786440 | tf_op jit(solution)/shard_map/ppermute | solution.py:182
  64.1 6.3 %collective-permute-start.23 = (f32[64,1024]{1,0:T(8,128)S(1)}, f32[64,1024]{1,0:T(8,128)S(1)}, u32[]{:S(2)}, u32[]{:S(2)}) collective-permute-start(f32[64,1024]{1,0:T(8,128)S(1)} %get-tuple-element.63.refs_0_), channel_id=1, source_target_pairs={{0,2},{1,31},{2,0},{3,5},{4,6},{5,3},{6,4},{7,9},{8,10},{9,7},{10,... | collective-permute-start | bytes 786440 | tf_op jit(solution)/shard_map/ppermute | solution.py:193
  65.4 5.0 %collective-permute-start.24 = (f32[64,1024]{1,0:T(8,128)S(1)}, f32[64,1024]{1,0:T(8,128)S(1)}, u32[]{:S(2)}, u32[]{:S(2)}) collective-permute-start(f32[64,1024]{1,0:T(8,128)S(1)} %get-tuple-element.64.refs_2_), channel_id=1, source_target_pairs={{0,2},{1,3},{2,0},{3,1},{4,6},{5,7},{6,4},{7,5},{8,10},{9,11},{10,... | collective-permute-start | bytes 786440 | tf_op jit(solution)/shard_map/ppermute | solution.py:193
  69.3 6.7 %collective-permute-start.10 = (f32[64,1024]{1,0:T(8,128)S(1)}, f32[64,1024]{1,0:T(8,128)S(1)}, u32[]{:S(2)}, u32[]{:S(2)}) collective-permute-start(f32[64,1024]{1,0:T(8,128)S(1)} %get-tuple-element.50.refs_0_), channel_id=1, source_target_pairs={{0,2},{1,31},{2,0},{3,5},{4,6},{5,3},{6,4},{7,9},{8,10},{9,7},{10,... | collective-permute-start | bytes 786440 | tf_op jit(solution)/shard_map/ppermute | solution.py:193
  70.3 5.7 %collective-permute-start.11 = (f32[64,1024]{1,0:T(8,128)S(1)}, f32[64,1024]{1,0:T(8,128)S(1)}, u32[]{:S(2)}, u32[]{:S(2)}) collective-permute-start(f32[64,1024]{1,0:T(8,128)S(1)} %get-tuple-element.51.refs_2_), channel_id=1, source_target_pairs={{0,2},{1,3},{2,0},{3,1},{4,6},{5,7},{6,4},{7,5},{8,10},{9,11},{10,... | collective-permute-start | bytes 786440 | tf_op jit(solution)/shard_map/ppermute | solution.py:193
  71.2 9.9 %collective-permute-start.25 = (f32[64,512]{1,0:T(8,128)S(1)}, f32[64,512]{1,0:T(8,128)S(1)}, u32[]{:S(2)}, u32[]{:S(2)}) collective-permute-start(f32[64,512]{1,0:T(8,128)S(1)} %get-tuple-element.66), channel_id=1, source_target_pairs={{0,1},{1,0},{2,3},{3,2},{4,5},{5,4},{6,7},{7,6},{8,9},{9,8},{10,11... | collective-permute-start | bytes 393224 | tf_op jit(solution)/shard_map/ppermute | solution.py:182
  76.8 7.7 %collective-permute-start.12 = (f32[64,512]{1,0:T(8,128)S(1)}, f32[64,512]{1,0:T(8,128)S(1)}, u32[]{:S(2)}, u32[]{:S(2)}) collective-permute-start(f32[64,512]{1,0:T(8,128)S(1)} %get-tuple-element.53), channel_id=1, source_target_pairs={{0,1},{1,0},{2,3},{3,2},{4,5},{5,4},{6,7},{7,6},{8,9},{9,8},{10,11... | collective-permute-start | bytes 393224 | tf_op jit(solution)/shard_map/ppermute | solution.py:182

commit v5 on v4

--- a/solution.py
+++ b/solution.py
@@ -129,23 +129,26 @@
     )
 
 
-def far_kernel(n_off, n_row, *refs):
+def far_kernel(n_off, steps, *refs):
     own_second, second, own_first, first, high_ref, low_ref, *outs = refs
     offset = lax.axis_index("off")
-    ahead_first = partner_order(n_off, n_row)
+    ahead_first = partner_order(n_off, lax.axis_size("row"))
 
     def received(own, if_ahead, if_not, at):
         value = jnp.where(ahead_first, if_ahead[:, at], if_not[:, at])
         return jnp.where(offset == 0, own[:, at], value)
 
-    total_ref = outs[-1]
     far = received(own_second, first, second, slice(None))
-    for at, value in product(far, high_ref, low_ref, 256):
-        total_ref[:, at] = value + received(own_first, second, first, at)
-    for step, out in enumerate(outs[:-1]):
+    for step, out in zip(steps, outs):
         rows = out.shape[1]
-        owner = lax.rem(offset + step, n_off)
-        out[...] = total_ref[:, pl.ds(pl.multiple_of(owner * rows, rows), rows)]
+        strip = min(256, rows)
+        base = 0 if step is None else lax.rem(offset + step, n_off) * rows
+        for start in range(0, rows, strip):
+            at = pl.ds(base + start, strip) if step is None else pl.ds(
+                pl.multiple_of(base + start, strip), strip
+            )
+            [(_, value)] = product(far, high_ref.at[:, at], low_ref.at[:, at], strip)
+            out[:, start : start + strip] = value + received(own_first, second, first, at)
 
 
 def last_kernel(n_off, groups, *refs):
@@ -240,14 +243,21 @@
             seconds.append(swapped(second, 0))
             firsts.append(swapped(first, 1))
         for g in range(GROUPS):
-            outs = kernel_call(
-                functools.partial(far_kernel, n_off, n_row),
-                [VMEM] * 6,
-                [piece_shape] * n_off if last else [group_shape],
-                [pltpu.VMEM(group_shape.shape, jnp.float32)] if last else [],
-                flops=flops,
-            )(*seconds[g], *firsts[g], high_t, low_t)
-            totals[g] = outs if last else outs[0]
+
+            def far_terms(*steps):
+                shape = group_shape if steps[0] is None else piece_shape
+                return kernel_call(
+                    functools.partial(far_kernel, n_off, steps),
+                    [VMEM] * 6,
+                    [shape] * len(steps),
+                    flops=flops,
+                )(*seconds[g], *firsts[g], high_t, low_t)
+
+            if last:
+                totals[g] = far_terms(*range(1, n_off))
+                totals[g] = far_terms(0) + totals[g]
+            else:
+                [totals[g]] = far_terms(None)
     terms = []
     for g in range(GROUPS):
         terms.append(totals[g][0])

time: 85.9 us -> 85.6 us (level)
  waiting for transfers between devices: 14.4 us -> 13.4 us
    ppermute x10, waiting for transfers between devices: 14.3 us -> 13.3 us  [shifted(): lax.ppermute(value, 'off', [(d, (d + distance) % n_off) for d in range(n_...]
    pallas_call x8 -> x10, Pallas kernels: 6.53 us -> 6.85 us  [far_terms(): kernel_call(functools.partial(far_kernel, n_off, steps), [VMEM] * 6, [sha...]
where the time goes in v5:
time: 85.6 us; the launch traced here: 85 us
  starting transfers between devices  53.1 us (62%)
  Pallas kernels  17.4 us (20%)
  waiting for transfers between devices  13.4 us (16%)
  local copies, waits for them, and re-layouts  0.95 us (1%)
    ppermute x10, starting transfers between devices, shifted(): lax.ppermute(value, 'off', [(d, (d + distance) % n_off) for d in range(n_...  37.8 us
    ppermute x16, starting transfers between devices, swapped(): return [value, lax.ppermute(value, ('row', 'off'), route)]  15.3 us
    ppermute x10, waiting for transfers between devices, shifted(): lax.ppermute(value, 'off', [(d, (d + distance) % n_off) for d in range(n_...  13.3 us
    pallas_call x10, Pallas kernels, far_terms(): kernel_call(functools.partial(far_kernel, n_off, steps), [VMEM] * 6, [sha...  6.85 us
    pallas_call x8, Pallas kernels, per_device(): kernel_call(body, [VMEM] * (len(terms) + 2), kept + [group_shape] * 2, fl...  6.36 us
    pallas_call x1, Pallas kernels, per_device(): kernel_call(dense_kernel, [HBM, HBM], [bf16] * 2, [pltpu.SMEM(lists.shape...  2.1 us
  transfers between devices with their start and end apart: 26, of which 8 were waited for; matrix products, arithmetic and copies ran while one was open for 0% of the time, Pallas kernels for 19%

profile of v5, /device:TPU:0, one launch (start us, length us, event | category | flops | bytes accessed | tf_op | source)
XLA Modules:
  0.0 85.0 jit_solution(13313143825604772469)
XLA Ops:
  0.0 0.9 %copy-done = f32[512,128]{1,0:T(8,128)S(1)} copy-done((f32[512,128]{1,0:T(8,128)S(1)}, f32[512,128]{1,0:T(8,128)}, u32[]{:S(2)}) %copy-start) | copy-done | bytes 262168
  1.0 0.1 shard_map.37
  1.1 3.0 %collective-permute-start.13 = (f32[64,512]{1,0:T(8,128)S(1)}, f32[64,512]{1,0:T(8,128)S(1)}, u32[]{:S(2)}, u32[]{:S(2)}) collective-permute-start(f32[64,512]{1,0:T(8,128)S(1)} %get-tuple-element.48.refs_0_), channel_id=1, source_target_pairs={{0,1},{1,0},{2,3},{3,2},{4,5},{5,4},{6,7},{7,6},{8,9},{9,8},{10,11... | collective-permute-start | bytes 393224 | tf_op jit(solution)/shard_map/ppermute | solution.py:185
  4.1 0.1 collective-permute-start
  4.2 2.1 %shard_map.38 = (bf16[1024,1024]{1,0:T(8,128)(2,1)S(1)}, bf16[1024,1024]{1,0:T(8,128)(2,1)S(1)}) custom-call(s32[1,1,2,48]{3,2,1,0:T(2,128)} %lists_hbm.1, f32[1,1,48,128,128]{4,3,2,1,0:T(8,128)} %blocks_hbm.1), custom_call_target="tpu_custom_call" | custom-call | tf_op jit(solution)/shard_map/pallas_call | solution.py:209
  6.3 2.1 %collective-permute-done.13.refs_1_ = f32[64,512]{1,0:T(8,128)S(1)} collective-permute-done((f32[64,512]{1,0:T(8,128)S(1)}, f32[64,512]{1,0:T(8,128)S(1)}, u32[]{:S(2)}, u32[]{:S(2)}) %collective-permute-start.13) | collective-permute-done | bytes 131104 | tf_op jit(solution)/shard_map/ppermute | solution.py:185
  8.4 0.8 shard_map.49
  9.3 0.5 collective-permute-start.15
  9.8 0.6 collective-permute-done.refs_1_
  10.4 0.8 shard_map.39
  11.3 0.5 collective-permute-start.2
  11.8 1.1 %shard_map.40 = (bf16[1024,1024]{1,0:T(8,128)(2,1)S(1)}, bf16[1024,1024]{1,0:T(8,128)(2,1)S(1)}) custom-call(bf16[1024,1024]{1,0:T(8,128)(2,1)S(1)} %get-tuple-element.34.refs_2_.high_ref.refs_3_, bf16[1024,1024]{1,0:T(8,128)(2,1)S(1)} %get-tuple-element.35.refs_3_.low_ref.refs_4_), custom_call_target="tpu_custom_call" | custom-call | flops 402653184 | tf_op jit(solution)/shard_map/pallas_call | solution.py:219
  12.9 0.8 shard_map.50.refs_0_
  13.8 7.0 %collective-permute-start.16 = (f32[64,1024]{1,0:T(8,128)S(1)}, f32[64,1024]{1,0:T(8,128)S(1)}, u32[]{:S(2)}, u32[]{:S(2)}) collective-permute-start(f32[64,1024]{1,0:T(8,128)S(1)} %shard_map.50.refs_0_), channel_id=1, source_target_pairs={{0,1},{1,0},{2,3},{3,2},{4,5},{5,4},{6,7},{7,6},{8,9},{9,8},{10,11... | collective-permute-start | bytes 786440 | tf_op jit(solution)/shard_map/ppermute | solution.py:185
  20.8 0.8 shard_map.41.refs_0_
  21.6 2.0 %collective-permute-start.3 = (f32[64,1024]{1,0:T(8,128)S(1)}, f32[64,1024]{1,0:T(8,128)S(1)}, u32[]{:S(2)}, u32[]{:S(2)}) collective-permute-start(f32[64,1024]{1,0:T(8,128)S(1)} %shard_map.41.refs_0_), channel_id=1, source_target_pairs={{0,1},{1,0},{2,3},{3,2},{4,5},{5,4},{6,7},{7,6},{8,9},{9,8},{10,11... | collective-permute-start | bytes 786440 | tf_op jit(solution)/shard_map/ppermute | solution.py:185
  23.6 2.1 %collective-permute-done.16.refs_1_ = f32[64,1024]{1,0:T(8,128)S(1)} collective-permute-done((f32[64,1024]{1,0:T(8,128)S(1)}, f32[64,1024]{1,0:T(8,128)S(1)}, u32[]{:S(2)}, u32[]{:S(2)}) %collective-permute-start.16) | collective-permute-done | bytes 262176 | tf_op jit(solution)/shard_map/ppermute | solution.py:185
  25.7 0.8 shard_map.51
  26.5 4.7 %collective-permute-start.17 = (f32[64,1024]{1,0:T(8,128)S(1)}, f32[64,1024]{1,0:T(8,128)S(1)}, u32[]{:S(2)}, u32[]{:S(2)}) collective-permute-start(f32[64,1024]{1,0:T(8,128)S(1)} %get-tuple-element.51.refs_0_), channel_id=1, source_target_pairs={{0,2},{1,31},{2,0},{3,5},{4,6},{5,3},{6,4},{7,9},{8,10},{9,7},{10,... | collective-permute-start | bytes 786440 | tf_op jit(solution)/shard_map/ppermute | solution.py:196
  31.3 0.8 shard_map.42
  32.1 2.1 %collective-permute-start.4 = (f32[64,1024]{1,0:T(8,128)S(1)}, f32[64,1024]{1,0:T(8,128)S(1)}, u32[]{:S(2)}, u32[]{:S(2)}) collective-permute-start(f32[64,1024]{1,0:T(8,128)S(1)} %get-tuple-element.40.refs_0_), channel_id=1, source_target_pairs={{0,2},{1,31},{2,0},{3,5},{4,6},{5,3},{6,4},{7,9},{8,10},{9,7},{10,... | collective-permute-start | bytes 786440 | tf_op jit(solution)/shard_map/ppermute | solution.py:196
  34.4 0.8 shard_map.52.refs_0_
  35.2 3.4 %collective-permute-start.19 = (f32[64,1024]{1,0:T(8,128)S(1)}, f32[64,1024]{1,0:T(8,128)S(1)}, u32[]{:S(2)}, u32[]{:S(2)}) collective-permute-start(f32[64,1024]{1,0:T(8,128)S(1)} %shard_map.52.refs_0_), channel_id=1, source_target_pairs={{0,1},{1,0},{2,3},{3,2},{4,5},{5,4},{6,7},{7,6},{8,9},{9,8},{10,11... | collective-permute-start | bytes 786440 | tf_op jit(solution)/shard_map/ppermute | solution.py:185
  38.5 0.8 shard_map.43.refs_0_
  39.4 4.6 %collective-permute-start.6 = (f32[64,1024]{1,0:T(8,128)S(1)}, f32[64,1024]{1,0:T(8,128)S(1)}, u32[]{:S(2)}, u32[]{:S(2)}) collective-permute-start(f32[64,1024]{1,0:T(8,128)S(1)} %shard_map.43.refs_0_), channel_id=1, source_target_pairs={{0,1},{1,0},{2,3},{3,2},{4,5},{5,4},{6,7},{7,6},{8,9},{9,8},{10,11... | collective-permute-start | bytes 786440 | tf_op jit(solution)/shard_map/ppermute | solution.py:185
  44.0 0.8 shard_map.53
  44.8 2.6 %collective-permute-start.20 = (f32[64,1024]{1,0:T(8,128)S(1)}, f32[64,1024]{1,0:T(8,128)S(1)}, u32[]{:S(2)}, u32[]{:S(2)}) collective-permute-start(f32[64,1024]{1,0:T(8,128)S(1)} %get-tuple-element.54.refs_0_), channel_id=1, source_target_pairs={{0,2},{1,31},{2,0},{3,5},{4,6},{5,3},{6,4},{7,9},{8,10},{9,7},{10,... | collective-permute-start | bytes 786440 | tf_op jit(solution)/shard_map/ppermute | solution.py:196
  47.5 1.8 %collective-permute-done.6.refs_1_ = f32[64,1024]{1,0:T(8,128)S(1)} collective-permute-done((f32[64,1024]{1,0:T(8,128)S(1)}, f32[64,1024]{1,0:T(8,128)S(1)}, u32[]{:S(2)}, u32[]{:S(2)}) %collective-permute-start.6) | collective-permute-done | bytes 262176 | tf_op jit(solution)/shard_map/ppermute | solution.py:185
  49.3 0.8 shard_map.44
  50.1 1.9 %collective-permute-start.7 = (f32[64,1024]{1,0:T(8,128)S(1)}, f32[64,1024]{1,0:T(8,128)S(1)}, u32[]{:S(2)}, u32[]{:S(2)}) collective-permute-start(f32[64,1024]{1,0:T(8,128)S(1)} %get-tuple-element.43.refs_0_), channel_id=1, source_target_pairs={{0,2},{1,31},{2,0},{3,5},{4,6},{5,3},{6,4},{7,9},{8,10},{9,7},{10,... | collective-permute-start | bytes 786440 | tf_op jit(solution)/shard_map/ppermute | solution.py:196
  52.1 0.8 shard_map.54.refs_0_
  52.9 3.9 %collective-permute-start.22 = (f32[64,1024]{1,0:T(8,128)S(1)}, f32[64,1024]{1,0:T(8,128)S(1)}, u32[]{:S(2)}, u32[]{:S(2)}) collective-permute-start(f32[64,1024]{1,0:T(8,128)S(1)} %shard_map.54.refs_0_), channel_id=1, source_target_pairs={{0,1},{1,0},{2,3},{3,2},{4,5},{5,4},{6,7},{7,6},{8,9},{9,8},{10,11... | collective-permute-start | bytes 786440 | tf_op jit(solution)/shard_map/ppermute | solution.py:185
  56.8 0.8 shard_map.45.refs_0_
  57.7 4.3 %collective-permute-start.9 = (f32[64,1024]{1,0:T(8,128)S(1)}, f32[64,1024]{1,0:T(8,128)S(1)}, u32[]{:S(2)}, u32[]{:S(2)}) collective-permute-start(f32[64,1024]{1,0:T(8,128)S(1)} %shard_map.45.refs_0_), channel_id=1, source_target_pairs={{0,1},{1,0},{2,3},{3,2},{4,5},{5,4},{6,7},{7,6},{8,9},{9,8},{10,11... | collective-permute-start | bytes 786440 | tf_op jit(solution)/shard_map/ppermute | solution.py:185
  61.9 1.3 %collective-permute-done.22.refs_1_ = f32[64,1024]{1,0:T(8,128)S(1)} collective-permute-done((f32[64,1024]{1,0:T(8,128)S(1)}, f32[64,1024]{1,0:T(8,128)S(1)}, u32[]{:S(2)}, u32[]{:S(2)}) %collective-permute-start.22) | collective-permute-done | bytes 262176 | tf_op jit(solution)/shard_map/ppermute | solution.py:185
  63.2 0.8 shard_map.55
  64.1 1.4 %collective-permute-start.23 = (f32[64,1024]{1,0:T(8,128)S(1)}, f32[64,1024]{1,0:T(8,128)S(1)}, u32[]{:S(2)}, u32[]{:S(2)}) collective-permute-start(f32[64,1024]{1,0:T(8,128)S(1)} %get-tuple-element.57.refs_0_), channel_id=1, source_target_pairs={{0,2},{1,31},{2,0},{3,5},{4,6},{5,3},{6,4},{7,9},{8,10},{9,7},{10,... | collective-permute-start | bytes 786440 | tf_op jit(solution)/shard_map/ppermute | solution.py:196
  65.5 3.0 %collective-permute-done.9.refs_1_ = f32[64,1024]{1,0:T(8,128)S(1)} collective-permute-done((f32[64,1024]{1,0:T(8,128)S(1)}, f32[64,1024]{1,0:T(8,128)S(1)}, u32[]{:S(2)}, u32[]{:S(2)}) %collective-permute-start.9) | collective-permute-done | bytes 262176 | tf_op jit(solution)/shard_map/ppermute | solution.py:185
  68.5 0.8 shard_map.46
  69.3 1.0 %collective-permute-start.10 = (f32[64,1024]{1,0:T(8,128)S(1)}, f32[64,1024]{1,0:T(8,128)S(1)}, u32[]{:S(2)}, u32[]{:S(2)}) collective-permute-start(f32[64,1024]{1,0:T(8,128)S(1)} %get-tuple-element.46.refs_0_), channel_id=1, source_target_pairs={{0,2},{1,31},{2,0},{3,5},{4,6},{5,3},{6,4},{7,9},{8,10},{9,7},{10,... | collective-permute-start | bytes 786440 | tf_op jit(solution)/shard_map/ppermute | solution.py:196
  70.4 0.5 shard_map.57
  70.9 4.7 %collective-permute-start.25 = (f32[64,512]{1,0:T(8,128)S(1)}, f32[64,512]{1,0:T(8,128)S(1)}, u32[]{:S(2)}, u32[]{:S(2)}) collective-permute-start(f32[64,512]{1,0:T(8,128)S(1)} %shard_map.57), channel_id=1, source_target_pairs={{0,1},{1,0},{2,3},{3,2},{4,5},{5,4},{6,7},{7,6},{8,9},{9,8},{10,11... | collective-permute-start | bytes 393224 | tf_op jit(solution)/shard_map/ppermute | solution.py:185
  75.6 0.5 shard_map.48
  76.1 4.7 %collective-permute-start.12 = (f32[64,512]{1,0:T(8,128)S(1)}, f32[64,512]{1,0:T(8,128)S(1)}, u32[]{:S(2)}, u32[]{:S(2)}) collective-permute-start(f32[64,512]{1,0:T(8,128)S(1)} %shard_map.48), channel_id=1, source_target_pairs={{0,1},{1,0},{2,3},{3,2},{4,5},{5,4},{6,7},{7,6},{8,9},{9,8},{10,11... | collective-permute-start | bytes 393224 | tf_op jit(solution)/shard_map/ppermute | solution.py:185
  80.8 0.5 shard_map.56.refs_2_
  81.3 0.5 shard_map.47.refs_0_
  81.9 2.3 %collective-permute-done.12.refs_1_ = f32[64,512]{1,0:T(8,128)S(1)} collective-permute-done((f32[64,512]{1,0:T(8,128)S(1)}, f32[64,512]{1,0:T(8,128)S(1)}, u32[]{:S(2)}, u32[]{:S(2)}) %collective-permute-start.12) | collective-permute-done | bytes 131104 | tf_op jit(solution)/shard_map/ppermute | solution.py:185
  84.2 0.8 shard_map.58
  (28 shorter events, 0.7 us)
Async XLA Ops:
  0.0 0.9 %copy-start = (f32[512,128]{1,0:T(8,128)S(1)}, f32[512,128]{1,0:T(8,128)}, u32[]{:S(2)}) copy-start(f32[512,128]{1,0:T(8,128)} %piece_ref.1) | copy-start | bytes 786436
  1.1 7.3 %collective-permute-start.13 = (f32[64,512]{1,0:T(8,128)S(1)}, f32[64,512]{1,0:T(8,128)S(1)}, u32[]{:S(2)}, u32[]{:S(2)}) collective-permute-start(f32[64,512]{1,0:T(8,128)S(1)} %get-tuple-element.48.refs_0_), channel_id=1, source_target_pairs={{0,1},{1,0},{2,3},{3,2},{4,5},{5,4},{6,7},{7,6},{8,9},{9,8},{10,11... | collective-permute-start | bytes 393224 | tf_op jit(solution)/shard_map/ppermute | solution.py:185
  4.1 6.3 %collective-permute-start = (f32[64,512]{1,0:T(8,128)S(1)}, f32[64,512]{1,0:T(8,128)S(1)}, u32[]{:S(2)}, u32[]{:S(2)}) collective-permute-start(f32[64,512]{1,0:T(8,128)S(1)} %get-tuple-element.33.refs_0_), channel_id=1, source_target_pairs={{0,1},{1,0},{2,3},{3,2},{4,5},{5,4},{6,7},{7,6},{8,9},{9,8},{10,11... | collective-permute-start | bytes 393224 | tf_op jit(solution)/shard_map/ppermute | solution.py:185
  9.2 3.7 %collective-permute-start.14 = (f32[64,1024]{1,0:T(8,128)S(1)}, f32[64,1024]{1,0:T(8,128)S(1)}, u32[]{:S(2)}, u32[]{:S(2)}) collective-permute-start(f32[64,1024]{1,0:T(8,128)S(1)} %get-tuple-element.49.refs_0_), channel_id=1, source_target_pairs={{0,2},{1,31},{2,0},{3,5},{4,6},{5,3},{6,4},{7,9},{8,10},{9,7},{10,... | collective-permute-start | bytes 786440 | tf_op jit(solution)/shard_map/ppermute | solution.py:196
  9.3 3.6 %collective-permute-start.15 = (f32[64,1024]{1,0:T(8,128)S(1)}, f32[64,1024]{1,0:T(8,128)S(1)}, u32[]{:S(2)}, u32[]{:S(2)}) collective-permute-start(f32[64,1024]{1,0:T(8,128)S(1)} %get-tuple-element.50.refs_2_), channel_id=1, source_target_pairs={{0,2},{1,3},{2,0},{3,1},{4,6},{5,7},{6,4},{7,5},{8,10},{9,11},{10,... | collective-permute-start | bytes 786440 | tf_op jit(solution)/shard_map/ppermute | solution.py:196
  11.2 9.6 %collective-permute-start.1 = (f32[64,1024]{1,0:T(8,128)S(1)}, f32[64,1024]{1,0:T(8,128)S(1)}, u32[]{:S(2)}, u32[]{:S(2)}) collective-permute-start(f32[64,1024]{1,0:T(8,128)S(1)} %get-tuple-element.36.refs_0_), channel_id=1, source_target_pairs={{0,2},{1,31},{2,0},{3,5},{4,6},{5,3},{6,4},{7,9},{8,10},{9,7},{10,... | collective-permute-start | bytes 786440 | tf_op jit(solution)/shard_map/ppermute | solution.py:196
  11.3 9.5 %collective-permute-start.2 = (f32[64,1024]{1,0:T(8,128)S(1)}, f32[64,1024]{1,0:T(8,128)S(1)}, u32[]{:S(2)}, u32[]{:S(2)}) collective-permute-start(f32[64,1024]{1,0:T(8,128)S(1)} %get-tuple-element.37.refs_2_), channel_id=1, source_target_pairs={{0,2},{1,3},{2,0},{3,1},{4,6},{5,7},{6,4},{7,5},{8,10},{9,11},{10,... | collective-permute-start | bytes 786440 | tf_op jit(solution)/shard_map/ppermute | solution.py:196
  13.8 12.0 %collective-permute-start.16 = (f32[64,1024]{1,0:T(8,128)S(1)}, f32[64,1024]{1,0:T(8,128)S(1)}, u32[]{:S(2)}, u32[]{:S(2)}) collective-permute-start(f32[64,1024]{1,0:T(8,128)S(1)} %shard_map.50.refs_0_), channel_id=1, source_target_pairs={{0,1},{1,0},{2,3},{3,2},{4,5},{5,4},{6,7},{7,6},{8,9},{9,8},{10,11... | collective-permute-start | bytes 786440 | tf_op jit(solution)/shard_map/ppermute | solution.py:185
  21.6 9.7 %collective-permute-start.3 = (f32[64,1024]{1,0:T(8,128)S(1)}, f32[64,1024]{1,0:T(8,128)S(1)}, u32[]{:S(2)}, u32[]{:S(2)}) collective-permute-start(f32[64,1024]{1,0:T(8,128)S(1)} %shard_map.41.refs_0_), channel_id=1, source_target_pairs={{0,1},{1,0},{2,3},{3,2},{4,5},{5,4},{6,7},{7,6},{8,9},{9,8},{10,11... | collective-permute-start | bytes 786440 | tf_op jit(solution)/shard_map/ppermute | solution.py:185
  26.5 7.8 %collective-permute-start.17 = (f32[64,1024]{1,0:T(8,128)S(1)}, f32[64,1024]{1,0:T(8,128)S(1)}, u32[]{:S(2)}, u32[]{:S(2)}) collective-permute-start(f32[64,1024]{1,0:T(8,128)S(1)} %get-tuple-element.51.refs_0_), channel_id=1, source_target_pairs={{0,2},{1,31},{2,0},{3,5},{4,6},{5,3},{6,4},{7,9},{8,10},{9,7},{10,... | collective-permute-start | bytes 786440 | tf_op jit(solution)/shard_map/ppermute | solution.py:196
  31.2 3.2 %collective-permute-start.18 = (f32[64,1024]{1,0:T(8,128)S(1)}, f32[64,1024]{1,0:T(8,128)S(1)}, u32[]{:S(2)}, u32[]{:S(2)}) collective-permute-start(f32[64,1024]{1,0:T(8,128)S(1)} %get-tuple-element.52.refs_2_), channel_id=1, source_target_pairs={{0,2},{1,3},{2,0},{3,1},{4,6},{5,7},{6,4},{7,5},{8,10},{9,11},{10,... | collective-permute-start | bytes 786440 | tf_op jit(solution)/shard_map/ppermute | solution.py:196
  32.1 6.4 %collective-permute-start.4 = (f32[64,1024]{1,0:T(8,128)S(1)}, f32[64,1024]{1,0:T(8,128)S(1)}, u32[]{:S(2)}, u32[]{:S(2)}) collective-permute-start(f32[64,1024]{1,0:T(8,128)S(1)} %get-tuple-element.40.refs_0_), channel_id=1, source_target_pairs={{0,2},{1,31},{2,0},{3,5},{4,6},{5,3},{6,4},{7,9},{8,10},{9,7},{10,... | collective-permute-start | bytes 786440 | tf_op jit(solution)/shard_map/ppermute | solution.py:196
  34.3 4.3 %collective-permute-start.5 = (f32[64,1024]{1,0:T(8,128)S(1)}, f32[64,1024]{1,0:T(8,128)S(1)}, u32[]{:S(2)}, u32[]{:S(2)}) collective-permute-start(f32[64,1024]{1,0:T(8,128)S(1)} %get-tuple-element.41.refs_2_), channel_id=1, source_target_pairs={{0,2},{1,3},{2,0},{3,1},{4,6},{5,7},{6,4},{7,5},{8,10},{9,11},{10,... | collective-permute-start | bytes 786440 | tf_op jit(solution)/shard_map/ppermute | solution.py:196
  35.2 8.8 %collective-permute-start.19 = (f32[64,1024]{1,0:T(8,128)S(1)}, f32[64,1024]{1,0:T(8,128)S(1)}, u32[]{:S(2)}, u32[]{:S(2)}) collective-permute-start(f32[64,1024]{1,0:T(8,128)S(1)} %shard_map.52.refs_0_), channel_id=1, source_target_pairs={{0,1},{1,0},{2,3},{3,2},{4,5},{5,4},{6,7},{7,6},{8,9},{9,8},{10,11... | collective-permute-start | bytes 786440 | tf_op jit(solution)/shard_map/ppermute | solution.py:185
  39.4 9.9 %collective-permute-start.6 = (f32[64,1024]{1,0:T(8,128)S(1)}, f32[64,1024]{1,0:T(8,128)S(1)}, u32[]{:S(2)}, u32[]{:S(2)}) collective-permute-start(f32[64,1024]{1,0:T(8,128)S(1)} %shard_map.43.refs_0_), channel_id=1, source_target_pairs={{0,1},{1,0},{2,3},{3,2},{4,5},{5,4},{6,7},{7,6},{8,9},{9,8},{10,11... | collective-permute-start | bytes 786440 | tf_op jit(solution)/shard_map/ppermute | solution.py:185
  44.8 7.3 %collective-permute-start.20 = (f32[64,1024]{1,0:T(8,128)S(1)}, f32[64,1024]{1,0:T(8,128)S(1)}, u32[]{:S(2)}, u32[]{:S(2)}) collective-permute-start(f32[64,1024]{1,0:T(8,128)S(1)} %get-tuple-element.54.refs_0_), channel_id=1, source_target_pairs={{0,2},{1,31},{2,0},{3,5},{4,6},{5,3},{6,4},{7,9},{8,10},{9,7},{10,... | collective-permute-start | bytes 786440 | tf_op jit(solution)/shard_map/ppermute | solution.py:196
  47.4 4.7 %collective-permute-start.21 = (f32[64,1024]{1,0:T(8,128)S(1)}, f32[64,1024]{1,0:T(8,128)S(1)}, u32[]{:S(2)}, u32[]{:S(2)}) collective-permute-start(f32[64,1024]{1,0:T(8,128)S(1)} %get-tuple-element.55.refs_2_), channel_id=1, source_target_pairs={{0,2},{1,3},{2,0},{3,1},{4,6},{5,7},{6,4},{7,5},{8,10},{9,11},{10,... | collective-permute-start | bytes 786440 | tf_op jit(solution)/shard_map/ppermute | solution.py:196
  50.1 6.7 %collective-permute-start.7 = (f32[64,1024]{1,0:T(8,128)S(1)}, f32[64,1024]{1,0:T(8,128)S(1)}, u32[]{:S(2)}, u32[]{:S(2)}) collective-permute-start(f32[64,1024]{1,0:T(8,128)S(1)} %get-tuple-element.43.refs_0_), channel_id=1, source_target_pairs={{0,2},{1,31},{2,0},{3,5},{4,6},{5,3},{6,4},{7,9},{8,10},{9,7},{10,... | collective-permute-start | bytes 786440 | tf_op jit(solution)/shard_map/ppermute | solution.py:196
  52.0 4.8 %collective-permute-start.8 = (f32[64,1024]{1,0:T(8,128)S(1)}, f32[64,1024]{1,0:T(8,128)S(1)}, u32[]{:S(2)}, u32[]{:S(2)}) collective-permute-start(f32[64,1024]{1,0:T(8,128)S(1)} %get-tuple-element.44.refs_2_), channel_id=1, source_target_pairs={{0,2},{1,3},{2,0},{3,1},{4,6},{5,7},{6,4},{7,5},{8,10},{9,11},{10,... | collective-permute-start | bytes 786440 | tf_op jit(solution)/shard_map/ppermute | solution.py:196
  52.9 10.3 %collective-permute-start.22 = (f32[64,1024]{1,0:T(8,128)S(1)}, f32[64,1024]{1,0:T(8,128)S(1)}, u32[]{:S(2)}, u32[]{:S(2)}) collective-permute-start(f32[64,1024]{1,0:T(8,128)S(1)} %shard_map.54.refs_0_), channel_id=1, source_target_pairs={{0,1},{1,0},{2,3},{3,2},{4,5},{5,4},{6,7},{7,6},{8,9},{9,8},{10,11... | collective-permute-start | bytes 786440 | tf_op jit(solution)/shard_map/ppermute | solution.py:185
  57.7 10.8 %collective-permute-start.9 = (f32[64,1024]{1,0:T(8,128)S(1)}, f32[64,1024]{1,0:T(8,128)S(1)}, u32[]{:S(2)}, u32[]{:S(2)}) collective-permute-start(f32[64,1024]{1,0:T(8,128)S(1)} %shard_map.45.refs_0_), channel_id=1, source_target_pairs={{0,1},{1,0},{2,3},{3,2},{4,5},{5,4},{6,7},{7,6},{8,9},{9,8},{10,11... | collective-permute-start | bytes 786440 | tf_op jit(solution)/shard_map/ppermute | solution.py:185
  64.1 6.3 %collective-permute-start.23 = (f32[64,1024]{1,0:T(8,128)S(1)}, f32[64,1024]{1,0:T(8,128)S(1)}, u32[]{:S(2)}, u32[]{:S(2)}) collective-permute-start(f32[64,1024]{1,0:T(8,128)S(1)} %get-tuple-element.57.refs_0_), channel_id=1, source_target_pairs={{0,2},{1,31},{2,0},{3,5},{4,6},{5,3},{6,4},{7,9},{8,10},{9,7},{10,... | collective-permute-start | bytes 786440 | tf_op jit(solution)/shard_map/ppermute | solution.py:196
  65.4 5.0 %collective-permute-start.24 = (f32[64,1024]{1,0:T(8,128)S(1)}, f32[64,1024]{1,0:T(8,128)S(1)}, u32[]{:S(2)}, u32[]{:S(2)}) collective-permute-start(f32[64,1024]{1,0:T(8,128)S(1)} %get-tuple-element.58.refs_2_), channel_id=1, source_target_pairs={{0,2},{1,3},{2,0},{3,1},{4,6},{5,7},{6,4},{7,5},{8,10},{9,11},{10,... | collective-permute-start | bytes 786440 | tf_op jit(solution)/shard_map/ppermute | solution.py:196
  69.3 6.3 %collective-permute-start.10 = (f32[64,1024]{1,0:T(8,128)S(1)}, f32[64,1024]{1,0:T(8,128)S(1)}, u32[]{:S(2)}, u32[]{:S(2)}) collective-permute-start(f32[64,1024]{1,0:T(8,128)S(1)} %get-tuple-element.46.refs_0_), channel_id=1, source_target_pairs={{0,2},{1,31},{2,0},{3,5},{4,6},{5,3},{6,4},{7,9},{8,10},{9,7},{10,... | collective-permute-start | bytes 786440 | tf_op jit(solution)/shard_map/ppermute | solution.py:196
  70.3 5.3 %collective-permute-start.11 = (f32[64,1024]{1,0:T(8,128)S(1)}, f32[64,1024]{1,0:T(8,128)S(1)}, u32[]{:S(2)}, u32[]{:S(2)}) collective-permute-start(f32[64,1024]{1,0:T(8,128)S(1)} %get-tuple-element.47.refs_2_), channel_id=1, source_target_pairs={{0,2},{1,3},{2,0},{3,1},{4,6},{5,7},{6,4},{7,5},{8,10},{9,11},{10,... | collective-permute-start | bytes 786440 | tf_op jit(solution)/shard_map/ppermute | solution.py:196
  70.9 10.9 %collective-permute-start.25 = (f32[64,512]{1,0:T(8,128)S(1)}, f32[64,512]{1,0:T(8,128)S(1)}, u32[]{:S(2)}, u32[]{:S(2)}) collective-permute-start(f32[64,512]{1,0:T(8,128)S(1)} %shard_map.57), channel_id=1, source_target_pairs={{0,1},{1,0},{2,3},{3,2},{4,5},{5,4},{6,7},{7,6},{8,9},{9,8},{10,11... | collective-permute-start | bytes 393224 | tf_op jit(solution)/shard_map/ppermute | solution.py:185
  76.1 8.0 %collective-permute-start.12 = (f32[64,512]{1,0:T(8,128)S(1)}, f32[64,512]{1,0:T(8,128)S(1)}, u32[]{:S(2)}, u32[]{:S(2)}) collective-permute-start(f32[64,512]{1,0:T(8,128)S(1)} %shard_map.48), channel_id=1, source_target_pairs={{0,1},{1,0},{2,3},{3,2},{4,5},{5,4},{6,7},{7,6},{8,9},{9,8},{10,11... | collective-permute-start | bytes 393224 | tf_op jit(solution)/shard_map/ppermute | solution.py:185
